TPU v7x, 32 devices: a whole 2x2x4 slice. The times are simulated.
32 devices in a mesh: gx: 4 (over z), gy: 8 (over y, x, core).
Axes of the slice: x: 2, y: 2, z: 4, core: 2. Of those that a mesh axis runs over, the one named last changes fastest.
Arguments:
- coupling: bfloat16 [4, 64, 1024, 512], P('gx', 'gy'), may hold values from -0.44921875 to 0.44921875
- local_block: bfloat16 [4, 64, 512, 512], P('gx', 'gy'), as said below
- counts: int32 [4, 64], P('gx', 'gy'), may hold values from 1 to 4, as said below
- primal: int32 [4, 64, 512], P('gx', 'gy'), may hold values from 0 to 511
- partner: int32 [3, 4], replicated, may hold values from 0 to 3, as said below
Outputs:
- coarse: float32 [4, 512, 512], P('gx')
Inputs may be any that keep to these rules, and one draw needn't show every extreme that they name: Each row of partner is a perfect matching of the 4 columns: partner[r, partner[r, c]] == c and partner[r, c] != c. `counts`: in each subdomain column at least one subdomain has all 4 blocks live. `primal`: any constraint may hold any number of rows. `local_block`: diagonal entries are positive.
All inputs are finite; a program needn't handle non-finite values. Where the computation divides by a largest or mean magnitude, that divisor is 1e-20 or more.
Results may differ from a plain program's by a relative error of at most 0.00078.
Values sent between devices are 32-bit elements; how exact they have to be, the bound alone decides.
No kernel may reach another device: no remote copies, remote signals or barrier semaphores. Data moves between devices by JAX's collectives and lax.ppermute only.
A program may use at most 192 MiB of HBM per device.

v0:
```python
import jax
import jax.numpy as jnp
from jax import lax
from jax.sharding import PartitionSpec as P

BLK = 128
NC = 512
ROUNDS = 3
R = 512


def per_device(coupling, local_block, counts, primal, partner):
    column = lax.axis_index("gx")
    stiff = jnp.diagonal(local_block[0], axis1=1, axis2=2).astype(jnp.float32)
    total = stiff
    for r in range(ROUNDS):
        mate = partner[r, column]
        piece = jax.tree.map(
            lambda part: lax.all_gather(part, "gx", axis=0, tiled=True), stiff[None]
        )
        index = jnp.arange(piece.shape[0], dtype=jnp.int32)
        hit = (index == mate)[:, None, None]
        total = total + (
            jnp.zeros_like(stiff)
            + jnp.sum(jnp.where(hit, piece, jnp.zeros((), jnp.float32)), axis=0)
        )
    weight = stiff / total
    rows = jnp.arange(R, dtype=jnp.int32)
    live = (rows[None, :] < counts[0][:, None] * BLK).astype(jnp.float32)
    gram = jnp.einsum("snr,snq->srq", coupling[0], coupling[0], preferred_element_type=jnp.float32)
    schur = (
        (local_block[0].astype(jnp.float32) - gram) * live[:, :, None] * live[:, None, :]
    ).astype(jnp.bfloat16)
    onehot = primal[0][:, :, None] == jnp.arange(NC, dtype=jnp.int32)[None, None, :]
    basis = jnp.where(onehot, weight[:, :, None], jnp.zeros((), jnp.float32)).astype(jnp.bfloat16)
    image = jnp.einsum("srq,sqk->srk", schur, basis, preferred_element_type=jnp.float32).astype(
        jnp.bfloat16
    )
    tile = jnp.einsum("srk,srl->kl", basis, image, preferred_element_type=jnp.float32)
    summed = lax.psum(tile, "gy")
    scale = 1.0 / jnp.sqrt(jnp.mean(jnp.abs(summed), axis=1) + 1e-06)
    result = summed * scale[:, None] * scale[None, :]
    return result[None]


def solution(mesh):
    placed = (
        P("gx", "gy", None, None),
        P("gx", "gy", None, None),
        P("gx", "gy"),
        P("gx", "gy", None),
        P(),
    )
    return jax.shard_map(
        per_device, mesh=mesh, in_specs=placed, out_specs=P("gx", None, None), check_vma=False
    )
```

profile of v0, /device:TPU:0, one launch (start us, length us, event | category | flops | bytes accessed | tf_op | source)
XLA Modules:
  0.0 167.9 jit_solution(11568143518739150617)
XLA Ops:
  6.5 0.0 all-reduce.2.cloned.1.call-start
  6.5 1.5 constant_dynamic-slice_fusion
  8.0 0.7 iota_compare_fusion.4
  8.7 44.1 %copy.19 = bf16[8,512,512]{0,2,1:T(8,128)(2,1)} copy(bf16[8,512,512]{2,1,0:T(8,128)(2,1)} %bitcast.35) | data formatting | bytes 8388608 | tf_op jit(solution)/shard_map/squeeze | solution.py:14
  52.8 6.5 %gather_fusion = bf16[512,8]{1,0:T(8,128)(2,1)S(1)} fusion(bf16[8,512,512]{0,2,1:T(8,128)(2,1)} %copy.19, s32[512]{0:T(512)S(1)} %bitcast.34), kind=kCustom, calls=%fused_computation | custom fusion | bytes 20480 | tf_op jit(solution)/shard_map/jit(diagonal)/gather | solution.py:14
  59.3 0.1 copy.20
  59.3 14.9 %all-gather = f32[32,512]{1,0:T(8,128)S(1)} all-gather(f32[8,512]{1,0:T(8,128)S(1)} %convert_bitcast_fusion), channel_id=2, replica_groups=mesh['gx'=4,'gy'=8] {'gx'}, dimensions={0}, use_global_device_ids=true | all-gather | bytes 81920 | tf_op jit(solution)/shard_map/all_gather | solution.py:19
  74.2 0.0 copy-start.1
  74.2 0.0 copy-start
  74.2 13.6 %fusion = f32[8,512,512]{2,1,0:T(8,128)} fusion(bf16[1,8,1024,512]{3,2,1,0:T(8,128)(2,1)} %param.5), kind=kOutput, calls=%fused_computation.1 | convolution fusion | flops 4294967296 | bytes 16777216 | tf_op jit(solution)/shard_map/snr,snq->srq/dot_general | solution.py:30
  87.8 0.0 copy-done.1
  87.8 0.1 fusion.21
  87.9 1.2 iota_compare_fusion.2
  89.1 0.1 fusion.18
  89.2 0.0 copy-done
  89.2 10.2 %fusion.15 = f32[512,512]{1,0:T(8,128)} fusion(f32[8,512,512]{2,1,0:T(8,128)} %fusion, f32[8,512]{1,0:T(8,128)S(1)} %fusion.21, bf16[8,512]{1,0:T(8,128)(2,1)S(1)} %add_divide_fusion, s32[8,512]{1,0:T(8,128)S(1)} %bitcast.36, bf16[1,8,512,512]{3,2,1,0:T(8,128)(2,1)} %param.6), kind=kOutput, calls=%fused_computation.14 | convolution fusion | flops 4315938816 | bytes 13672448 | tf_op jit(solution)/shard_map/srk,srl->kl/dot_general | solution.py:39
  99.4 0.0 all-reduce.2.cloned.1.call-update
  99.4 57.9 %all-reduce.2.cloned.1.call-done = f32[512,512]{1,0:T(8,128)} async-done(((f32[512,512]{1,0:T(8,128)}), f32[512,512]{1,0:T(8,128)}) %all-reduce.2.cloned.1.call-update) | async-done | bytes 1048592 | tf_op jit(solution)/shard_map/psum | solution.py:40
  157.3 1.4 abs_reduce_fusion
  158.7 2.4 %multiply_bitcast_fusion = f32[1,512,512]{2,1,0:T(8,128)} fusion(f32[512,512]{1,0:T(8,128)} %all-reduce.2.cloned.1.call-done, f32[512]{0:T(512)S(1)} %add_rsqrt_fusion), kind=kLoop, calls=%fused_computation.15 | loop fusion | flops 524288 | bytes 2099200 | tf_op jit(solution)/shard_map/broadcast_in_dim | solution.py:43
  (5 shorter events, 0.0 us)
Async XLA Ops:
  6.5 150.8 %all-reduce.2.cloned.1.call-start = ((), (), s32[]{:S(2)}) async-start(), calls=%async_computation | async-start | bytes 2097152 | tf_op jit(solution)/shard_map/psum | solution.py:40
  74.2 13.6 %copy-start.1 = (s32[1,8]{1,0:T(1,128)S(1)}, s32[1,8]{1,0:T(1,128)}, u32[]{:S(2)}) copy-start(s32[1,8]{1,0:T(1,128)} %param.7) | copy-start | bytes 100
  74.2 15.0 %copy-start = (s32[1,8,512]{2,1,0:T(8,128)S(1)}, s32[1,8,512]{2,1,0:T(8,128)}, u32[]{:S(2)}) copy-start(s32[1,8,512]{2,1,0:T(8,128)} %param.8) | copy-start | bytes 49156
Sparse Core Ops, SparseCore 0:
  99.6 57.6 all-reduce.1
where the time goes:
time: 171 us; the launch traced here: 168 us
  waiting for transfers between devices  57.9 us (34%)
  local copies, waits for them, and re-layouts  52.1 us (30%)
  matrix products  23.7 us (14%)
  blocking collectives  14.9 us (9%)
  between operations  13.4 us (8%)
  other arithmetic  5.84 us (3%)
    psum x1, waiting for transfers between devices, per_device(): summed = lax.psum(tile, 'gy')  57.9 us
    squeeze x1, local copies, waits for them, and re-layouts, per_device(): stiff = jnp.diagonal(local_block[0], axis1=1, axis2=2).astype(jnp.float32)  44.1 us
    all_gather x1, blocking collectives, per_device(): lax.all_gather(part, 'gx', axis=0, tiled=True)  14.9 us
    dot_general x1, matrix products, per_device(): jnp.einsum('snr,snq->srq', coupling[0], coupling[0], preferred_element_ty...  13.6 us
    dot_general x1, matrix products, per_device(): jnp.einsum('srk,srl->kl', basis, image, preferred_element_type=jnp.float32)  10.2 us
    gather x2, local copies, waits for them, and re-layouts, per_device(): stiff = jnp.diagonal(local_block[0], axis1=1, axis2=2).astype(jnp.float32)  6.53 us
  transfers between devices with their start and end apart: 1, of which 1 were waited for; matrix products, arithmetic and copies ran while one was open for 0% of the time, Pallas kernels for 0%

commit v1 on v0

v1 whole, which is shorter than its diff:
```python
import functools

import jax
import jax.numpy as jnp
from jax import lax
from jax.experimental import pallas as pl
from jax.experimental.pallas import tpu as pltpu
from jax.sharding import PartitionSpec as P

BLK = 128
NC = 512
ROUNDS = 3
R = 512
NI = 1024
RB = 4
VMEM_LIMIT = 24 << 20

F32 = jnp.float32
BF16 = jnp.bfloat16


def params():
    return pltpu.CompilerParams(vmem_limit_bytes=VMEM_LIMIT)


def in_vmem(*arrays):
    return [pltpu.with_memory_space_constraint(a, pltpu.VMEM) for a in arrays]


VSPEC = pl.BlockSpec(memory_space=pltpu.VMEM)
SSPEC = pl.BlockSpec(memory_space=pltpu.SMEM)
ASPEC = pl.BlockSpec(memory_space=pl.ANY)


def diag_kernel(block_ref, stiff_ref, held, sems):
    def copy(b):
        part = pl.ds(b * BLK, BLK)
        return pltpu.make_async_copy(block_ref.at[:, part, part], held.at[b], sems.at[b])

    for b in range(RB):
        copy(b).start()
    shape = (BLK, BLK)
    on = lax.broadcasted_iota(jnp.int32, shape, 0) == lax.broadcasted_iota(jnp.int32, shape, 1)
    for b in range(RB):
        copy(b).wait()
        tile = held[b].astype(F32)
        stiff_ref[:, b * BLK : (b + 1) * BLK] = jnp.sum(jnp.where(on[None], tile, 0.0), axis=1)


def diagonal(local_block):
    subs = local_block.shape[0]
    return pl.pallas_call(
        diag_kernel,
        out_shape=pltpu.VMEM((subs, R), F32),
        in_specs=[ASPEC],
        out_specs=VSPEC,
        scratch_shapes=[pltpu.VMEM((RB, subs, BLK, BLK), BF16), pltpu.SemaphoreType.DMA((RB,))],
        compiler_params=params(),
        name="diag",
    )(pltpu.with_memory_space_constraint(local_block, pltpu.HBM))


def schur_kernel(counts_ref, coupling_ref, block_ref, schur_ref):
    j = pl.program_id(0)
    for live in range(1, RB + 1):

        @pl.when(counts_ref[j] == live)
        def _():
            n = live * BLK
            c = coupling_ref[0, :, :n]
            gram = lax.dot_general(c, c, (((0,), (0,)), ((), ())), preferred_element_type=F32)
            schur_ref[0, :n, :n] = (block_ref[0, :n, :n].astype(F32) - gram).astype(BF16)
            if n < R:
                schur_ref[0, :n, n:] = jnp.zeros((n, R - n), BF16)
                schur_ref[0, n:, :] = jnp.zeros((R - n, R), BF16)


def schur_blocks(counts, coupling, local_block):
    subs = local_block.shape[0]
    return pl.pallas_call(
        schur_kernel,
        grid_spec=pltpu.PrefetchScalarGridSpec(
            num_scalar_prefetch=1,
            grid=(subs,),
            in_specs=[
                pl.BlockSpec((1, NI, R), lambda j, c: (j, 0, 0)),
                pl.BlockSpec((1, R, R), lambda j, c: (j, 0, 0)),
            ],
            out_specs=pl.BlockSpec((1, R, R), lambda j, c: (j, 0, 0)),
        ),
        out_shape=pltpu.VMEM((subs, R, R), BF16),
        compiler_params=params(),
        name="schur",
    )(counts, coupling, local_block)


def first_kernel(half, off_ref, times_ref, primal_ref, stiff_ref, *refs):
    *others, schur_ref, tile_ref, basis_ref = refs
    total = stiff_ref[...]
    for d, other in enumerate(others):
        total = total + times_ref[d].astype(F32) * other[...]
    weight = stiff_ref[...] / total
    subs = schur_ref.shape[0]
    rows = lax.broadcasted_iota(jnp.int32, (NC, R), 0)
    for j in range(subs):
        hit = rows == primal_ref[j : j + 1, :]
        basis_ref[j] = jnp.where(hit, weight[j : j + 1, :], 0.0).astype(BF16)
        add_tile(half, j, off_ref, schur_ref, basis_ref, tile_ref)


def second_kernel(half, off_ref, schur_ref, basis_ref, tile_ref):
    for j in range(schur_ref.shape[0]):
        add_tile(half, j, off_ref, schur_ref, basis_ref, tile_ref)


def add_tile(half, j, off_ref, schur_ref, basis_ref, tile_ref):
    off = pl.multiple_of(off_ref[0], half)
    part = basis_ref[j, pl.ds(off, half), :]
    image = lax.dot_general(
        schur_ref[j], part, (((1,), (1,)), ((), ())), preferred_element_type=F32
    ).astype(BF16)
    term = jnp.dot(basis_ref[j], image, preferred_element_type=F32)
    if j == 0:
        tile_ref[...] = term
    else:
        tile_ref[...] += term


def split_kernel(rows, me_ref, own_ref, other_ref, *outs):
    for d, out in enumerate(outs):
        at = pl.ds(pl.multiple_of((me_ref[0] ^ d) * rows, rows), rows)
        out[...] = own_ref[at, :] + other_ref[at, :]


def sum_kernel(*refs):
    *pieces, out = refs
    total = pieces[0][...]
    for piece in pieces[1:]:
        total = total + piece[...]
    out[...] = total


def scale_kernel(chips, rows, half, me_ref, *refs):
    own, other = refs[:chips], refs[chips : 2 * chips]
    out_ref, tile, sems = refs[2 * chips :]
    chip, core = me_ref[0], me_ref[1]
    for pieces, column in ((own, core), (other, 1 - core)):
        for d, piece in enumerate(pieces):
            at = pl.ds(pl.multiple_of((chip ^ d) * rows, rows), rows)
            tile[at, pl.ds(pl.multiple_of(column * half, half), half)] = piece[...]
    mean = jnp.sum(jnp.abs(tile[...]), axis=1, keepdims=True) / NC
    scale = 1.0 / jnp.sqrt(mean + 1e-06)
    across = jnp.broadcast_to(scale, (NC, BLK)).T[:1, :]

    def copy(b):
        at = pl.ds(b * BLK, BLK)
        return pltpu.make_async_copy(tile.at[at], out_ref.at[at], sems.at[b])

    for b in range(NC // BLK):
        at = slice(b * BLK, (b + 1) * BLK)
        tile[at, :] = tile[at, :] * scale[at, :] * across
        copy(b).start()
    for b in range(NC // BLK):
        copy(b).wait()


def per_device(columns, line, coupling, local_block, counts, primal, partner):
    chips, half, rows = line // 2, NC // 2, NC // (line // 2)
    coupling, local_block, counts, primal = coupling[0], local_block[0], counts[0], primal[0]
    subs = coupling.shape[0]
    column, place = lax.axis_index("gx"), lax.axis_index("gy")
    core, chip = place % 2, place // 2
    spot = jnp.stack([chip, core]).astype(jnp.int32)

    stiff = diagonal(local_block)
    others, times = [], []
    for d in range(1, columns):
        others.append(lax.ppermute(stiff, "gx", [(i, i ^ d) for i in range(columns)]))
        times.append(jnp.sum((partner[:, column] == (column ^ d)).astype(jnp.int32)))
    times = jnp.stack(times)

    schur = schur_blocks(counts, coupling, local_block)

    first, basis = pl.pallas_call(
        functools.partial(first_kernel, half),
        out_shape=(pltpu.VMEM((NC, half), F32), pltpu.VMEM((subs, NC, R), BF16)),
        in_specs=[SSPEC, SSPEC] + [VSPEC] * (columns + 2),
        out_specs=(VSPEC, VSPEC),
        compiler_params=params(),
        name="first_half",
    )(((1 - core) * half)[None], times, primal, *in_vmem(stiff, *others, schur))
    swap = [(i, i ^ 1) for i in range(line)]
    other_core = lax.ppermute(first, "gy", swap)
    second = pl.pallas_call(
        functools.partial(second_kernel, half),
        out_shape=pltpu.VMEM((NC, half), F32),
        in_specs=[SSPEC, VSPEC, VSPEC],
        out_specs=VSPEC,
        compiler_params=params(),
        name="second_half",
    )((core * half)[None], *in_vmem(schur, basis))

    pieces = pl.pallas_call(
        functools.partial(split_kernel, rows),
        out_shape=tuple(pltpu.VMEM((rows, half), F32) for _ in range(chips)),
        in_specs=[SSPEC, VSPEC, VSPEC],
        out_specs=(VSPEC,) * chips,
        compiler_params=params(),
        name="split",
    )(spot, *in_vmem(second, other_core))

    def hop(d):
        return [(i, i ^ (2 * d)) for i in range(line)]

    arrived = [lax.ppermute(pieces[d], "gy", hop(d)) for d in range(1, chips)]
    mine = pl.pallas_call(
        sum_kernel,
        out_shape=pltpu.VMEM((rows, half), F32),
        in_specs=[VSPEC] * chips,
        out_specs=VSPEC,
        compiler_params=params(),
        name="sum",
    )(*in_vmem(pieces[0], *arrived))
    own = [mine] + [lax.ppermute(mine, "gy", hop(d)) for d in range(1, chips)]
    other = [lax.ppermute(piece, "gy", swap) for piece in own]
    result = pl.pallas_call(
        functools.partial(scale_kernel, chips, rows, half),
        out_shape=jax.ShapeDtypeStruct((NC, NC), F32),
        in_specs=[SSPEC] + [VSPEC] * (2 * chips),
        out_specs=ASPEC,
        scratch_shapes=[pltpu.VMEM((NC, NC), F32), pltpu.SemaphoreType.DMA((NC // BLK,))],
        compiler_params=params(),
        name="scale",
    )(spot, *in_vmem(*own, *other))
    return result[None]


def solution(mesh):
    placed = (
        P("gx", "gy", None, None),
        P("gx", "gy", None, None),
        P("gx", "gy"),
        P("gx", "gy", None),
        P(),
    )
    body = functools.partial(per_device, mesh.shape["gx"], mesh.shape["gy"])
    return jax.shard_map(
        body, mesh=mesh, in_specs=placed, out_specs=P("gx", None, None), check_vma=False
    )
```

time: 171 us -> 60.2 us (0.35); the launches traced: 168 us -> 59.9 us
  waiting for transfers between devices: 57.9 us -> 13.4 us
  local copies, waits for them, and re-layouts: 52.1 us -> 13.9 us
  matrix products: 23.7 us -> 0 us
  Pallas kernels: 0 us -> 16.1 us
  blocking collectives: 14.9 us -> 0 us
  starting transfers between devices: 0.01 us -> 13.4 us
  between operations: 13.4 us -> 0.11 us
  other arithmetic: 5.84 us -> 2.84 us
    psum x1 -> x0, waiting for transfers between devices: 57.9 us -> none  [per_device(): summed = lax.psum(tile, 'gy')]
    squeeze x1 -> x0, local copies, waits for them, and re-layouts: 44.1 us -> none  [per_device(): stiff = jnp.diagonal(local_block[0], axis1=1, axis2=2).astype(jnp.float32)]
    dot_general x2 -> x0, matrix products: 23.7 us -> none  [the longest x1 13.6 us: per_device(): jnp.einsum('snr,snq->srq', coupling[0], coupling[0], preferred_element_ty...]
    pallas_call x0 -> x7, Pallas kernels: none -> 16.1 us  [the longest x1 4.83 us: per_device(): pl.pallas_call(functools.partial(first_kernel, half), out_shape=(pltpu.VM...]
    all_gather x1 -> x0, blocking collectives: 14.9 us -> none  [per_device(): lax.all_gather(part, 'gx', axis=0, tiled=True)]
    unnamed x4 -> x18, local copies, waits for them, and re-layouts: 0.01 us -> 13.9 us
    ppermute x0 -> x14, waiting for transfers between devices: none -> 13.4 us  [the longest x3 6.7 us: per_device(): arrived = [lax.ppermute(pieces[d], 'gy', hop(d)) for d in range(1, chips)]]
    ppermute x0 -> x14, starting transfers between devices: none -> 13.4 us  [the longest x3 5.76 us: per_device(): lax.ppermute(stiff, 'gx', [(i, i ^ d) for i in range(columns)])]
  transfers between devices with their start and end apart: 1 -> 14, of which waited for: 1 -> 7; matrix products, arithmetic and copies ran while one was open for 0% -> 5% of each run, Pallas kernels for 0% -> 12%
where the time goes in v1:
time: 60.2 us; the launch traced here: 59.9 us
  Pallas kernels  16.1 us (27%)
  local copies, waits for them, and re-layouts  13.9 us (23%)
  starting transfers between devices  13.4 us (22%)
  waiting for transfers between devices  13.4 us (22%)
  other arithmetic  2.84 us (5%)
    unnamed x18, local copies, waits for them, and re-layouts  13.9 us
    ppermute x3, waiting for transfers between devices, per_device(): arrived = [lax.ppermute(pieces[d], 'gy', hop(d)) for d in range(1, chips)]  6.7 us
    ppermute x3, starting transfers between devices, per_device(): lax.ppermute(stiff, 'gx', [(i, i ^ d) for i in range(columns)])  5.76 us
    ppermute x3, waiting for transfers between devices, per_device(): own = [mine] + [lax.ppermute(mine, 'gy', hop(d)) for d in range(1, chips)]  5.4 us
    pallas_call x1, Pallas kernels, per_device(): pl.pallas_call(functools.partial(first_kernel, half), out_shape=(pltpu.VM...  4.83 us
    pallas_call x1, Pallas kernels, schur_blocks(): pl.pallas_call(schur_kernel, grid_spec=pltpu.PrefetchScalarGridSpec(num_s...  4.58 us
    ppermute x3, starting transfers between devices, per_device(): arrived = [lax.ppermute(pieces[d], 'gy', hop(d)) for d in range(1, chips)]  4.09 us
    ppermute x3, starting transfers between devices, per_device(): own = [mine] + [lax.ppermute(mine, 'gy', hop(d)) for d in range(1, chips)]  3.55 us
  transfers between devices with their start and end apart: 14, of which 7 were waited for; matrix products, arithmetic and copies ran while one was open for 5% of the time, Pallas kernels for 12%

profile of v1, /device:TPU:0, one launch (start us, length us, event | category | flops | bytes accessed | tf_op | source)
XLA Modules:
  0.0 59.9 jit_solution(6556976071007139464)
XLA Ops:
  0.0 1.4 %diag.1.stiff_ref = f32[8,512]{1,0:T(8,128)S(1)} custom-call(bf16[8,512,512]{2,1,0:T(8,128)(2,1)} %bitcast.12), custom_call_target="tpu_custom_call" | custom-call | tf_op jit(solution)/shard_map/diag/pallas_call | solution.py:52
  1.4 5.1 %collective-permute-start.2 = (f32[8,512]{1,0:T(8,128)S(1)}, f32[8,512]{1,0:T(8,128)S(1)}, u32[]{:S(2)}, u32[]{:S(2)}) collective-permute-start(f32[8,512]{1,0:T(8,128)S(1)} %diag.1.stiff_ref), channel_id=1, source_target_pairs={{0,24},{8,16},{16,8},{24,0},{1,25},{9,17},{17,9},{25,1},{2,26},{10... | collective-permute-start | bytes 49160 | tf_op jit(solution)/shard_map/ppermute | solution.py:178
  6.5 0.0 collective-permute-start.1
  6.5 0.6 %collective-permute-start = (f32[8,512]{1,0:T(8,128)S(1)}, f32[8,512]{1,0:T(8,128)S(1)}, u32[]{:S(2)}, u32[]{:S(2)}) collective-permute-start(f32[8,512]{1,0:T(8,128)S(1)} %diag.1.stiff_ref), channel_id=1, source_target_pairs={{0,8},{8,0},{16,24},{24,16},{1,9},{9,1},{17,25},{25,17},{2,10},{10... | collective-permute-start | bytes 49160 | tf_op jit(solution)/shard_map/ppermute | solution.py:178
  7.1 0.8 %convert_reduce_fusion.2 = (s32[]{:T(128)}, s32[]{:T(128)}, s32[]{:T(128)}) fusion(s32[3,4]{1,0:T(4,128)S(1)} %copy-done.8, s32[]{:T(128)S(6)} %select_n.18, s32[]{:T(128)S(6)} %xor.9, s32[]{:T(128)S(6)} %xor.10, s32[]{:T(128)S(6)} %xor.11), kind=kLoop, calls=%fused_computation.2 | loop fusion | flops 24 | bytes 40 | tf_op jit(solution)/shard_map/reduce_sum | solution.py:179
  8.0 2.0 %pad_add_fusion.1.times_ref = s32[3]{0:T(128)S(1)} fusion(s32[1]{0:T(128)} %bitcast.9, s32[1]{0:T(128)} %bitcast.8, s32[1]{0:T(128)} %bitcast.7), kind=kLoop, calls=%fused_computation.4 | loop fusion | flops 6 | bytes 24 | tf_op jit(solution)/shard_map/stack | solution.py:180
  9.9 2.2 %copy-done.2 = bf16[1,8,512,512]{3,2,1,0:T(8,128)(2,1)S(1)} copy-done((bf16[1,8,512,512]{3,2,1,0:T(8,128)(2,1)S(1)}, bf16[1,8,512,512]{3,2,1,0:T(8,128)(2,1)}, u32[]{:S(2)}) %copy-start.2) | copy-done | bytes 4194328
  12.1 3.4 %copy-done.3 = bf16[1,8,1024,512]{3,2,1,0:T(8,128)(2,1)S(1)} copy-done((bf16[1,8,1024,512]{3,2,1,0:T(8,128)(2,1)S(1)}, bf16[1,8,1024,512]{3,2,1,0:T(8,128)(2,1)}, u32[]{:S(2)}) %copy-start.3) | copy-done | bytes 8388632
  15.5 4.6 %schur.1.refs_3_.schur_ref = bf16[8,512,512]{2,1,0:T(8,128)(2,1)S(1)} custom-call(s32[8]{0:T(128)S(1)} %bitcast.16, bf16[8,1024,512]{2,1,0:T(8,128)(2,1)S(1)} %bitcast.14, bf16[8,512,512]{2,1,0:T(8,128)(2,1)S(1)} %bitcast.13), custom_call_target="tpu_custom_call" | custom-call | tf_op jit(solution)/shard_map/schur/pallas_call | solution.py:80
  20.1 0.0 collective-permute-done.2.refs_2_
  20.1 0.0 collective-permute-done.1.refs_1_
  20.1 4.8 %first_half.1 = (f32[512,256]{1,0:T(8,128)S(1)}, bf16[8,512,512]{2,1,0:T(8,128)(2,1)S(1)}) custom-call(s32[1]{0:T(128)} %bitcast.6.off_ref, s32[3]{0:T(128)S(1)} %pad_add_fusion.1.times_ref, s32[8,512]{1,0:T(8,128)S(1)} %bitcast.15, f32[8,512]{1,0:T(8,128)S(1)} %diag.1.stiff_ref, f32[8,512]{1,0:T(8,128)S(1)} %collective-permute-done.refs_0_, ...), custom_call_target="tpu_custom_call" | custom-call | tf_op jit(solution)/shard_map/first_half/pallas_call | solution.py:184
  25.0 2.0 %copy-done = bf16[8,512,512]{2,1,0:T(8,128)(2,1)} copy-done((bf16[8,512,512]{2,1,0:T(8,128)(2,1)}, bf16[8,512,512]{2,1,0:T(8,128)(2,1)S(1)}, u32[]{:S(2)}) %copy-start) | copy-done | bytes 4194328
  26.9 2.0 %copy-done.4 = bf16[8,512,512]{2,1,0:T(8,128)(2,1)} copy-done((bf16[8,512,512]{2,1,0:T(8,128)(2,1)}, bf16[8,512,512]{2,1,0:T(8,128)(2,1)S(1)}, u32[]{:S(2)}) %copy-start.4) | copy-done | bytes 4194328
  28.9 0.1 pad_add_fusion.me_ref
  29.0 2.2 %copy-done.1 = bf16[8,512,512]{2,1,0:T(8,128)(2,1)S(1)} copy-done((bf16[8,512,512]{2,1,0:T(8,128)(2,1)S(1)}, bf16[8,512,512]{2,1,0:T(8,128)(2,1)}, u32[]{:S(2)}) %copy-start.1) | copy-done | bytes 4194328
  31.2 2.2 %copy-done.5 = bf16[8,512,512]{2,1,0:T(8,128)(2,1)S(1)} copy-done((bf16[8,512,512]{2,1,0:T(8,128)(2,1)S(1)}, bf16[8,512,512]{2,1,0:T(8,128)(2,1)}, u32[]{:S(2)}) %copy-start.5) | copy-done | bytes 4194328
  33.4 2.8 %second_half.1.own_ref = f32[512,256]{1,0:T(8,128)S(1)} custom-call(s32[1]{0:T(128)} %bitcast.2.off_ref, bf16[8,512,512]{2,1,0:T(8,128)(2,1)S(1)} %copy-done.1, bf16[8,512,512]{2,1,0:T(8,128)(2,1)S(1)} %copy-done.5), custom_call_target="tpu_custom_call" | custom-call | tf_op jit(solution)/shard_map/second_half/pallas_call | solution.py:194
  36.2 0.6 %split.1 = (f32[128,256]{1,0:T(8,128)S(1)}, f32[128,256]{1,0:T(8,128)S(1)}, f32[128,256]{1,0:T(8,128)S(1)}, f32[128,256]{1,0:T(8,128)S(1)}) custom-call(s32[2]{0:T(128)S(1)} %pad_add_fusion.me_ref, f32[512,256]{1,0:T(8,128)S(1)} %second_half.1.own_ref, f32[512,256]{1,0:T(8,128)S(1)} %collective-permute-done.3.other_ref), custom_call_target="tpu_custom_call" | custom-call | tf_op jit(solution)/shard_map/split/pallas_call | solution.py:203
  36.8 1.7 %collective-permute-start.4 = (f32[128,256]{1,0:T(8,128)S(1)}, f32[128,256]{1,0:T(8,128)S(1)}, u32[]{:S(2)}, u32[]{:S(2)}) collective-permute-start(f32[128,256]{1,0:T(8,128)S(1)} %get-tuple-element.14), channel_id=1, source_target_pairs={{0,2},{1,3},{2,0},{3,1},{4,6},{5,7},{6,4},{7,5},{8,10},{9,11},{10,... | collective-permute-start | bytes 393224 | tf_op jit(solution)/shard_map/ppermute | solution.py:215
  38.5 2.4 %collective-permute-start.5 = (f32[128,256]{1,0:T(8,128)S(1)}, f32[128,256]{1,0:T(8,128)S(1)}, u32[]{:S(2)}, u32[]{:S(2)}) collective-permute-start(f32[128,256]{1,0:T(8,128)S(1)} %get-tuple-element.15), channel_id=1, source_target_pairs={{0,4},{1,5},{2,6},{3,7},{4,0},{5,1},{6,2},{7,3},{8,12},{9,13},{10,... | collective-permute-start | bytes 393224 | tf_op jit(solution)/shard_map/ppermute | solution.py:215
  40.9 1.9 %collective-permute-done.4.refs_1_ = f32[128,256]{1,0:T(8,128)S(1)} collective-permute-done((f32[128,256]{1,0:T(8,128)S(1)}, f32[128,256]{1,0:T(8,128)S(1)}, u32[]{:S(2)}, u32[]{:S(2)}) %collective-permute-start.4) | collective-permute-done | bytes 131104 | tf_op jit(solution)/shard_map/ppermute | solution.py:215
  42.8 4.8 %collective-permute-done.5.refs_2_ = f32[128,256]{1,0:T(8,128)S(1)} collective-permute-done((f32[128,256]{1,0:T(8,128)S(1)}, f32[128,256]{1,0:T(8,128)S(1)}, u32[]{:S(2)}, u32[]{:S(2)}) %collective-permute-start.5) | collective-permute-done | bytes 131104 | tf_op jit(solution)/shard_map/ppermute | solution.py:215
  47.6 1.6 %collective-permute-start.9 = (f32[128,256]{1,0:T(8,128)S(1)}, f32[128,256]{1,0:T(8,128)S(1)}, u32[]{:S(2)}, u32[]{:S(2)}) collective-permute-start(f32[128,256]{1,0:T(8,128)S(1)} %sum.1.refs_0_), channel_id=1, source_target_pairs={{0,6},{1,7},{2,4},{3,5},{4,2},{5,3},{6,0},{7,1},{8,14},{9,15},{10,... | collective-permute-start | bytes 393224 | tf_op jit(solution)/shard_map/ppermute | solution.py:224
  49.2 1.4 %collective-permute-start.8 = (f32[128,256]{1,0:T(8,128)S(1)}, f32[128,256]{1,0:T(8,128)S(1)}, u32[]{:S(2)}, u32[]{:S(2)}) collective-permute-start(f32[128,256]{1,0:T(8,128)S(1)} %sum.1.refs_0_), channel_id=1, source_target_pairs={{0,4},{1,5},{2,6},{3,7},{4,0},{5,1},{6,2},{7,3},{8,12},{9,13},{10,... | collective-permute-start | bytes 393224 | tf_op jit(solution)/shard_map/ppermute | solution.py:224
  50.6 0.6 collective-permute-start.7
  51.2 3.5 %collective-permute-done.9.refs_3_ = f32[128,256]{1,0:T(8,128)S(1)} collective-permute-done((f32[128,256]{1,0:T(8,128)S(1)}, f32[128,256]{1,0:T(8,128)S(1)}, u32[]{:S(2)}, u32[]{:S(2)}) %collective-permute-start.9) | collective-permute-done | bytes 131104 | tf_op jit(solution)/shard_map/ppermute | solution.py:224
  54.7 1.2 %collective-permute-done.8.refs_2_ = f32[128,256]{1,0:T(8,128)S(1)} collective-permute-done((f32[128,256]{1,0:T(8,128)S(1)}, f32[128,256]{1,0:T(8,128)S(1)}, u32[]{:S(2)}, u32[]{:S(2)}) %collective-permute-start.8) | collective-permute-done | bytes 131104 | tf_op jit(solution)/shard_map/ppermute | solution.py:224
  55.8 0.8 %collective-permute-done.7.refs_1_ = f32[128,256]{1,0:T(8,128)S(1)} collective-permute-done((f32[128,256]{1,0:T(8,128)S(1)}, f32[128,256]{1,0:T(8,128)S(1)}, u32[]{:S(2)}, u32[]{:S(2)}) %collective-permute-start.7) | collective-permute-done | bytes 131104 | tf_op jit(solution)/shard_map/ppermute | solution.py:224
  56.6 0.6 collective-permute-done.12.refs_6_
  57.2 0.8 %collective-permute-done.11.refs_5_ = f32[128,256]{1,0:T(8,128)S(1)} collective-permute-done((f32[128,256]{1,0:T(8,128)S(1)}, f32[128,256]{1,0:T(8,128)S(1)}, u32[]{:S(2)}, u32[]{:S(2)}) %collective-permute-start.11) | collective-permute-done | bytes 131104 | tf_op jit(solution)/shard_map/ppermute | solution.py:225
  58.0 1.9 %scale.1 = f32[512,512]{1,0:T(8,128)} custom-call(s32[2]{0:T(128)S(1)} %pad_add_fusion.me_ref, f32[128,256]{1,0:T(8,128)S(1)} %sum.1.refs_0_, f32[128,256]{1,0:T(8,128)S(1)} %collective-permute-done.7.refs_1_, f32[128,256]{1,0:T(8,128)S(1)} %collective-permute-done.8.refs_2_, f32[128,256]{1,0:T(8,128)S(1)} %collective-permute-done.9.refs_3_, ...), custom_call_target="tpu_custom_call" | custom-call | tf_op jit(solution)/shard_map/scale/pallas_call | solution.py:226
  (24 shorter events, 0.1 us)
Async XLA Ops:
  0.0 7.1 %copy-start.8 = (s32[3,4]{1,0:T(4,128)S(1)}, s32[3,4]{1,0:T(4,128)}, u32[]{:S(2)}) copy-start(s32[3,4]{1,0:T(4,128)} %param.9) | copy-start | bytes 148
  0.0 9.9 %copy-start.7 = (s32[1,8]{1,0:T(1,128)S(1)}, s32[1,8]{1,0:T(1,128)}, u32[]{:S(2)}) copy-start(s32[1,8]{1,0:T(1,128)} %param.7) | copy-start | bytes 100
  1.4 18.7 %collective-permute-start.2 = (f32[8,512]{1,0:T(8,128)S(1)}, f32[8,512]{1,0:T(8,128)S(1)}, u32[]{:S(2)}, u32[]{:S(2)}) collective-permute-start(f32[8,512]{1,0:T(8,128)S(1)} %diag.1.stiff_ref), channel_id=1, source_target_pairs={{0,24},{8,16},{16,8},{24,0},{1,25},{9,17},{17,9},{25,1},{2,26},{10... | collective-permute-start | bytes 49160 | tf_op jit(solution)/shard_map/ppermute | solution.py:178
  6.5 13.6 %collective-permute-start.1 = (f32[8,512]{1,0:T(8,128)S(1)}, f32[8,512]{1,0:T(8,128)S(1)}, u32[]{:S(2)}, u32[]{:S(2)}) collective-permute-start(f32[8,512]{1,0:T(8,128)S(1)} %diag.1.stiff_ref), channel_id=1, source_target_pairs={{0,16},{8,24},{16,0},{24,8},{1,17},{9,25},{17,1},{25,9},{2,18},{10... | collective-permute-start | bytes 49160 | tf_op jit(solution)/shard_map/ppermute | solution.py:178
  6.5 13.6 %collective-permute-start = (f32[8,512]{1,0:T(8,128)S(1)}, f32[8,512]{1,0:T(8,128)S(1)}, u32[]{:S(2)}, u32[]{:S(2)}) collective-permute-start(f32[8,512]{1,0:T(8,128)S(1)} %diag.1.stiff_ref), channel_id=1, source_target_pairs={{0,8},{8,0},{16,24},{24,16},{1,9},{9,1},{17,25},{25,17},{2,10},{10... | collective-permute-start | bytes 49160 | tf_op jit(solution)/shard_map/ppermute | solution.py:178
  9.9 2.2 %copy-start.2 = (bf16[1,8,512,512]{3,2,1,0:T(8,128)(2,1)S(1)}, bf16[1,8,512,512]{3,2,1,0:T(8,128)(2,1)}, u32[]{:S(2)}) copy-start(bf16[1,8,512,512]{3,2,1,0:T(8,128)(2,1)} %param.6) | copy-start | bytes 12582916
  12.1 3.4 %copy-start.3 = (bf16[1,8,1024,512]{3,2,1,0:T(8,128)(2,1)S(1)}, bf16[1,8,1024,512]{3,2,1,0:T(8,128)(2,1)}, u32[]{:S(2)}) copy-start(bf16[1,8,1024,512]{3,2,1,0:T(8,128)(2,1)} %param.5) | copy-start | bytes 25165828
  15.5 4.6 %copy-start.6 = (s32[1,8,512]{2,1,0:T(8,128)S(1)}, s32[1,8,512]{2,1,0:T(8,128)}, u32[]{:S(2)}) copy-start(s32[1,8,512]{2,1,0:T(8,128)} %param.8) | copy-start | bytes 49156
  25.0 2.0 %copy-start = (bf16[8,512,512]{2,1,0:T(8,128)(2,1)}, bf16[8,512,512]{2,1,0:T(8,128)(2,1)S(1)}, u32[]{:S(2)}) copy-start(bf16[8,512,512]{2,1,0:T(8,128)(2,1)S(1)} %schur.1.refs_3_.schur_ref) | copy-start | bytes 12582916
  26.9 2.0 %copy-start.4 = (bf16[8,512,512]{2,1,0:T(8,128)(2,1)}, bf16[8,512,512]{2,1,0:T(8,128)(2,1)S(1)}, u32[]{:S(2)}) copy-start(bf16[8,512,512]{2,1,0:T(8,128)(2,1)S(1)} %get-tuple-element.11.basis_ref) | copy-start | bytes 12582916
  28.9 7.3 %collective-permute-start.3 = (f32[512,256]{1,0:T(8,128)S(1)}, f32[512,256]{1,0:T(8,128)S(1)}, u32[]{:S(2)}, u32[]{:S(2)}) collective-permute-start(f32[512,256]{1,0:T(8,128)S(1)} %get-tuple-element.12), channel_id=1, source_target_pairs={{0,1},{1,0},{2,3},{3,2},{4,5},{5,4},{6,7},{7,6},{8,9},{9,8},{10,11... | collective-permute-start | bytes 1572872 | tf_op jit(solution)/shard_map/ppermute | solution.py:193
  29.0 2.2 %copy-start.1 = (bf16[8,512,512]{2,1,0:T(8,128)(2,1)S(1)}, bf16[8,512,512]{2,1,0:T(8,128)(2,1)}, u32[]{:S(2)}) copy-start(bf16[8,512,512]{2,1,0:T(8,128)(2,1)} %copy-done) | copy-start | bytes 12582916
  31.2 2.2 %copy-start.5 = (bf16[8,512,512]{2,1,0:T(8,128)(2,1)S(1)}, bf16[8,512,512]{2,1,0:T(8,128)(2,1)}, u32[]{:S(2)}) copy-start(bf16[8,512,512]{2,1,0:T(8,128)(2,1)} %copy-done.4) | copy-start | bytes 12582916
  36.8 6.0 %collective-permute-start.4 = (f32[128,256]{1,0:T(8,128)S(1)}, f32[128,256]{1,0:T(8,128)S(1)}, u32[]{:S(2)}, u32[]{:S(2)}) collective-permute-start(f32[128,256]{1,0:T(8,128)S(1)} %get-tuple-element.14), channel_id=1, source_target_pairs={{0,2},{1,3},{2,0},{3,1},{4,6},{5,7},{6,4},{7,5},{8,10},{9,11},{10,... | collective-permute-start | bytes 393224 | tf_op jit(solution)/shard_map/ppermute | solution.py:215
  38.5 9.1 %collective-permute-start.5 = (f32[128,256]{1,0:T(8,128)S(1)}, f32[128,256]{1,0:T(8,128)S(1)}, u32[]{:S(2)}, u32[]{:S(2)}) collective-permute-start(f32[128,256]{1,0:T(8,128)S(1)} %get-tuple-element.15), channel_id=1, source_target_pairs={{0,4},{1,5},{2,6},{3,7},{4,0},{5,1},{6,2},{7,3},{8,12},{9,13},{10,... | collective-permute-start | bytes 393224 | tf_op jit(solution)/shard_map/ppermute | solution.py:215
  40.9 6.7 %collective-permute-start.6 = (f32[128,256]{1,0:T(8,128)S(1)}, f32[128,256]{1,0:T(8,128)S(1)}, u32[]{:S(2)}, u32[]{:S(2)}) collective-permute-start(f32[128,256]{1,0:T(8,128)S(1)} %get-tuple-element.16), channel_id=1, source_target_pairs={{0,6},{1,7},{2,4},{3,5},{4,2},{5,3},{6,0},{7,1},{8,14},{9,15},{10,... | collective-permute-start | bytes 393224 | tf_op jit(solution)/shard_map/ppermute | solution.py:215
  47.6 7.0 %collective-permute-start.9 = (f32[128,256]{1,0:T(8,128)S(1)}, f32[128,256]{1,0:T(8,128)S(1)}, u32[]{:S(2)}, u32[]{:S(2)}) collective-permute-start(f32[128,256]{1,0:T(8,128)S(1)} %sum.1.refs_0_), channel_id=1, source_target_pairs={{0,6},{1,7},{2,4},{3,5},{4,2},{5,3},{6,0},{7,1},{8,14},{9,15},{10,... | collective-permute-start | bytes 393224 | tf_op jit(solution)/shard_map/ppermute | solution.py:224
  49.2 6.6 %collective-permute-start.8 = (f32[128,256]{1,0:T(8,128)S(1)}, f32[128,256]{1,0:T(8,128)S(1)}, u32[]{:S(2)}, u32[]{:S(2)}) collective-permute-start(f32[128,256]{1,0:T(8,128)S(1)} %sum.1.refs_0_), channel_id=1, source_target_pairs={{0,4},{1,5},{2,6},{3,7},{4,0},{5,1},{6,2},{7,3},{8,12},{9,13},{10,... | collective-permute-start | bytes 393224 | tf_op jit(solution)/shard_map/ppermute | solution.py:224
  50.6 6.0 %collective-permute-start.7 = (f32[128,256]{1,0:T(8,128)S(1)}, f32[128,256]{1,0:T(8,128)S(1)}, u32[]{:S(2)}, u32[]{:S(2)}) collective-permute-start(f32[128,256]{1,0:T(8,128)S(1)} %sum.1.refs_0_), channel_id=1, source_target_pairs={{0,2},{1,3},{2,0},{3,1},{4,6},{5,7},{6,4},{7,5},{8,10},{9,11},{10,... | collective-permute-start | bytes 393224 | tf_op jit(solution)/shard_map/ppermute | solution.py:224
  51.2 5.4 %collective-permute-start.10 = (f32[128,256]{1,0:T(8,128)S(1)}, f32[128,256]{1,0:T(8,128)S(1)}, u32[]{:S(2)}, u32[]{:S(2)}) collective-permute-start(f32[128,256]{1,0:T(8,128)S(1)} %sum.1.refs_0_), channel_id=1, source_target_pairs={{0,1},{1,0},{2,3},{3,2},{4,5},{5,4},{6,7},{7,6},{8,9},{9,8},{10,11... | collective-permute-start | bytes 393224 | tf_op jit(solution)/shard_map/ppermute | solution.py:225
  54.7 1.9 %collective-permute-start.13 = (f32[128,256]{1,0:T(8,128)S(1)}, f32[128,256]{1,0:T(8,128)S(1)}, u32[]{:S(2)}, u32[]{:S(2)}) collective-permute-start(f32[128,256]{1,0:T(8,128)S(1)} %collective-permute-done.9.refs_3_), channel_id=1, source_target_pairs={{0,1},{1,0},{2,3},{3,2},{4,5},{5,4},{6,7},{7,6},{8,9},{9,8},{10,11... | collective-permute-start | bytes 393224 | tf_op jit(solution)/shard_map/ppermute | solution.py:225
  55.8 1.3 %collective-permute-start.12 = (f32[128,256]{1,0:T(8,128)S(1)}, f32[128,256]{1,0:T(8,128)S(1)}, u32[]{:S(2)}, u32[]{:S(2)}) collective-permute-start(f32[128,256]{1,0:T(8,128)S(1)} %collective-permute-done.8.refs_2_), channel_id=1, source_target_pairs={{0,1},{1,0},{2,3},{3,2},{4,5},{5,4},{6,7},{7,6},{8,9},{9,8},{10,11... | collective-permute-start | bytes 393224 | tf_op jit(solution)/shard_map/ppermute | solution.py:225
  56.6 1.3 %collective-permute-start.11 = (f32[128,256]{1,0:T(8,128)S(1)}, f32[128,256]{1,0:T(8,128)S(1)}, u32[]{:S(2)}, u32[]{:S(2)}) collective-permute-start(f32[128,256]{1,0:T(8,128)S(1)} %collective-permute-done.7.refs_1_), channel_id=1, source_target_pairs={{0,1},{1,0},{2,3},{3,2},{4,5},{5,4},{6,7},{7,6},{8,9},{9,8},{10,11... | collective-permute-start | bytes 393224 | tf_op jit(solution)/shard_map/ppermute | solution.py:225

commit v2 on v1

--- a/solution.py
+++ b/solution.py
@@ -25,6 +25,10 @@
 
 def in_vmem(*arrays):
     return [pltpu.with_memory_space_constraint(a, pltpu.VMEM) for a in arrays]
+
+
+def in_hbm(*arrays):
+    return [pltpu.with_memory_space_constraint(a, pltpu.HBM) for a in arrays]
 
 
 VSPEC = pl.BlockSpec(memory_space=pltpu.VMEM)
@@ -57,7 +61,7 @@
         scratch_shapes=[pltpu.VMEM((RB, subs, BLK, BLK), BF16), pltpu.SemaphoreType.DMA((RB,))],
         compiler_params=params(),
         name="diag",
-    )(pltpu.with_memory_space_constraint(local_block, pltpu.HBM))
+    )(*in_hbm(local_block))
 
 
 def schur_kernel(counts_ref, coupling_ref, block_ref, schur_ref):
@@ -91,31 +95,41 @@
         out_shape=pltpu.VMEM((subs, R, R), BF16),
         compiler_params=params(),
         name="schur",
-    )(counts, coupling, local_block)
-
-
-def first_kernel(half, off_ref, times_ref, primal_ref, stiff_ref, *refs):
+    )(counts, *in_hbm(coupling, local_block))
+
+
+def place():
+    at = lax.axis_index("gy")
+    return lax.shift_right_logical(at, 1), at & 1
+
+
+def first_kernel(half, partner_ref, primal_ref, stiff_ref, *refs):
     *others, schur_ref, tile_ref, basis_ref = refs
+    column = lax.axis_index("gx")
+    off = (1 - place()[1]) * half
     total = stiff_ref[...]
     for d, other in enumerate(others):
-        total = total + times_ref[d].astype(F32) * other[...]
+        times = jnp.int32(0)
+        for r in range(ROUNDS):
+            times += (partner_ref[r, column] == (column ^ (d + 1))).astype(jnp.int32)
+        total = total + times.astype(F32) * other[...]
     weight = stiff_ref[...] / total
     subs = schur_ref.shape[0]
     rows = lax.broadcasted_iota(jnp.int32, (NC, R), 0)
     for j in range(subs):
         hit = rows == primal_ref[j : j + 1, :]
         basis_ref[j] = jnp.where(hit, weight[j : j + 1, :], 0.0).astype(BF16)
-        add_tile(half, j, off_ref, schur_ref, basis_ref, tile_ref)
-
-
-def second_kernel(half, off_ref, schur_ref, basis_ref, tile_ref):
+        add_tile(half, j, off, schur_ref, basis_ref, tile_ref)
+
+
+def second_kernel(half, schur_ref, basis_ref, tile_ref):
+    off = place()[1] * half
     for j in range(schur_ref.shape[0]):
-        add_tile(half, j, off_ref, schur_ref, basis_ref, tile_ref)
-
-
-def add_tile(half, j, off_ref, schur_ref, basis_ref, tile_ref):
-    off = pl.multiple_of(off_ref[0], half)
-    part = basis_ref[j, pl.ds(off, half), :]
+        add_tile(half, j, off, schur_ref, basis_ref, tile_ref)
+
+
+def add_tile(half, j, off, schur_ref, basis_ref, tile_ref):
+    part = basis_ref[j, pl.ds(pl.multiple_of(off, half), half), :]
     image = lax.dot_general(
         schur_ref[j], part, (((1,), (1,)), ((), ())), preferred_element_type=F32
     ).astype(BF16)
@@ -126,9 +140,10 @@
         tile_ref[...] += term
 
 
-def split_kernel(rows, me_ref, own_ref, other_ref, *outs):
+def split_kernel(rows, own_ref, other_ref, *outs):
+    chip = place()[0]
     for d, out in enumerate(outs):
-        at = pl.ds(pl.multiple_of((me_ref[0] ^ d) * rows, rows), rows)
+        at = pl.ds(pl.multiple_of((chip ^ d) * rows, rows), rows)
         out[...] = own_ref[at, :] + other_ref[at, :]
 
 
@@ -140,10 +155,10 @@
     out[...] = total
 
 
-def scale_kernel(chips, rows, half, me_ref, *refs):
+def scale_kernel(chips, rows, half, *refs):
     own, other = refs[:chips], refs[chips : 2 * chips]
     out_ref, tile, sems = refs[2 * chips :]
-    chip, core = me_ref[0], me_ref[1]
+    chip, core = place()
     for pieces, column in ((own, core), (other, 1 - core)):
         for d, piece in enumerate(pieces):
             at = pl.ds(pl.multiple_of((chip ^ d) * rows, rows), rows)
@@ -168,46 +183,40 @@
     chips, half, rows = line // 2, NC // 2, NC // (line // 2)
     coupling, local_block, counts, primal = coupling[0], local_block[0], counts[0], primal[0]
     subs = coupling.shape[0]
-    column, place = lax.axis_index("gx"), lax.axis_index("gy")
-    core, chip = place % 2, place // 2
-    spot = jnp.stack([chip, core]).astype(jnp.int32)
-
     stiff = diagonal(local_block)
-    others, times = [], []
-    for d in range(1, columns):
-        others.append(lax.ppermute(stiff, "gx", [(i, i ^ d) for i in range(columns)]))
-        times.append(jnp.sum((partner[:, column] == (column ^ d)).astype(jnp.int32)))
-    times = jnp.stack(times)
+    others = [
+        lax.ppermute(stiff, "gx", [(i, i ^ d) for i in range(columns)]) for d in range(1, columns)
+    ]
 
     schur = schur_blocks(counts, coupling, local_block)
 
     first, basis = pl.pallas_call(
         functools.partial(first_kernel, half),
         out_shape=(pltpu.VMEM((NC, half), F32), pltpu.VMEM((subs, NC, R), BF16)),
-        in_specs=[SSPEC, SSPEC] + [VSPEC] * (columns + 2),
+        in_specs=[SSPEC] + [VSPEC] * (columns + 2),
         out_specs=(VSPEC, VSPEC),
         compiler_params=params(),
         name="first_half",
-    )(((1 - core) * half)[None], times, primal, *in_vmem(stiff, *others, schur))
+    )(partner, primal, *in_vmem(stiff, *others, schur))
     swap = [(i, i ^ 1) for i in range(line)]
     other_core = lax.ppermute(first, "gy", swap)
     second = pl.pallas_call(
         functools.partial(second_kernel, half),
         out_shape=pltpu.VMEM((NC, half), F32),
-        in_specs=[SSPEC, VSPEC, VSPEC],
+        in_specs=[VSPEC, VSPEC],
         out_specs=VSPEC,
         compiler_params=params(),
         name="second_half",
-    )((core * half)[None], *in_vmem(schur, basis))
+    )(*in_vmem(schur, basis))
 
     pieces = pl.pallas_call(
         functools.partial(split_kernel, rows),
         out_shape=tuple(pltpu.VMEM((rows, half), F32) for _ in range(chips)),
-        in_specs=[SSPEC, VSPEC, VSPEC],
+        in_specs=[VSPEC, VSPEC],
         out_specs=(VSPEC,) * chips,
         compiler_params=params(),
         name="split",
-    )(spot, *in_vmem(second, other_core))
+    )(*in_vmem(second, other_core))
 
     def hop(d):
         return [(i, i ^ (2 * d)) for i in range(line)]
@@ -226,12 +235,12 @@
     result = pl.pallas_call(
         functools.partial(scale_kernel, chips, rows, half),
         out_shape=jax.ShapeDtypeStruct((NC, NC), F32),
-        in_specs=[SSPEC] + [VSPEC] * (2 * chips),
+        in_specs=[VSPEC] * (2 * chips),
         out_specs=ASPEC,
         scratch_shapes=[pltpu.VMEM((NC, NC), F32), pltpu.SemaphoreType.DMA((NC // BLK,))],
         compiler_params=params(),
         name="scale",
-    )(spot, *in_vmem(*own, *other))
+    )(*in_vmem(*own, *other))
     return result[None]
 
 

time: 60.2 us -> 45.5 us (0.76)
  local copies, waits for them, and re-layouts: 13.9 us -> 0.01 us
  other arithmetic: 2.84 us -> 0 us
  Pallas kernels: 16.1 us -> 18.5 us
  waiting for transfers between devices: 13.4 us -> 12.7 us
    unnamed x18 -> x6, local copies, waits for them, and re-layouts: 13.9 us -> 0.01 us
    pallas_call x1, Pallas kernels: 4.58 us -> 8.78 us  [schur_blocks(): pl.pallas_call(schur_kernel, grid_spec=pltpu.PrefetchScalarGridSpec(num_s...]
    another operation x2 -> x0, other arithmetic: 2.03 us -> none  [the longest x1 1.95 us: per_device(): times = jnp.stack(times)]
    reduce_sum x1 -> x0, other arithmetic: 0.81 us -> none  [per_device(): times.append(jnp.sum((partner[:, column] == column ^ d).astype(jnp.int32)))]
    pallas_call x1, Pallas kernels: 4.83 us -> 4.05 us  [per_device(): pl.pallas_call(functools.partial(first_kernel, half), out_shape=(pltpu.VM...]
  transfers between devices with their start and end apart: 14 -> 14, of which waited for: 7 -> 7; matrix products, arithmetic and copies ran while one was open for 5% -> 0% of each run, Pallas kernels for 12% -> 26%
where the time goes in v2:
time: 45.5 us; the launch traced here: 45.2 us
  Pallas kernels  18.5 us (41%)
  starting transfers between devices  13.8 us (30%)
  waiting for transfers between devices  12.7 us (28%)
    pallas_call x1, Pallas kernels, schur_blocks(): pl.pallas_call(schur_kernel, grid_spec=pltpu.PrefetchScalarGridSpec(num_s...  8.78 us
    ppermute x3, waiting for transfers between devices, per_device(): arrived = [lax.ppermute(pieces[d], 'gy', hop(d)) for d in range(1, chips)]  6.88 us
    ppermute x3, starting transfers between devices, per_device(): lax.ppermute(stiff, 'gx', [(i, i ^ d) for i in range(columns)])  5.76 us
    ppermute x3, waiting for transfers between devices, per_device(): own = [mine] + [lax.ppermute(mine, 'gy', hop(d)) for d in range(1, chips)]  4.83 us
    pallas_call x1, Pallas kernels, per_device(): pl.pallas_call(functools.partial(first_kernel, half), out_shape=(pltpu.VM...  4.05 us
    ppermute x3, starting transfers between devices, per_device(): arrived = [lax.ppermute(pieces[d], 'gy', hop(d)) for d in range(1, chips)]  3.97 us
    ppermute x3, starting transfers between devices, per_device(): own = [mine] + [lax.ppermute(mine, 'gy', hop(d)) for d in range(1, chips)]  3.55 us
    pallas_call x1, Pallas kernels, per_device(): pl.pallas_call(functools.partial(second_kernel, half), out_shape=pltpu.VM...  2.85 us
  transfers between devices with their start and end apart: 14, of which 7 were waited for; matrix products, arithmetic and copies ran while one was open for 0% of the time, Pallas kernels for 26%

profile of v2, /device:TPU:0, one launch (start us, length us, event | category | flops | bytes accessed | tf_op | source)
XLA Modules:
  0.0 45.2 jit_solution(5602609010622358579)
XLA Ops:
  0.0 1.4 %diag.1.stiff_ref = f32[8,512]{1,0:T(8,128)S(1)} custom-call(bf16[8,512,512]{2,1,0:T(8,128)(2,1)} %bitcast.7), custom_call_target="tpu_custom_call" | custom-call | tf_op jit(solution)/shard_map/diag/pallas_call | solution.py:56
  1.4 5.1 %collective-permute-start.2 = (f32[8,512]{1,0:T(8,128)S(1)}, f32[8,512]{1,0:T(8,128)S(1)}, u32[]{:S(2)}, u32[]{:S(2)}) collective-permute-start(f32[8,512]{1,0:T(8,128)S(1)} %diag.1.stiff_ref), channel_id=1, source_target_pairs={{0,24},{8,16},{16,8},{24,0},{1,25},{9,17},{17,9},{25,1},{2,26},{10... | collective-permute-start | bytes 49160 | tf_op jit(solution)/shard_map/ppermute | solution.py:188
  6.5 0.0 collective-permute-start.1
  6.5 0.6 %collective-permute-start = (f32[8,512]{1,0:T(8,128)S(1)}, f32[8,512]{1,0:T(8,128)S(1)}, u32[]{:S(2)}, u32[]{:S(2)}) collective-permute-start(f32[8,512]{1,0:T(8,128)S(1)} %diag.1.stiff_ref), channel_id=1, source_target_pairs={{0,8},{8,0},{16,24},{24,16},{1,9},{9,1},{17,25},{25,17},{2,10},{10... | collective-permute-start | bytes 49160 | tf_op jit(solution)/shard_map/ppermute | solution.py:188
  7.1 8.8 %schur.1.refs_3_.schur_ref = bf16[8,512,512]{2,1,0:T(8,128)(2,1)S(1)} custom-call(s32[8]{0:T(128)S(1)} %bitcast.6, bf16[8,1024,512]{2,1,0:T(8,128)(2,1)} %bitcast.9, bf16[8,512,512]{2,1,0:T(8,128)(2,1)} %bitcast.8), custom_call_target="tpu_custom_call" | custom-call | tf_op jit(solution)/shard_map/schur/pallas_call | solution.py:84
  15.9 0.0 collective-permute-done.2.refs_2_
  15.9 0.0 collective-permute-done.1.refs_1_
  15.9 0.0 collective-permute-done.refs_0_
  16.0 4.1 %first_half.1 = (f32[512,256]{1,0:T(8,128)S(1)}, bf16[8,512,512]{2,1,0:T(8,128)(2,1)S(1)}) custom-call(s32[3,4]{1,0:T(4,128)S(1)} %copy-done.1, s32[8,512]{1,0:T(8,128)S(1)} %bitcast.5, f32[8,512]{1,0:T(8,128)S(1)} %diag.1.stiff_ref, f32[8,512]{1,0:T(8,128)S(1)} %collective-permute-done.refs_0_, f32[8,512]{1,0:T(8,128)S(1)} %collective-permute-done.1.refs_1_, ...), custom_call_target="tpu_custom_call" | custom-call | tf_op jit(solution)/shard_map/first_half/pallas_call | solution.py:193
  20.0 0.1 collective-permute-start.3
  20.1 2.9 %second_half.1.own_ref = f32[512,256]{1,0:T(8,128)S(1)} custom-call(bf16[8,512,512]{2,1,0:T(8,128)(2,1)S(1)} %schur.1.refs_3_.schur_ref, bf16[8,512,512]{2,1,0:T(8,128)(2,1)S(1)} %get-tuple-element.11.basis_ref), custom_call_target="tpu_custom_call" | custom-call | tf_op jit(solution)/shard_map/second_half/pallas_call | solution.py:203
  23.0 0.0 collective-permute-done.3.other_ref
  23.0 0.1 split.1
  23.1 2.4 %collective-permute-start.4 = (f32[128,256]{1,0:T(8,128)S(1)}, f32[128,256]{1,0:T(8,128)S(1)}, u32[]{:S(2)}, u32[]{:S(2)}) collective-permute-start(f32[128,256]{1,0:T(8,128)S(1)} %get-tuple-element.14), channel_id=1, source_target_pairs={{0,2},{1,3},{2,0},{3,1},{4,6},{5,7},{6,4},{7,5},{8,10},{9,11},{10,... | collective-permute-start | bytes 393224 | tf_op jit(solution)/shard_map/ppermute | solution.py:224
  25.5 1.2 %collective-permute-start.5 = (f32[128,256]{1,0:T(8,128)S(1)}, f32[128,256]{1,0:T(8,128)S(1)}, u32[]{:S(2)}, u32[]{:S(2)}) collective-permute-start(f32[128,256]{1,0:T(8,128)S(1)} %get-tuple-element.15), channel_id=1, source_target_pairs={{0,4},{1,5},{2,6},{3,7},{4,0},{5,1},{6,2},{7,3},{8,12},{9,13},{10,... | collective-permute-start | bytes 393224 | tf_op jit(solution)/shard_map/ppermute | solution.py:224
  26.7 0.3 collective-permute-start.6
  27.0 2.7 %collective-permute-done.4.refs_1_ = f32[128,256]{1,0:T(8,128)S(1)} collective-permute-done((f32[128,256]{1,0:T(8,128)S(1)}, f32[128,256]{1,0:T(8,128)S(1)}, u32[]{:S(2)}, u32[]{:S(2)}) %collective-permute-start.4) | collective-permute-done | bytes 131104 | tf_op jit(solution)/shard_map/ppermute | solution.py:224
  29.7 4.2 %collective-permute-done.5.refs_2_ = f32[128,256]{1,0:T(8,128)S(1)} collective-permute-done((f32[128,256]{1,0:T(8,128)S(1)}, f32[128,256]{1,0:T(8,128)S(1)}, u32[]{:S(2)}, u32[]{:S(2)}) %collective-permute-start.5) | collective-permute-done | bytes 131104 | tf_op jit(solution)/shard_map/ppermute | solution.py:224
  33.9 0.0 collective-permute-done.6.refs_3_
  33.9 1.4 %collective-permute-start.9 = (f32[128,256]{1,0:T(8,128)S(1)}, f32[128,256]{1,0:T(8,128)S(1)}, u32[]{:S(2)}, u32[]{:S(2)}) collective-permute-start(f32[128,256]{1,0:T(8,128)S(1)} %sum.1.refs_0_), channel_id=1, source_target_pairs={{0,6},{1,7},{2,4},{3,5},{4,2},{5,3},{6,0},{7,1},{8,14},{9,15},{10,... | collective-permute-start | bytes 393224 | tf_op jit(solution)/shard_map/ppermute | solution.py:233
  35.3 1.1 %collective-permute-start.8 = (f32[128,256]{1,0:T(8,128)S(1)}, f32[128,256]{1,0:T(8,128)S(1)}, u32[]{:S(2)}, u32[]{:S(2)}) collective-permute-start(f32[128,256]{1,0:T(8,128)S(1)} %sum.1.refs_0_), channel_id=1, source_target_pairs={{0,4},{1,5},{2,6},{3,7},{4,0},{5,1},{6,2},{7,3},{8,12},{9,13},{10,... | collective-permute-start | bytes 393224 | tf_op jit(solution)/shard_map/ppermute | solution.py:233
  36.4 1.1 %collective-permute-start.7 = (f32[128,256]{1,0:T(8,128)S(1)}, f32[128,256]{1,0:T(8,128)S(1)}, u32[]{:S(2)}, u32[]{:S(2)}) collective-permute-start(f32[128,256]{1,0:T(8,128)S(1)} %sum.1.refs_0_), channel_id=1, source_target_pairs={{0,2},{1,3},{2,0},{3,1},{4,6},{5,7},{6,4},{7,5},{8,10},{9,11},{10,... | collective-permute-start | bytes 393224 | tf_op jit(solution)/shard_map/ppermute | solution.py:233
  37.5 0.0 collective-permute-start.10
  37.5 3.7 %collective-permute-done.9.refs_3_ = f32[128,256]{1,0:T(8,128)S(1)} collective-permute-done((f32[128,256]{1,0:T(8,128)S(1)}, f32[128,256]{1,0:T(8,128)S(1)}, u32[]{:S(2)}, u32[]{:S(2)}) %collective-permute-start.9) | collective-permute-done | bytes 131104 | tf_op jit(solution)/shard_map/ppermute | solution.py:233
  41.3 1.0 %collective-permute-done.8.refs_2_ = f32[128,256]{1,0:T(8,128)S(1)} collective-permute-done((f32[128,256]{1,0:T(8,128)S(1)}, f32[128,256]{1,0:T(8,128)S(1)}, u32[]{:S(2)}, u32[]{:S(2)}) %collective-permute-start.8) | collective-permute-done | bytes 131104 | tf_op jit(solution)/shard_map/ppermute | solution.py:233
  42.3 0.1 collective-permute-done.7.refs_1_
  42.3 0.4 collective-permute-start.11
  42.8 0.0 collective-permute-done.10.refs_4_
  42.8 0.0 collective-permute-done.13.refs_7_
  42.8 0.8 %collective-permute-done.12.refs_6_ = f32[128,256]{1,0:T(8,128)S(1)} collective-permute-done((f32[128,256]{1,0:T(8,128)S(1)}, f32[128,256]{1,0:T(8,128)S(1)}, u32[]{:S(2)}, u32[]{:S(2)}) %collective-permute-start.12) | collective-permute-done | bytes 131104 | tf_op jit(solution)/shard_map/ppermute | solution.py:234
  43.6 0.2 collective-permute-done.11.refs_5_
  43.8 1.4 %scale.1 = f32[512,512]{1,0:T(8,128)} custom-call(f32[128,256]{1,0:T(8,128)S(1)} %sum.1.refs_0_, f32[128,256]{1,0:T(8,128)S(1)} %collective-permute-done.7.refs_1_, f32[128,256]{1,0:T(8,128)S(1)} %collective-permute-done.8.refs_2_, f32[128,256]{1,0:T(8,128)S(1)} %collective-permute-done.9.refs_3_, f32[128,256]{1,0:T(8,128)S(1)} %collective-permute-done.10.refs_4_, ...), custom_call_target="tpu_custom_call" | custom-call | tf_op jit(solution)/shard_map/scale/pallas_call | solution.py:235
  (9 shorter events, 0.0 us)
Async XLA Ops:
  0.0 7.1 %copy-start.2 = (s32[1,8]{1,0:T(1,128)S(1)}, s32[1,8]{1,0:T(1,128)}, u32[]{:S(2)}) copy-start(s32[1,8]{1,0:T(1,128)} %param.7) | copy-start | bytes 100
  1.4 14.6 %collective-permute-start.2 = (f32[8,512]{1,0:T(8,128)S(1)}, f32[8,512]{1,0:T(8,128)S(1)}, u32[]{:S(2)}, u32[]{:S(2)}) collective-permute-start(f32[8,512]{1,0:T(8,128)S(1)} %diag.1.stiff_ref), channel_id=1, source_target_pairs={{0,24},{8,16},{16,8},{24,0},{1,25},{9,17},{17,9},{25,1},{2,26},{10... | collective-permute-start | bytes 49160 | tf_op jit(solution)/shard_map/ppermute | solution.py:188
  6.5 9.4 %collective-permute-start.1 = (f32[8,512]{1,0:T(8,128)S(1)}, f32[8,512]{1,0:T(8,128)S(1)}, u32[]{:S(2)}, u32[]{:S(2)}) collective-permute-start(f32[8,512]{1,0:T(8,128)S(1)} %diag.1.stiff_ref), channel_id=1, source_target_pairs={{0,16},{8,24},{16,0},{24,8},{1,17},{9,25},{17,1},{25,9},{2,18},{10... | collective-permute-start | bytes 49160 | tf_op jit(solution)/shard_map/ppermute | solution.py:188
  6.5 9.5 %collective-permute-start = (f32[8,512]{1,0:T(8,128)S(1)}, f32[8,512]{1,0:T(8,128)S(1)}, u32[]{:S(2)}, u32[]{:S(2)}) collective-permute-start(f32[8,512]{1,0:T(8,128)S(1)} %diag.1.stiff_ref), channel_id=1, source_target_pairs={{0,8},{8,0},{16,24},{24,16},{1,9},{9,1},{17,25},{25,17},{2,10},{10... | collective-permute-start | bytes 49160 | tf_op jit(solution)/shard_map/ppermute | solution.py:188
  7.1 8.8 %copy-start = (s32[1,8,512]{2,1,0:T(8,128)S(1)}, s32[1,8,512]{2,1,0:T(8,128)}, u32[]{:S(2)}) copy-start(s32[1,8,512]{2,1,0:T(8,128)} %param.8) | copy-start | bytes 49156
  7.1 8.8 %copy-start.1 = (s32[3,4]{1,0:T(4,128)S(1)}, s32[3,4]{1,0:T(4,128)}, u32[]{:S(2)}) copy-start(s32[3,4]{1,0:T(4,128)} %partner_ref.1) | copy-start | bytes 148
  20.0 2.9 %collective-permute-start.3 = (f32[512,256]{1,0:T(8,128)S(1)}, f32[512,256]{1,0:T(8,128)S(1)}, u32[]{:S(2)}, u32[]{:S(2)}) collective-permute-start(f32[512,256]{1,0:T(8,128)S(1)} %get-tuple-element.12), channel_id=1, source_target_pairs={{0,1},{1,0},{2,3},{3,2},{4,5},{5,4},{6,7},{7,6},{8,9},{9,8},{10,11... | collective-permute-start | bytes 1572872 | tf_op jit(solution)/shard_map/ppermute | solution.py:202
  23.1 6.7 %collective-permute-start.4 = (f32[128,256]{1,0:T(8,128)S(1)}, f32[128,256]{1,0:T(8,128)S(1)}, u32[]{:S(2)}, u32[]{:S(2)}) collective-permute-start(f32[128,256]{1,0:T(8,128)S(1)} %get-tuple-element.14), channel_id=1, source_target_pairs={{0,2},{1,3},{2,0},{3,1},{4,6},{5,7},{6,4},{7,5},{8,10},{9,11},{10,... | collective-permute-start | bytes 393224 | tf_op jit(solution)/shard_map/ppermute | solution.py:224
  25.5 8.4 %collective-permute-start.5 = (f32[128,256]{1,0:T(8,128)S(1)}, f32[128,256]{1,0:T(8,128)S(1)}, u32[]{:S(2)}, u32[]{:S(2)}) collective-permute-start(f32[128,256]{1,0:T(8,128)S(1)} %get-tuple-element.15), channel_id=1, source_target_pairs={{0,4},{1,5},{2,6},{3,7},{4,0},{5,1},{6,2},{7,3},{8,12},{9,13},{10,... | collective-permute-start | bytes 393224 | tf_op jit(solution)/shard_map/ppermute | solution.py:224
  26.7 7.2 %collective-permute-start.6 = (f32[128,256]{1,0:T(8,128)S(1)}, f32[128,256]{1,0:T(8,128)S(1)}, u32[]{:S(2)}, u32[]{:S(2)}) collective-permute-start(f32[128,256]{1,0:T(8,128)S(1)} %get-tuple-element.16), channel_id=1, source_target_pairs={{0,6},{1,7},{2,4},{3,5},{4,2},{5,3},{6,0},{7,1},{8,14},{9,15},{10,... | collective-permute-start | bytes 393224 | tf_op jit(solution)/shard_map/ppermute | solution.py:224
  33.9 7.3 %collective-permute-start.9 = (f32[128,256]{1,0:T(8,128)S(1)}, f32[128,256]{1,0:T(8,128)S(1)}, u32[]{:S(2)}, u32[]{:S(2)}) collective-permute-start(f32[128,256]{1,0:T(8,128)S(1)} %sum.1.refs_0_), channel_id=1, source_target_pairs={{0,6},{1,7},{2,4},{3,5},{4,2},{5,3},{6,0},{7,1},{8,14},{9,15},{10,... | collective-permute-start | bytes 393224 | tf_op jit(solution)/shard_map/ppermute | solution.py:233
  35.3 7.0 %collective-permute-start.8 = (f32[128,256]{1,0:T(8,128)S(1)}, f32[128,256]{1,0:T(8,128)S(1)}, u32[]{:S(2)}, u32[]{:S(2)}) collective-permute-start(f32[128,256]{1,0:T(8,128)S(1)} %sum.1.refs_0_), channel_id=1, source_target_pairs={{0,4},{1,5},{2,6},{3,7},{4,0},{5,1},{6,2},{7,3},{8,12},{9,13},{10,... | collective-permute-start | bytes 393224 | tf_op jit(solution)/shard_map/ppermute | solution.py:233
  36.4 6.0 %collective-permute-start.7 = (f32[128,256]{1,0:T(8,128)S(1)}, f32[128,256]{1,0:T(8,128)S(1)}, u32[]{:S(2)}, u32[]{:S(2)}) collective-permute-start(f32[128,256]{1,0:T(8,128)S(1)} %sum.1.refs_0_), channel_id=1, source_target_pairs={{0,2},{1,3},{2,0},{3,1},{4,6},{5,7},{6,4},{7,5},{8,10},{9,11},{10,... | collective-permute-start | bytes 393224 | tf_op jit(solution)/shard_map/ppermute | solution.py:233
  37.5 5.3 %collective-permute-start.10 = (f32[128,256]{1,0:T(8,128)S(1)}, f32[128,256]{1,0:T(8,128)S(1)}, u32[]{:S(2)}, u32[]{:S(2)}) collective-permute-start(f32[128,256]{1,0:T(8,128)S(1)} %sum.1.refs_0_), channel_id=1, source_target_pairs={{0,1},{1,0},{2,3},{3,2},{4,5},{5,4},{6,7},{7,6},{8,9},{9,8},{10,11... | collective-permute-start | bytes 393224 | tf_op jit(solution)/shard_map/ppermute | solution.py:234
  41.2 1.5 %collective-permute-start.13 = (f32[128,256]{1,0:T(8,128)S(1)}, f32[128,256]{1,0:T(8,128)S(1)}, u32[]{:S(2)}, u32[]{:S(2)}) collective-permute-start(f32[128,256]{1,0:T(8,128)S(1)} %collective-permute-done.9.refs_3_), channel_id=1, source_target_pairs={{0,1},{1,0},{2,3},{3,2},{4,5},{5,4},{6,7},{7,6},{8,9},{9,8},{10,11... | collective-permute-start | bytes 393224 | tf_op jit(solution)/shard_map/ppermute | solution.py:234
  42.3 1.3 %collective-permute-start.12 = (f32[128,256]{1,0:T(8,128)S(1)}, f32[128,256]{1,0:T(8,128)S(1)}, u32[]{:S(2)}, u32[]{:S(2)}) collective-permute-start(f32[128,256]{1,0:T(8,128)S(1)} %collective-permute-done.8.refs_2_), channel_id=1, source_target_pairs={{0,1},{1,0},{2,3},{3,2},{4,5},{5,4},{6,7},{7,6},{8,9},{9,8},{10,11... | collective-permute-start | bytes 393224 | tf_op jit(solution)/shard_map/ppermute | solution.py:234
  42.3 1.5 %collective-permute-start.11 = (f32[128,256]{1,0:T(8,128)S(1)}, f32[128,256]{1,0:T(8,128)S(1)}, u32[]{:S(2)}, u32[]{:S(2)}) collective-permute-start(f32[128,256]{1,0:T(8,128)S(1)} %collective-permute-done.7.refs_1_), channel_id=1, source_target_pairs={{0,1},{1,0},{2,3},{3,2},{4,5},{5,4},{6,7},{7,6},{8,9},{9,8},{10,11... | collective-permute-start | bytes 393224 | tf_op jit(solution)/shard_map/ppermute | solution.py:234

commit v3 on v2

--- a/solution.py
+++ b/solution.py
@@ -13,6 +13,7 @@
 R = 512
 NI = 1024
 RB = 4
+HEAD = 1
 VMEM_LIMIT = 24 << 20
 
 F32 = jnp.float32
@@ -36,66 +37,114 @@
 ASPEC = pl.BlockSpec(memory_space=pl.ANY)
 
 
-def diag_kernel(block_ref, stiff_ref, held, sems):
+def diag_kernel(block_ref, coupling_ref, stiff_ref, head_ref, held, sems, head_sems):
     def copy(b):
         part = pl.ds(b * BLK, BLK)
         return pltpu.make_async_copy(block_ref.at[:, part, part], held.at[b], sems.at[b])
 
+    def head(j):
+        return pltpu.make_async_copy(coupling_ref.at[j], head_ref.at[j], head_sems.at[j])
+
     for b in range(RB):
         copy(b).start()
+    for j in range(HEAD):
+        head(j).start()
     shape = (BLK, BLK)
     on = lax.broadcasted_iota(jnp.int32, shape, 0) == lax.broadcasted_iota(jnp.int32, shape, 1)
     for b in range(RB):
         copy(b).wait()
         tile = held[b].astype(F32)
         stiff_ref[:, b * BLK : (b + 1) * BLK] = jnp.sum(jnp.where(on[None], tile, 0.0), axis=1)
-
-
-def diagonal(local_block):
+    for j in range(HEAD):
+        head(j).wait()
+
+
+def diagonal(local_block, coupling):
     subs = local_block.shape[0]
     return pl.pallas_call(
         diag_kernel,
-        out_shape=pltpu.VMEM((subs, R), F32),
-        in_specs=[ASPEC],
-        out_specs=VSPEC,
-        scratch_shapes=[pltpu.VMEM((RB, subs, BLK, BLK), BF16), pltpu.SemaphoreType.DMA((RB,))],
+        out_shape=(pltpu.VMEM((subs, R), F32), pltpu.VMEM((HEAD, NI, R), BF16)),
+        in_specs=[ASPEC, ASPEC],
+        out_specs=(VSPEC, VSPEC),
+        scratch_shapes=[
+            pltpu.VMEM((RB, subs, BLK, BLK), BF16),
+            pltpu.SemaphoreType.DMA((RB,)),
+            pltpu.SemaphoreType.DMA((HEAD,)),
+        ],
         compiler_params=params(),
         name="diag",
-    )(*in_hbm(local_block))
-
-
-def schur_kernel(counts_ref, coupling_ref, block_ref, schur_ref):
-    j = pl.program_id(0)
-    for live in range(1, RB + 1):
-
-        @pl.when(counts_ref[j] == live)
-        def _():
-            n = live * BLK
-            c = coupling_ref[0, :, :n]
-            gram = lax.dot_general(c, c, (((0,), (0,)), ((), ())), preferred_element_type=F32)
-            schur_ref[0, :n, :n] = (block_ref[0, :n, :n].astype(F32) - gram).astype(BF16)
-            if n < R:
-                schur_ref[0, :n, n:] = jnp.zeros((n, R - n), BF16)
-                schur_ref[0, n:, :] = jnp.zeros((R - n, R), BF16)
-
-
-def schur_blocks(counts, coupling, local_block):
+    )(*in_hbm(local_block, coupling))
+
+
+def schur_block(n, c, block, schur):
+    at = 0
+    while at < n:
+        stop = min(n, at + 2 * BLK)
+        here, rest = slice(at, stop), slice(stop, n)
+        gram = lax.dot_general(
+            c[:, here], c[:, here], (((0,), (0,)), ((), ())), preferred_element_type=F32
+        )
+        schur[here, here] = (block[here, here].astype(F32) - gram).astype(BF16)
+        if stop < n:
+            gram = lax.dot_general(
+                c[:, here], c[:, rest], (((0,), (0,)), ((), ())), preferred_element_type=F32
+            )
+            schur[here, rest] = (block[here, rest].astype(F32) - gram).astype(BF16)
+            schur[rest, here] = (block[rest, here].astype(F32) - gram.T).astype(BF16)
+        at = stop
+    if n < R:
+        schur[:n, n:] = jnp.zeros((n, R - n), BF16)
+        schur[n:, :] = jnp.zeros((R - n, R), BF16)
+
+
+def schur_kernel(counts_ref, coupling_ref, head_ref, block_ref, schur_ref, held, sems):
+    subs = block_ref.shape[0]
+
+    def copy(j, n):
+        part = pl.ds(0, n)
+        return pltpu.make_async_copy(
+            coupling_ref.at[j, :, part], held.at[j - HEAD, :, part], sems.at[j - HEAD]
+        )
+
+    def by_count(j, body):
+        for live in range(1, RB + 1):
+            pl.when(counts_ref[j] == live)(functools.partial(body, live * BLK))
+
+    def send(j, _):
+        by_count(j, lambda n: copy(j, n).start())
+        return 0
+
+    def from_head(j, _):
+        by_count(j, lambda n: schur_block(n, head_ref.at[j], block_ref.at[j], schur_ref.at[j]))
+        return 0
+
+    def from_held(j, _):
+        def body(n):
+            copy(j, n).wait()
+            schur_block(n, held.at[j - HEAD], block_ref.at[j], schur_ref.at[j])
+
+        by_count(j, body)
+        return 0
+
+    lax.fori_loop(HEAD, subs, send, 0)
+    lax.fori_loop(0, HEAD, from_head, 0)
+    lax.fori_loop(HEAD, subs, from_held, 0)
+
+
+def schur_blocks(counts, coupling, head, local_block):
     subs = local_block.shape[0]
     return pl.pallas_call(
         schur_kernel,
-        grid_spec=pltpu.PrefetchScalarGridSpec(
-            num_scalar_prefetch=1,
-            grid=(subs,),
-            in_specs=[
-                pl.BlockSpec((1, NI, R), lambda j, c: (j, 0, 0)),
-                pl.BlockSpec((1, R, R), lambda j, c: (j, 0, 0)),
-            ],
-            out_specs=pl.BlockSpec((1, R, R), lambda j, c: (j, 0, 0)),
-        ),
         out_shape=pltpu.VMEM((subs, R, R), BF16),
+        in_specs=[SSPEC, ASPEC, VSPEC, VSPEC],
+        out_specs=VSPEC,
+        scratch_shapes=[
+            pltpu.VMEM((subs - HEAD, NI, R), BF16),
+            pltpu.SemaphoreType.DMA((subs - HEAD,)),
+        ],
         compiler_params=params(),
         name="schur",
-    )(counts, *in_hbm(coupling, local_block))
+    )(counts, *in_hbm(coupling), *in_vmem(head, local_block))
 
 
 def place():
@@ -113,31 +162,28 @@
         for r in range(ROUNDS):
             times += (partner_ref[r, column] == (column ^ (d + 1))).astype(jnp.int32)
         total = total + times.astype(F32) * other[...]
-    weight = stiff_ref[...] / total
-    subs = schur_ref.shape[0]
-    rows = lax.broadcasted_iota(jnp.int32, (NC, R), 0)
-    for j in range(subs):
-        hit = rows == primal_ref[j : j + 1, :]
-        basis_ref[j] = jnp.where(hit, weight[j : j + 1, :], 0.0).astype(BF16)
-        add_tile(half, j, off, schur_ref, basis_ref, tile_ref)
+    weight = (stiff_ref[...] / total).astype(BF16)
+    rows = lax.broadcasted_iota(jnp.int32, (NC, R), 0).astype(jnp.int16)
+    primal = primal_ref[...].astype(jnp.int16)
+    for j in range(schur_ref.shape[0]):
+        hit = rows == primal[j : j + 1, :]
+        basis_ref[:, j * R : (j + 1) * R] = jnp.where(hit, weight[j : j + 1, :], jnp.zeros((), BF16))
+    add_tiles(half, off, schur_ref, basis_ref, tile_ref)
 
 
 def second_kernel(half, schur_ref, basis_ref, tile_ref):
     off = place()[1] * half
+    add_tiles(half, off, schur_ref, basis_ref, tile_ref)
+
+
+def add_tiles(half, off, schur_ref, basis_ref, tile_ref):
+    images = []
     for j in range(schur_ref.shape[0]):
-        add_tile(half, j, off, schur_ref, basis_ref, tile_ref)
-
-
-def add_tile(half, j, off, schur_ref, basis_ref, tile_ref):
-    part = basis_ref[j, pl.ds(pl.multiple_of(off, half), half), :]
-    image = lax.dot_general(
-        schur_ref[j], part, (((1,), (1,)), ((), ())), preferred_element_type=F32
-    ).astype(BF16)
-    term = jnp.dot(basis_ref[j], image, preferred_element_type=F32)
-    if j == 0:
-        tile_ref[...] = term
-    else:
-        tile_ref[...] += term
+        part = basis_ref[pl.ds(pl.multiple_of(off, half), half), j * R : (j + 1) * R]
+        images.append(lax.dot_general(
+            schur_ref[j], part, (((1,), (1,)), ((), ())), preferred_element_type=F32
+        ).astype(BF16))
+    tile_ref[...] = jnp.dot(basis_ref[...], jnp.concatenate(images, axis=0), preferred_element_type=F32)
 
 
 def split_kernel(rows, own_ref, other_ref, *outs):
@@ -183,16 +229,16 @@
     chips, half, rows = line // 2, NC // 2, NC // (line // 2)
     coupling, local_block, counts, primal = coupling[0], local_block[0], counts[0], primal[0]
     subs = coupling.shape[0]
-    stiff = diagonal(local_block)
+    stiff, head = diagonal(local_block, coupling)
     others = [
         lax.ppermute(stiff, "gx", [(i, i ^ d) for i in range(columns)]) for d in range(1, columns)
     ]
 
-    schur = schur_blocks(counts, coupling, local_block)
+    schur = schur_blocks(counts, coupling, head, local_block)
 
     first, basis = pl.pallas_call(
         functools.partial(first_kernel, half),
-        out_shape=(pltpu.VMEM((NC, half), F32), pltpu.VMEM((subs, NC, R), BF16)),
+        out_shape=(pltpu.VMEM((NC, half), F32), pltpu.VMEM((NC, subs * R), BF16)),
         in_specs=[SSPEC] + [VSPEC] * (columns + 2),
         out_specs=(VSPEC, VSPEC),
         compiler_params=params(),

time: 45.5 us -> 41.4 us (0.910); the launches traced: 45.2 us -> 41.6 us
  Pallas kernels: 18.5 us -> 16 us
  starting transfers between devices: 13.8 us -> 12.9 us
    pallas_call x2, Pallas kernels: 10.1 us -> 7.9 us  [the longest x1 6.13 us: schur_blocks(): pl.pallas_call(schur_kernel, out_shape=pltpu.VMEM((subs, R, R), BF16), in...]
    ppermute x3, waiting for transfers between devices: 6.88 us -> 5.86 us  [per_device(): arrived = [lax.ppermute(pieces[d], 'gy', hop(d)) for d in range(1, chips)]]
    ppermute x3, waiting for transfers between devices: 4.83 us -> 5.37 us  [per_device(): own = [mine] + [lax.ppermute(mine, 'gy', hop(d)) for d in range(1, chips)]]
  transfers between devices with their start and end apart: 14 -> 14, of which waited for: 7 -> 7; matrix products, arithmetic and copies ran while one was open for 0% -> 0% of each run, Pallas kernels for 26% -> 21%
where the time goes in v3:
time: 41.4 us; the launch traced here: 41.6 us
  Pallas kernels  16 us (39%)
  starting transfers between devices  12.9 us (31%)
  waiting for transfers between devices  12.6 us (30%)
    pallas_call x1, Pallas kernels, schur_blocks(): pl.pallas_call(schur_kernel, out_shape=pltpu.VMEM((subs, R, R), BF16), in...  6.13 us
    ppermute x3, waiting for transfers between devices, per_device(): arrived = [lax.ppermute(pieces[d], 'gy', hop(d)) for d in range(1, chips)]  5.86 us
    ppermute x3, starting transfers between devices, per_device(): lax.ppermute(stiff, 'gx', [(i, i ^ d) for i in range(columns)])  5.76 us
    ppermute x3, waiting for transfers between devices, per_device(): own = [mine] + [lax.ppermute(mine, 'gy', hop(d)) for d in range(1, chips)]  5.37 us
    pallas_call x1, Pallas kernels, per_device(): pl.pallas_call(functools.partial(first_kernel, half), out_shape=(pltpu.VM...  3.87 us
    ppermute x3, starting transfers between devices, per_device(): own = [mine] + [lax.ppermute(mine, 'gy', hop(d)) for d in range(1, chips)]  3.55 us
    ppermute x3, starting transfers between devices, per_device(): arrived = [lax.ppermute(pieces[d], 'gy', hop(d)) for d in range(1, chips)]  3.55 us
    pallas_call x1, Pallas kernels, per_device(): pl.pallas_call(functools.partial(second_kernel, half), out_shape=pltpu.VM...  2.72 us
  transfers between devices with their start and end apart: 14, of which 7 were waited for; matrix products, arithmetic and copies ran while one was open for 0% of the time, Pallas kernels for 21%

profile of v3, /device:TPU:0, one launch (start us, length us, event | category | flops | bytes accessed | tf_op | source)
XLA Modules:
  0.0 41.6 jit_solution(8475855898197585270)
XLA Ops:
  0.0 1.8 %diag.1 = (f32[8,512]{1,0:T(8,128)S(1)}, bf16[1,1024,512]{2,1,0:T(8,128)(2,1)S(1)}) custom-call(bf16[8,512,512]{2,1,0:T(8,128)(2,1)} %bitcast.5, bf16[8,1024,512]{2,1,0:T(8,128)(2,1)} %bitcast.9), custom_call_target="tpu_custom_call" | custom-call | tf_op jit(solution)/shard_map/diag/pallas_call | solution.py:64
  1.8 5.1 %collective-permute-start.2 = (f32[8,512]{1,0:T(8,128)S(1)}, f32[8,512]{1,0:T(8,128)S(1)}, u32[]{:S(2)}, u32[]{:S(2)}) collective-permute-start(f32[8,512]{1,0:T(8,128)S(1)} %get-tuple-element.14.stiff_ref), channel_id=1, source_target_pairs={{0,24},{8,16},{16,8},{24,0},{1,25},{9,17},{17,9},{25,1},{2,26},{10... | collective-permute-start | bytes 49160 | tf_op jit(solution)/shard_map/ppermute | solution.py:234
  6.9 0.0 collective-permute-start.1
  6.9 0.6 %collective-permute-start = (f32[8,512]{1,0:T(8,128)S(1)}, f32[8,512]{1,0:T(8,128)S(1)}, u32[]{:S(2)}, u32[]{:S(2)}) collective-permute-start(f32[8,512]{1,0:T(8,128)S(1)} %get-tuple-element.14.stiff_ref), channel_id=1, source_target_pairs={{0,8},{8,0},{16,24},{24,16},{1,9},{9,1},{17,25},{25,17},{2,10},{10... | collective-permute-start | bytes 49160 | tf_op jit(solution)/shard_map/ppermute | solution.py:234
  7.6 6.1 %schur.1.refs_3_.schur_ref = bf16[8,512,512]{2,1,0:T(8,128)(2,1)S(1)} custom-call(s32[8]{0:T(128)S(1)} %bitcast.8, bf16[8,1024,512]{2,1,0:T(8,128)(2,1)} %bitcast.10, bf16[1,1024,512]{2,1,0:T(8,128)(2,1)S(1)} %get-tuple-element.13.head_ref, bf16[8,512,512]{2,1,0:T(8,128)(2,1)S(1)} %bitcast.6), custom_call_target="tpu_custom_call" | custom-call | tf_op jit(solution)/shard_map/schur/pallas_call | solution.py:136
  13.7 0.0 collective-permute-done.2.refs_2_
  13.7 0.0 collective-permute-done.1.refs_1_
  13.7 0.0 collective-permute-done.refs_0_
  13.7 3.9 %first_half.1 = (f32[512,256]{1,0:T(8,128)S(1)}, bf16[512,4096]{1,0:T(8,128)(2,1)S(1)}) custom-call(s32[3,4]{1,0:T(4,128)S(1)} %copy-done.2, s32[8,512]{1,0:T(8,128)S(1)} %bitcast.7, f32[8,512]{1,0:T(8,128)S(1)} %get-tuple-element.14.stiff_ref, f32[8,512]{1,0:T(8,128)S(1)} %collective-permute-done.refs_0_, f32[8,512]{1,0:T(8,128)S(1)} %collective-permute-done.1.refs_1_, ...), custom_call_target="tpu_custom_call" | custom-call | tf_op jit(solution)/shard_map/first_half/pallas_call | solution.py:239
  17.6 0.1 collective-permute-start.3
  17.7 2.7 %second_half.1.own_ref = f32[512,256]{1,0:T(8,128)S(1)} custom-call(bf16[8,512,512]{2,1,0:T(8,128)(2,1)S(1)} %schur.1.refs_3_.schur_ref, bf16[512,4096]{1,0:T(8,128)(2,1)S(1)} %get-tuple-element.15.basis_ref), custom_call_target="tpu_custom_call" | custom-call | tf_op jit(solution)/shard_map/second_half/pallas_call | solution.py:249
  20.4 0.0 collective-permute-done.3.other_ref
  20.4 0.1 split.1
  20.5 0.7 %collective-permute-start.4 = (f32[128,256]{1,0:T(8,128)S(1)}, f32[128,256]{1,0:T(8,128)S(1)}, u32[]{:S(2)}, u32[]{:S(2)}) collective-permute-start(f32[128,256]{1,0:T(8,128)S(1)} %get-tuple-element.18), channel_id=1, source_target_pairs={{0,2},{1,3},{2,0},{3,1},{4,6},{5,7},{6,4},{7,5},{8,10},{9,11},{10,... | collective-permute-start | bytes 393224 | tf_op jit(solution)/shard_map/ppermute | solution.py:270
  21.2 2.1 %collective-permute-start.5 = (f32[128,256]{1,0:T(8,128)S(1)}, f32[128,256]{1,0:T(8,128)S(1)}, u32[]{:S(2)}, u32[]{:S(2)}) collective-permute-start(f32[128,256]{1,0:T(8,128)S(1)} %get-tuple-element.19), channel_id=1, source_target_pairs={{0,4},{1,5},{2,6},{3,7},{4,0},{5,1},{6,2},{7,3},{8,12},{9,13},{10,... | collective-permute-start | bytes 393224 | tf_op jit(solution)/shard_map/ppermute | solution.py:270
  23.2 0.8 %collective-permute-start.6 = (f32[128,256]{1,0:T(8,128)S(1)}, f32[128,256]{1,0:T(8,128)S(1)}, u32[]{:S(2)}, u32[]{:S(2)}) collective-permute-start(f32[128,256]{1,0:T(8,128)S(1)} %get-tuple-element.20), channel_id=1, source_target_pairs={{0,6},{1,7},{2,4},{3,5},{4,2},{5,3},{6,0},{7,1},{8,14},{9,15},{10,... | collective-permute-start | bytes 393224 | tf_op jit(solution)/shard_map/ppermute | solution.py:270
  24.1 2.8 %collective-permute-done.4.refs_1_ = f32[128,256]{1,0:T(8,128)S(1)} collective-permute-done((f32[128,256]{1,0:T(8,128)S(1)}, f32[128,256]{1,0:T(8,128)S(1)}, u32[]{:S(2)}, u32[]{:S(2)}) %collective-permute-start.4) | collective-permute-done | bytes 131104 | tf_op jit(solution)/shard_map/ppermute | solution.py:270
  26.9 3.0 %collective-permute-done.5.refs_2_ = f32[128,256]{1,0:T(8,128)S(1)} collective-permute-done((f32[128,256]{1,0:T(8,128)S(1)}, f32[128,256]{1,0:T(8,128)S(1)}, u32[]{:S(2)}, u32[]{:S(2)}) %collective-permute-start.5) | collective-permute-done | bytes 131104 | tf_op jit(solution)/shard_map/ppermute | solution.py:270
  29.9 0.0 collective-permute-done.6.refs_3_
  30.0 1.6 %collective-permute-start.9 = (f32[128,256]{1,0:T(8,128)S(1)}, f32[128,256]{1,0:T(8,128)S(1)}, u32[]{:S(2)}, u32[]{:S(2)}) collective-permute-start(f32[128,256]{1,0:T(8,128)S(1)} %sum.1.refs_0_), channel_id=1, source_target_pairs={{0,6},{1,7},{2,4},{3,5},{4,2},{5,3},{6,0},{7,1},{8,14},{9,15},{10,... | collective-permute-start | bytes 393224 | tf_op jit(solution)/shard_map/ppermute | solution.py:279
  31.6 1.4 %collective-permute-start.8 = (f32[128,256]{1,0:T(8,128)S(1)}, f32[128,256]{1,0:T(8,128)S(1)}, u32[]{:S(2)}, u32[]{:S(2)}) collective-permute-start(f32[128,256]{1,0:T(8,128)S(1)} %sum.1.refs_0_), channel_id=1, source_target_pairs={{0,4},{1,5},{2,6},{3,7},{4,0},{5,1},{6,2},{7,3},{8,12},{9,13},{10,... | collective-permute-start | bytes 393224 | tf_op jit(solution)/shard_map/ppermute | solution.py:279
  32.9 0.6 %collective-permute-start.7 = (f32[128,256]{1,0:T(8,128)S(1)}, f32[128,256]{1,0:T(8,128)S(1)}, u32[]{:S(2)}, u32[]{:S(2)}) collective-permute-start(f32[128,256]{1,0:T(8,128)S(1)} %sum.1.refs_0_), channel_id=1, source_target_pairs={{0,2},{1,3},{2,0},{3,1},{4,6},{5,7},{6,4},{7,5},{8,10},{9,11},{10,... | collective-permute-start | bytes 393224 | tf_op jit(solution)/shard_map/ppermute | solution.py:279
  33.5 0.0 collective-permute-start.10
  33.5 3.8 %collective-permute-done.9.refs_3_ = f32[128,256]{1,0:T(8,128)S(1)} collective-permute-done((f32[128,256]{1,0:T(8,128)S(1)}, f32[128,256]{1,0:T(8,128)S(1)}, u32[]{:S(2)}, u32[]{:S(2)}) %collective-permute-start.9) | collective-permute-done | bytes 131104 | tf_op jit(solution)/shard_map/ppermute | solution.py:279
  37.3 0.0 collective-permute-start.13
  37.3 0.8 %collective-permute-done.8.refs_2_ = f32[128,256]{1,0:T(8,128)S(1)} collective-permute-done((f32[128,256]{1,0:T(8,128)S(1)}, f32[128,256]{1,0:T(8,128)S(1)}, u32[]{:S(2)}, u32[]{:S(2)}) %collective-permute-start.8) | collective-permute-done | bytes 131104 | tf_op jit(solution)/shard_map/ppermute | solution.py:279
  38.1 0.8 %collective-permute-done.7.refs_1_ = f32[128,256]{1,0:T(8,128)S(1)} collective-permute-done((f32[128,256]{1,0:T(8,128)S(1)}, f32[128,256]{1,0:T(8,128)S(1)}, u32[]{:S(2)}, u32[]{:S(2)}) %collective-permute-start.7) | collective-permute-done | bytes 131104 | tf_op jit(solution)/shard_map/ppermute | solution.py:279
  38.9 0.0 collective-permute-done.10.refs_4_
  38.9 0.0 collective-permute-done.13.refs_7_
  38.9 0.6 %collective-permute-done.12.refs_6_ = f32[128,256]{1,0:T(8,128)S(1)} collective-permute-done((f32[128,256]{1,0:T(8,128)S(1)}, f32[128,256]{1,0:T(8,128)S(1)}, u32[]{:S(2)}, u32[]{:S(2)}) %collective-permute-start.12) | collective-permute-done | bytes 131104 | tf_op jit(solution)/shard_map/ppermute | solution.py:280
  39.5 0.8 %collective-permute-done.11.refs_5_ = f32[128,256]{1,0:T(8,128)S(1)} collective-permute-done((f32[128,256]{1,0:T(8,128)S(1)}, f32[128,256]{1,0:T(8,128)S(1)}, u32[]{:S(2)}, u32[]{:S(2)}) %collective-permute-start.11) | collective-permute-done | bytes 131104 | tf_op jit(solution)/shard_map/ppermute | solution.py:280
  40.2 1.4 %scale.1 = f32[512,512]{1,0:T(8,128)} custom-call(f32[128,256]{1,0:T(8,128)S(1)} %sum.1.refs_0_, f32[128,256]{1,0:T(8,128)S(1)} %collective-permute-done.7.refs_1_, f32[128,256]{1,0:T(8,128)S(1)} %collective-permute-done.8.refs_2_, f32[128,256]{1,0:T(8,128)S(1)} %collective-permute-done.9.refs_3_, f32[128,256]{1,0:T(8,128)S(1)} %collective-permute-done.10.refs_4_, ...), custom_call_target="tpu_custom_call" | custom-call | tf_op jit(solution)/shard_map/scale/pallas_call | solution.py:281
  (11 shorter events, 0.0 us)
Async XLA Ops:
  0.0 7.5 %copy-start = (bf16[1,8,512,512]{3,2,1,0:T(8,128)(2,1)S(1)}, bf16[1,8,512,512]{3,2,1,0:T(8,128)(2,1)}, u32[]{:S(2)}) copy-start(bf16[1,8,512,512]{3,2,1,0:T(8,128)(2,1)} %param.6) | copy-start | bytes 12582916
  0.0 7.5 %copy-start.3 = (s32[1,8]{1,0:T(1,128)S(1)}, s32[1,8]{1,0:T(1,128)}, u32[]{:S(2)}) copy-start(s32[1,8]{1,0:T(1,128)} %param.7) | copy-start | bytes 100
  1.8 11.9 %collective-permute-start.2 = (f32[8,512]{1,0:T(8,128)S(1)}, f32[8,512]{1,0:T(8,128)S(1)}, u32[]{:S(2)}, u32[]{:S(2)}) collective-permute-start(f32[8,512]{1,0:T(8,128)S(1)} %get-tuple-element.14.stiff_ref), channel_id=1, source_target_pairs={{0,24},{8,16},{16,8},{24,0},{1,25},{9,17},{17,9},{25,1},{2,26},{10... | collective-permute-start | bytes 49160 | tf_op jit(solution)/shard_map/ppermute | solution.py:234
  6.9 6.8 %collective-permute-start.1 = (f32[8,512]{1,0:T(8,128)S(1)}, f32[8,512]{1,0:T(8,128)S(1)}, u32[]{:S(2)}, u32[]{:S(2)}) collective-permute-start(f32[8,512]{1,0:T(8,128)S(1)} %get-tuple-element.14.stiff_ref), channel_id=1, source_target_pairs={{0,16},{8,24},{16,0},{24,8},{1,17},{9,25},{17,1},{25,9},{2,18},{10... | collective-permute-start | bytes 49160 | tf_op jit(solution)/shard_map/ppermute | solution.py:234
  6.9 6.8 %collective-permute-start = (f32[8,512]{1,0:T(8,128)S(1)}, f32[8,512]{1,0:T(8,128)S(1)}, u32[]{:S(2)}, u32[]{:S(2)}) collective-permute-start(f32[8,512]{1,0:T(8,128)S(1)} %get-tuple-element.14.stiff_ref), channel_id=1, source_target_pairs={{0,8},{8,0},{16,24},{24,16},{1,9},{9,1},{17,25},{25,17},{2,10},{10... | collective-permute-start | bytes 49160 | tf_op jit(solution)/shard_map/ppermute | solution.py:234
  7.5 6.2 %copy-start.1 = (s32[1,8,512]{2,1,0:T(8,128)S(1)}, s32[1,8,512]{2,1,0:T(8,128)}, u32[]{:S(2)}) copy-start(s32[1,8,512]{2,1,0:T(8,128)} %param.8) | copy-start | bytes 49156
  7.5 6.2 %copy-start.2 = (s32[3,4]{1,0:T(4,128)S(1)}, s32[3,4]{1,0:T(4,128)}, u32[]{:S(2)}) copy-start(s32[3,4]{1,0:T(4,128)} %partner_ref.1) | copy-start | bytes 148
  17.6 2.8 %collective-permute-start.3 = (f32[512,256]{1,0:T(8,128)S(1)}, f32[512,256]{1,0:T(8,128)S(1)}, u32[]{:S(2)}, u32[]{:S(2)}) collective-permute-start(f32[512,256]{1,0:T(8,128)S(1)} %get-tuple-element.16), channel_id=1, source_target_pairs={{0,1},{1,0},{2,3},{3,2},{4,5},{5,4},{6,7},{7,6},{8,9},{9,8},{10,11... | collective-permute-start | bytes 1572872 | tf_op jit(solution)/shard_map/ppermute | solution.py:248
  20.5 6.4 %collective-permute-start.4 = (f32[128,256]{1,0:T(8,128)S(1)}, f32[128,256]{1,0:T(8,128)S(1)}, u32[]{:S(2)}, u32[]{:S(2)}) collective-permute-start(f32[128,256]{1,0:T(8,128)S(1)} %get-tuple-element.18), channel_id=1, source_target_pairs={{0,2},{1,3},{2,0},{3,1},{4,6},{5,7},{6,4},{7,5},{8,10},{9,11},{10,... | collective-permute-start | bytes 393224 | tf_op jit(solution)/shard_map/ppermute | solution.py:270
  21.2 8.7 %collective-permute-start.5 = (f32[128,256]{1,0:T(8,128)S(1)}, f32[128,256]{1,0:T(8,128)S(1)}, u32[]{:S(2)}, u32[]{:S(2)}) collective-permute-start(f32[128,256]{1,0:T(8,128)S(1)} %get-tuple-element.19), channel_id=1, source_target_pairs={{0,4},{1,5},{2,6},{3,7},{4,0},{5,1},{6,2},{7,3},{8,12},{9,13},{10,... | collective-permute-start | bytes 393224 | tf_op jit(solution)/shard_map/ppermute | solution.py:270
  23.2 6.7 %collective-permute-start.6 = (f32[128,256]{1,0:T(8,128)S(1)}, f32[128,256]{1,0:T(8,128)S(1)}, u32[]{:S(2)}, u32[]{:S(2)}) collective-permute-start(f32[128,256]{1,0:T(8,128)S(1)} %get-tuple-element.20), channel_id=1, source_target_pairs={{0,6},{1,7},{2,4},{3,5},{4,2},{5,3},{6,0},{7,1},{8,14},{9,15},{10,... | collective-permute-start | bytes 393224 | tf_op jit(solution)/shard_map/ppermute | solution.py:270
  30.0 7.4 %collective-permute-start.9 = (f32[128,256]{1,0:T(8,128)S(1)}, f32[128,256]{1,0:T(8,128)S(1)}, u32[]{:S(2)}, u32[]{:S(2)}) collective-permute-start(f32[128,256]{1,0:T(8,128)S(1)} %sum.1.refs_0_), channel_id=1, source_target_pairs={{0,6},{1,7},{2,4},{3,5},{4,2},{5,3},{6,0},{7,1},{8,14},{9,15},{10,... | collective-permute-start | bytes 393224 | tf_op jit(solution)/shard_map/ppermute | solution.py:279
  31.6 6.6 %collective-permute-start.8 = (f32[128,256]{1,0:T(8,128)S(1)}, f32[128,256]{1,0:T(8,128)S(1)}, u32[]{:S(2)}, u32[]{:S(2)}) collective-permute-start(f32[128,256]{1,0:T(8,128)S(1)} %sum.1.refs_0_), channel_id=1, source_target_pairs={{0,4},{1,5},{2,6},{3,7},{4,0},{5,1},{6,2},{7,3},{8,12},{9,13},{10,... | collective-permute-start | bytes 393224 | tf_op jit(solution)/shard_map/ppermute | solution.py:279
  32.9 6.0 %collective-permute-start.7 = (f32[128,256]{1,0:T(8,128)S(1)}, f32[128,256]{1,0:T(8,128)S(1)}, u32[]{:S(2)}, u32[]{:S(2)}) collective-permute-start(f32[128,256]{1,0:T(8,128)S(1)} %sum.1.refs_0_), channel_id=1, source_target_pairs={{0,2},{1,3},{2,0},{3,1},{4,6},{5,7},{6,4},{7,5},{8,10},{9,11},{10,... | collective-permute-start | bytes 393224 | tf_op jit(solution)/shard_map/ppermute | solution.py:279
  33.5 5.4 %collective-permute-start.10 = (f32[128,256]{1,0:T(8,128)S(1)}, f32[128,256]{1,0:T(8,128)S(1)}, u32[]{:S(2)}, u32[]{:S(2)}) collective-permute-start(f32[128,256]{1,0:T(8,128)S(1)} %sum.1.refs_0_), channel_id=1, source_target_pairs={{0,1},{1,0},{2,3},{3,2},{4,5},{5,4},{6,7},{7,6},{8,9},{9,8},{10,11... | collective-permute-start | bytes 393224 | tf_op jit(solution)/shard_map/ppermute | solution.py:280
  37.3 1.6 %collective-permute-start.13 = (f32[128,256]{1,0:T(8,128)S(1)}, f32[128,256]{1,0:T(8,128)S(1)}, u32[]{:S(2)}, u32[]{:S(2)}) collective-permute-start(f32[128,256]{1,0:T(8,128)S(1)} %collective-permute-done.9.refs_3_), channel_id=1, source_target_pairs={{0,1},{1,0},{2,3},{3,2},{4,5},{5,4},{6,7},{7,6},{8,9},{9,8},{10,11... | collective-permute-start | bytes 393224 | tf_op jit(solution)/shard_map/ppermute | solution.py:280
  38.1 1.3 %collective-permute-start.12 = (f32[128,256]{1,0:T(8,128)S(1)}, f32[128,256]{1,0:T(8,128)S(1)}, u32[]{:S(2)}, u32[]{:S(2)}) collective-permute-start(f32[128,256]{1,0:T(8,128)S(1)} %collective-permute-done.8.refs_2_), channel_id=1, source_target_pairs={{0,1},{1,0},{2,3},{3,2},{4,5},{5,4},{6,7},{7,6},{8,9},{9,8},{10,11... | collective-permute-start | bytes 393224 | tf_op jit(solution)/shard_map/ppermute | solution.py:280
  38.9 1.3 %collective-permute-start.11 = (f32[128,256]{1,0:T(8,128)S(1)}, f32[128,256]{1,0:T(8,128)S(1)}, u32[]{:S(2)}, u32[]{:S(2)}) collective-permute-start(f32[128,256]{1,0:T(8,128)S(1)} %collective-permute-done.7.refs_1_), channel_id=1, source_target_pairs={{0,1},{1,0},{2,3},{3,2},{4,5},{5,4},{6,7},{7,6},{8,9},{9,8},{10,11... | collective-permute-start | bytes 393224 | tf_op jit(solution)/shard_map/ppermute | solution.py:280

commit v4 on v0

v4 whole, which is shorter than its diff:
```python
import functools

import jax
import jax.numpy as jnp
from jax import lax
from jax.experimental import pallas as pl
from jax.experimental.pallas import tpu as pltpu
from jax.sharding import PartitionSpec as P

BLK = 128
NC = 512
ROUNDS = 3
R = 512
NI = 1024
RB = 4
HEAD = 2
HALF = NC // 2
PIECE = 128
VMEM_LIMIT = 24 << 20

F32 = jnp.float32
BF16 = jnp.bfloat16


def in_vmem(*arrays):
    return [pltpu.with_memory_space_constraint(a, pltpu.VMEM) for a in arrays]


def in_hbm(*arrays):
    return [pltpu.with_memory_space_constraint(a, pltpu.HBM) for a in arrays]


VSPEC = pl.BlockSpec(memory_space=pltpu.VMEM)
SSPEC = pl.BlockSpec(memory_space=pltpu.SMEM)
ASPEC = pl.BlockSpec(memory_space=pl.ANY)


def call(name, kernel, outs, in_specs, scratch=(), aliases={}):
    shapes = tuple(pltpu.VMEM(shape, dtype) for shape, dtype in outs)
    return pl.pallas_call(
        kernel,
        out_shape=shapes,
        in_specs=in_specs,
        out_specs=(VSPEC,) * len(shapes),
        scratch_shapes=list(scratch),
        input_output_aliases=aliases,
        compiler_params=pltpu.CompilerParams(vmem_limit_bytes=VMEM_LIMIT),
        name=name,
    )


def diag_kernel(block_ref, coupling_ref, stiff_ref, coupled_ref, held, sems, head_sems):
    def copy(b):
        part = pl.ds(b * BLK, BLK)
        return pltpu.make_async_copy(block_ref.at[:, part, part], held.at[b], sems.at[b])

    def head(j):
        return pltpu.make_async_copy(coupling_ref.at[j], coupled_ref.at[j], head_sems.at[j])

    for b in range(RB):
        copy(b).start()
    for j in range(HEAD):
        head(j).start()
    shape = (BLK, BLK)
    on = lax.broadcasted_iota(jnp.int32, shape, 0) == lax.broadcasted_iota(jnp.int32, shape, 1)
    for b in range(RB):
        copy(b).wait()
        tile = held[b].astype(F32)
        stiff_ref[:, b * BLK : (b + 1) * BLK] = jnp.sum(jnp.where(on[None], tile, 0.0), axis=1)
    for j in range(HEAD):
        head(j).wait()


def put(live, gram, block, schur, row, col):
    for r in range(0, gram.shape[0], BLK):
        for q in range(0, gram.shape[1], BLK):
            at = slice(row + r, row + r + BLK), slice(col + q, col + q + BLK)
            value = block[at].astype(F32) - gram[r : r + BLK, q : q + BLK]
            last = max(row + r, col + q) // BLK
            if last > 0:
                value = jnp.where(live > last, value, 0.0)
            schur[at] = value.astype(BF16)


def schur_block(live, c, block, schur):
    half = R // 2
    a, b = c[:, :half], c[:, half:]
    dims = (((0,), (0,)), ((), ()))
    gram = lax.dot_general(a, a, dims, preferred_element_type=F32)
    put(live, gram, block, schur, 0, 0)
    gram = lax.dot_general(a, b, dims, preferred_element_type=F32)
    put(live, gram, block, schur, 0, half)
    put(live, gram.T, block, schur, half, 0)
    gram = lax.dot_general(b, b, dims, preferred_element_type=F32)
    put(live, gram, block, schur, half, half)


def schur_kernel(first, last, here, stop, counts_ref, coupling_ref, _, block_ref, schur_ref, coupled_ref, sems):
    def copy(j):
        return pltpu.make_async_copy(coupling_ref.at[j], coupled_ref.at[j], sems.at[j - here])

    def start(j, carry):
        copy(j).start()
        return carry

    def wait(j, carry):
        copy(j).wait()
        return carry

    def pair(p, carry):
        j = first + 2 * p
        if last > here:
            @pl.when(j >= here)
            def _():
                copy(j).wait()
                copy(j + 1).wait()

        for k in range(2):
            schur_block(counts_ref[j + k], coupled_ref.at[j + k], block_ref.at[j + k], schur_ref.at[j + k - first])
        return carry

    lax.fori_loop(here, stop, start, 0)
    lax.fori_loop(0, (last - first) // 2, pair, 0)
    lax.fori_loop(max(here, last), stop, wait, 0)


def core():
    return lax.axis_index("gy") & 1


def first_kernel(partner_ref, primal_ref, stiff_ref, *refs):
    *others, schur_ref, up_ref, down_ref, basis_ref = refs
    subs = schur_ref.shape[0]
    column = lax.axis_index("gx")
    mine = stiff_ref[...]
    total = mine
    for d, other in enumerate(others, 1):
        times = jnp.int32(0)
        for r in range(ROUNDS):
            times += (partner_ref[r, column] == (column ^ d)).astype(jnp.int32)
        total = total + times.astype(F32) * other[...]
    weight = (mine / total).astype(BF16)
    primal = primal_ref[...]
    rows = lax.broadcasted_iota(jnp.int32, (NC, R), 0).astype(jnp.int16)
    part_rows = rows[:HALF]
    local = (primal - (1 - core()) * HALF).astype(jnp.int16)
    primal = primal.astype(jnp.int16)
    none = jnp.zeros((), BF16)
    images = []
    for j in range(subs):
        one = slice(j, j + 1)
        basis_ref[:, j * R : (j + 1) * R] = jnp.where(rows == primal[one], weight[one], none)
        part = jnp.where(part_rows == local[one], weight[one], none)
        images.append(image_of(schur_ref[j], part))
    image = jnp.concatenate(images, axis=0)
    for at, out_ref in ((0, up_ref), (HALF, down_ref)):
        out_ref[...] = jnp.dot(basis_ref[at : at + HALF], image, preferred_element_type=F32)


def image_of(schur, part):
    return lax.dot_general(
        schur, part, (((1,), (1,)), ((), ())), preferred_element_type=F32
    ).astype(BF16)


def upper_kernel(schur_ref, basis_ref, image_ref, up_ref):
    subs = schur_ref.shape[0]
    at = pl.ds(pl.multiple_of(core() * HALF, HALF), HALF)
    for j in range(subs):
        part = basis_ref[at, j * R : (j + 1) * R]
        image_ref[j * R : (j + 1) * R] = image_of(schur_ref[j], part)
    up_ref[...] = jnp.dot(basis_ref[:HALF], image_ref[...], preferred_element_type=F32)


def lower_kernel(basis_ref, image_ref, down_ref):
    down_ref[...] = jnp.dot(basis_ref[HALF:], image_ref[...], preferred_element_type=F32)


def pair_kernel(own_ref, other_ref, *outs):
    for d, out in enumerate(outs):
        at = slice(d * PIECE, (d + 1) * PIECE)
        out[...] = own_ref[at] + other_ref[at]


def add_kernel(own_ref, other_ref, out_ref):
    out_ref[...] = own_ref[...] + other_ref[...]


def scale_kernel(*refs):
    count = NC // PIECE
    own, other = refs[:count], refs[count : 2 * count]
    out_ref, tile, sems = refs[2 * count :]
    for pieces, column in ((own, core()), (other, 1 - core())):
        across = pl.ds(pl.multiple_of(column * HALF, HALF), HALF)
        for d, piece in enumerate(pieces):
            tile[d * PIECE : (d + 1) * PIECE, across] = piece[...]
    mean = jnp.sum(jnp.abs(tile[...]), axis=1, keepdims=True) / NC
    scale = 1.0 / jnp.sqrt(mean + 1e-06)
    across = jnp.broadcast_to(scale, (NC, BLK)).T[:1, :]

    def copy(b):
        at = pl.ds(b * BLK, BLK)
        return pltpu.make_async_copy(tile.at[at], out_ref.at[at], sems.at[b])

    for b in range(NC // BLK):
        at = slice(b * BLK, (b + 1) * BLK)
        tile[at, :] = tile[at, :] * scale[at, :] * across
        copy(b).start()
    for b in range(NC // BLK):
        copy(b).wait()


def per_device(columns, line, coupling, local_block, counts, primal, partner):
    coupling, local_block, counts, primal = coupling[0], local_block[0], counts[0], primal[0]
    subs = coupling.shape[0]
    coupled_shape = ((subs, NI, R), BF16)

    def swap(a, axis, size, bit):
        return lax.ppermute(a, axis, [(i, i ^ bit) for i in range(size)])

    stiff, coupled = call(
        "diag",
        diag_kernel,
        [((subs, R), F32), coupled_shape],
        [ASPEC, ASPEC],
        [
            pltpu.VMEM((RB, subs, BLK, BLK), BF16),
            pltpu.SemaphoreType.DMA((RB,)),
            pltpu.SemaphoreType.DMA((HEAD,)),
        ],
    )(*in_hbm(local_block, coupling))
    def schur(first, last, here, stop, coupled):
        return call(
            "schur",
            functools.partial(schur_kernel, first, last, here, stop),
            [((last - first, R, R), BF16), coupled_shape],
            [SSPEC, ASPEC, VSPEC, VSPEC],
            [pltpu.SemaphoreType.DMA((max(stop - here, 1),))],
            {2: 1},
        )(counts, *in_hbm(coupling), *in_vmem(coupled, local_block))

    others = [swap(stiff, "gx", columns, d) for d in range(1, columns)]
    schur_all, _ = schur(0, subs, HEAD, subs, coupled)

    block = ((HALF, HALF), F32)
    up, down, basis = call(
        "first_half", first_kernel, [block, block, ((NC, subs * R), BF16)], [SSPEC] + [VSPEC] * (columns + 2)
    )(partner, primal, *in_vmem(stiff, *others, schur_all))
    other_up, other_down = swap(up, "gy", line, 1), swap(down, "gy", line, 1)
    image, up = call(
        "upper", upper_kernel, [((subs * R, HALF), BF16), block], [VSPEC] * 2
    )(*in_vmem(schur_all, basis))
    pieces = ((PIECE, HALF), F32)
    pair = call("pair", pair_kernel, [pieces] * (HALF // PIECE), [VSPEC] * 2)
    upper = pair(*in_vmem(up, other_up))
    (down,) = call("lower", lower_kernel, [block], [VSPEC] * 2)(*in_vmem(basis, image))
    lower = pair(*in_vmem(down, other_down))

    add = call("add", add_kernel, [pieces], [VSPEC] * 2)
    steps = [2 << b for b in range((line // 2 - 1).bit_length())]
    own = [*upper, *lower]
    for step in range(len(steps)):
        for d in range(len(own)):
            bit = steps[step] if d % 2 == 0 else steps[-1 - step]
            (own[d],) = add(*in_vmem(own[d], swap(own[d], "gy", line, bit)))
    other = [swap(piece, "gy", line, 1) for piece in own]
    result = pl.pallas_call(
        scale_kernel,
        out_shape=jax.ShapeDtypeStruct((NC, NC), F32),
        in_specs=[VSPEC] * (2 * len(own)),
        out_specs=ASPEC,
        scratch_shapes=[pltpu.VMEM((NC, NC), F32), pltpu.SemaphoreType.DMA((NC // BLK,))],
        compiler_params=pltpu.CompilerParams(vmem_limit_bytes=VMEM_LIMIT),
        name="scale",
    )(*in_vmem(*own, *other))
    return result[None]


def solution(mesh):
    placed = (
        P("gx", "gy", None, None),
        P("gx", "gy", None, None),
        P("gx", "gy"),
        P("gx", "gy", None),
        P(),
    )
    body = functools.partial(per_device, mesh.shape["gx"], mesh.shape["gy"])
    return jax.shard_map(
        body, mesh=mesh, in_specs=placed, out_specs=P("gx", None, None), check_vma=False
    )
```

time: 171 us -> 38.7 us (0.23); the launches traced: 168 us -> 38.6 us
  local copies, waits for them, and re-layouts: 52.1 us -> 0.02 us
  waiting for transfers between devices: 57.9 us -> 6.82 us
  matrix products: 23.7 us -> 0 us
  starting transfers between devices: 0.01 us -> 16.7 us
  Pallas kernels: 0 us -> 14.9 us
  blocking collectives: 14.9 us -> 0 us
  between operations: 13.4 us -> 0.21 us
  other arithmetic: 5.84 us -> 0 us
    psum x1 -> x0, waiting for transfers between devices: 57.9 us -> none  [per_device(): summed = lax.psum(tile, 'gy')]
    squeeze x1 -> x0, local copies, waits for them, and re-layouts: 44.1 us -> none  [per_device(): stiff = jnp.diagonal(local_block[0], axis1=1, axis2=2).astype(jnp.float32)]
    dot_general x2 -> x0, matrix products: 23.7 us -> none  [the longest x1 13.6 us: per_device(): jnp.einsum('snr,snq->srq', coupling[0], coupling[0], preferred_element_ty...]
    ppermute x0 -> x17, starting transfers between devices: none -> 16.7 us  [swap(): return lax.ppermute(a, axis, [(i, i ^ bit) for i in range(size)])]
    all_gather x1 -> x0, blocking collectives: 14.9 us -> none  [per_device(): lax.all_gather(part, 'gx', axis=0, tiled=True)]
    pallas_call x0 -> x16, Pallas kernels: none -> 14.9 us  [the longest x1 5.5 us: schur(): call('schur', functools.partial(schur_kernel, first, last, here, stop), [...]
    ppermute x0 -> x17, waiting for transfers between devices: none -> 6.82 us  [swap(): return lax.ppermute(a, axis, [(i, i ^ bit) for i in range(size)])]
    gather x2 -> x0, local copies, waits for them, and re-layouts: 6.53 us -> none  [per_device(): stiff = jnp.diagonal(local_block[0], axis1=1, axis2=2).astype(jnp.float32)]
  transfers between devices with their start and end apart: 1 -> 17, of which waited for: 1 -> 8; matrix products, arithmetic and copies ran while one was open for 0% -> 0% of each run, Pallas kernels for 0% -> 22%
where the time goes in v4:
time: 38.7 us; the launch traced here: 38.6 us
  starting transfers between devices  16.7 us (43%)
  Pallas kernels  14.9 us (39%)
  waiting for transfers between devices  6.82 us (18%)
    ppermute x17, starting transfers between devices, swap(): return lax.ppermute(a, axis, [(i, i ^ bit) for i in range(size)])  16.7 us
    ppermute x17, waiting for transfers between devices, swap(): return lax.ppermute(a, axis, [(i, i ^ bit) for i in range(size)])  6.82 us
    pallas_call x1, Pallas kernels, schur(): call('schur', functools.partial(schur_kernel, first, last, here, stop), [...  5.5 us
    pallas_call x1, Pallas kernels, per_device(): call('first_half', first_kernel, [block, block, ((NC, subs * R), BF16)],...  2.97 us
    pallas_call x1, Pallas kernels, per_device(): call('diag', diag_kernel, [((subs, R), F32), coupled_shape], [ASPEC, ASPE...  2.09 us
    pallas_call x1, Pallas kernels, per_device(): call('upper', upper_kernel, [((subs * R, HALF), BF16), block], [VSPEC] * 2)  2.03 us
    pallas_call x1, Pallas kernels, per_device(): pl.pallas_call(scale_kernel, out_shape=jax.ShapeDtypeStruct((NC, NC), F32...  1.38 us
  transfers between devices with their start and end apart: 17, of which 8 were waited for; matrix products, arithmetic and copies ran while one was open for 0% of the time, Pallas kernels for 22%

profile of v4, /device:TPU:0, one launch (start us, length us, event | category | flops | bytes accessed | tf_op | source)
XLA Modules:
  0.0 38.6 jit_solution(17843060490488543031)
XLA Ops:
  0.0 2.1 %diag.1 = (f32[8,512]{1,0:T(8,128)S(1)}, bf16[8,1024,512]{2,1,0:T(8,128)(2,1)S(1)}) custom-call(bf16[8,512,512]{2,1,0:T(8,128)(2,1)} %bitcast.5, bf16[8,1024,512]{2,1,0:T(8,128)(2,1)} %bitcast.9), custom_call_target="tpu_custom_call" | custom-call | tf_op jit(solution)/shard_map/diag/pallas_call | solution.py:221
  2.1 3.1 %collective-permute-start = (f32[8,512]{1,0:T(8,128)S(1)}, f32[8,512]{1,0:T(8,128)S(1)}, u32[]{:S(2)}, u32[]{:S(2)}) collective-permute-start(f32[8,512]{1,0:T(8,128)S(1)} %get-tuple-element.19.stiff_ref), channel_id=1, source_target_pairs={{0,8},{8,0},{16,24},{24,16},{1,9},{9,1},{17,25},{25,17},{2,10},{10... | collective-permute-start | bytes 49160 | tf_op jit(solution)/shard_map/ppermute | solution.py:219
  5.2 2.6 %collective-permute-start.1 = (f32[8,512]{1,0:T(8,128)S(1)}, f32[8,512]{1,0:T(8,128)S(1)}, u32[]{:S(2)}, u32[]{:S(2)}) collective-permute-start(f32[8,512]{1,0:T(8,128)S(1)} %get-tuple-element.19.stiff_ref), channel_id=1, source_target_pairs={{0,16},{8,24},{16,0},{24,8},{1,17},{9,25},{17,1},{25,9},{2,18},{10... | collective-permute-start | bytes 49160 | tf_op jit(solution)/shard_map/ppermute | solution.py:219
  7.8 0.0 copy-start.1
  7.8 0.0 copy-start.2
  7.8 5.5 %schur.1 = (bf16[8,512,512]{2,1,0:T(8,128)(2,1)S(1)}, bf16[8,1024,512]{2,1,0:T(8,128)(2,1)S(1)}) custom-call(s32[8]{0:T(128)S(1)} %bitcast.8, bf16[8,1024,512]{2,1,0:T(8,128)(2,1)} %bitcast.10, bf16[8,1024,512]{2,1,0:T(8,128)(2,1)S(1)} %get-tuple-element.17._, bf16[8,512,512]{2,1,0:T(8,128)(2,1)S(1)} %bitcast.6), custom_call_target="tpu_custom_call", output_to_operand_aliasing={{1}: (2, {})} | custom-call | tf_op jit(solution)/shard_map/schur/pallas_call | solution.py:233
  13.4 3.0 %first_half.1 = (f32[256,256]{1,0:T(8,128)S(1)}, f32[256,256]{1,0:T(8,128)S(1)}, bf16[512,4096]{1,0:T(8,128)(2,1)S(1)}) custom-call(s32[3,4]{1,0:T(4,128)S(1)} %copy-done.2, s32[8,512]{1,0:T(8,128)S(1)} %bitcast.7, f32[8,512]{1,0:T(8,128)S(1)} %get-tuple-element.19.stiff_ref, f32[8,512]{1,0:T(8,128)S(1)} %collective-permute-done.refs_0_, ...), custom_call_target="tpu_custom_call" | custom-call | tf_op jit(solution)/shard_map/first_half/pallas_call | solution.py:246
  16.4 0.1 collective-permute-start.8
  16.4 0.5 %collective-permute-start.3 = (f32[256,256]{1,0:T(8,128)S(1)}, f32[256,256]{1,0:T(8,128)S(1)}, u32[]{:S(2)}, u32[]{:S(2)}) collective-permute-start(f32[256,256]{1,0:T(8,128)S(1)} %get-tuple-element.22), channel_id=1, source_target_pairs={{0,1},{1,0},{2,3},{3,2},{4,5},{5,4},{6,7},{7,6},{8,9},{9,8},{10,11... | collective-permute-start | bytes 786440 | tf_op jit(solution)/shard_map/ppermute | solution.py:219
  16.9 2.0 %upper.1 = (bf16[4096,256]{1,0:T(8,128)(2,1)S(1)}, f32[256,256]{1,0:T(8,128)S(1)}) custom-call(bf16[8,512,512]{2,1,0:T(8,128)(2,1)S(1)} %get-tuple-element.18.refs_3_.schur_ref, bf16[512,4096]{1,0:T(8,128)(2,1)S(1)} %get-tuple-element.20.basis_ref), custom_call_target="tpu_custom_call" | custom-call | tf_op jit(solution)/shard_map/upper/pallas_call | solution.py:250
  19.0 0.7 %lower.1.own_ref = f32[256,256]{1,0:T(8,128)S(1)} custom-call(bf16[512,4096]{1,0:T(8,128)(2,1)S(1)} %get-tuple-element.20.basis_ref, bf16[4096,256]{1,0:T(8,128)(2,1)S(1)} %get-tuple-element.25.image_ref), custom_call_target="tpu_custom_call" | custom-call | tf_op jit(solution)/shard_map/lower/pallas_call | solution.py:256
  19.8 1.8 %collective-permute-start.11 = (f32[128,256]{1,0:T(8,128)S(1)}, f32[128,256]{1,0:T(8,128)S(1)}, u32[]{:S(2)}, u32[]{:S(2)}) collective-permute-start(f32[128,256]{1,0:T(8,128)S(1)} %get-tuple-element.28.own_ref), channel_id=1, source_target_pairs={{0,4},{1,5},{2,6},{3,7},{4,0},{5,1},{6,2},{7,3},{8,12},{9,13},{10,... | collective-permute-start | bytes 393224 | tf_op jit(solution)/shard_map/ppermute | solution.py:219
  21.5 1.5 %collective-permute-start.9 = (f32[128,256]{1,0:T(8,128)S(1)}, f32[128,256]{1,0:T(8,128)S(1)}, u32[]{:S(2)}, u32[]{:S(2)}) collective-permute-start(f32[128,256]{1,0:T(8,128)S(1)} %get-tuple-element.27.own_ref), channel_id=1, source_target_pairs={{0,2},{1,3},{2,0},{3,1},{4,6},{5,7},{6,4},{7,5},{8,10},{9,11},{10,... | collective-permute-start | bytes 393224 | tf_op jit(solution)/shard_map/ppermute | solution.py:219
  23.1 0.6 %collective-permute-start.6 = (f32[128,256]{1,0:T(8,128)S(1)}, f32[128,256]{1,0:T(8,128)S(1)}, u32[]{:S(2)}, u32[]{:S(2)}) collective-permute-start(f32[128,256]{1,0:T(8,128)S(1)} %get-tuple-element.24.own_ref), channel_id=1, source_target_pairs={{0,4},{1,5},{2,6},{3,7},{4,0},{5,1},{6,2},{7,3},{8,12},{9,13},{10,... | collective-permute-start | bytes 393224 | tf_op jit(solution)/shard_map/ppermute | solution.py:219
  23.6 0.3 collective-permute-start.4
  24.0 1.4 %collective-permute-done.11.other_ref = f32[128,256]{1,0:T(8,128)S(1)} collective-permute-done((f32[128,256]{1,0:T(8,128)S(1)}, f32[128,256]{1,0:T(8,128)S(1)}, u32[]{:S(2)}, u32[]{:S(2)}) %collective-permute-start.11) | collective-permute-done | bytes 131104 | tf_op jit(solution)/shard_map/ppermute | solution.py:219
  25.4 2.5 %collective-permute-start.12 = (f32[128,256]{1,0:T(8,128)S(1)}, f32[128,256]{1,0:T(8,128)S(1)}, u32[]{:S(2)}, u32[]{:S(2)}) collective-permute-start(f32[128,256]{1,0:T(8,128)S(1)} %add.14.own_ref), channel_id=1, source_target_pairs={{0,2},{1,3},{2,0},{3,1},{4,6},{5,7},{6,4},{7,5},{8,10},{9,11},{10,... | collective-permute-start | bytes 393224 | tf_op jit(solution)/shard_map/ppermute | solution.py:219
  28.0 1.6 %collective-permute-start.10 = (f32[128,256]{1,0:T(8,128)S(1)}, f32[128,256]{1,0:T(8,128)S(1)}, u32[]{:S(2)}, u32[]{:S(2)}) collective-permute-start(f32[128,256]{1,0:T(8,128)S(1)} %add.12.own_ref), channel_id=1, source_target_pairs={{0,4},{1,5},{2,6},{3,7},{4,0},{5,1},{6,2},{7,3},{8,12},{9,13},{10,... | collective-permute-start | bytes 393224 | tf_op jit(solution)/shard_map/ppermute | solution.py:219
  29.6 0.6 %collective-permute-start.7 = (f32[128,256]{1,0:T(8,128)S(1)}, f32[128,256]{1,0:T(8,128)S(1)}, u32[]{:S(2)}, u32[]{:S(2)}) collective-permute-start(f32[128,256]{1,0:T(8,128)S(1)} %add.10.own_ref), channel_id=1, source_target_pairs={{0,2},{1,3},{2,0},{3,1},{4,6},{5,7},{6,4},{7,5},{8,10},{9,11},{10,... | collective-permute-start | bytes 393224 | tf_op jit(solution)/shard_map/ppermute | solution.py:219
  30.2 0.6 %collective-permute-done.4.other_ref = f32[128,256]{1,0:T(8,128)S(1)} collective-permute-done((f32[128,256]{1,0:T(8,128)S(1)}, f32[128,256]{1,0:T(8,128)S(1)}, u32[]{:S(2)}, u32[]{:S(2)}) %collective-permute-start.4) | collective-permute-done | bytes 131104 | tf_op jit(solution)/shard_map/ppermute | solution.py:219
  30.8 1.2 %collective-permute-start.5 = (f32[128,256]{1,0:T(8,128)S(1)}, f32[128,256]{1,0:T(8,128)S(1)}, u32[]{:S(2)}, u32[]{:S(2)}) collective-permute-start(f32[128,256]{1,0:T(8,128)S(1)} %add.8.own_ref), channel_id=1, source_target_pairs={{0,4},{1,5},{2,6},{3,7},{4,0},{5,1},{6,2},{7,3},{8,12},{9,13},{10,... | collective-permute-start | bytes 393224 | tf_op jit(solution)/shard_map/ppermute | solution.py:219
  32.0 1.5 %collective-permute-done.12.other_ref = f32[128,256]{1,0:T(8,128)S(1)} collective-permute-done((f32[128,256]{1,0:T(8,128)S(1)}, f32[128,256]{1,0:T(8,128)S(1)}, u32[]{:S(2)}, u32[]{:S(2)}) %collective-permute-start.12) | collective-permute-done | bytes 131104 | tf_op jit(solution)/shard_map/ppermute | solution.py:219
  33.6 0.1 collective-permute-start.16
  33.6 0.7 %collective-permute-done.10.other_ref = f32[128,256]{1,0:T(8,128)S(1)} collective-permute-done((f32[128,256]{1,0:T(8,128)S(1)}, f32[128,256]{1,0:T(8,128)S(1)}, u32[]{:S(2)}, u32[]{:S(2)}) %collective-permute-start.10) | collective-permute-done | bytes 131104 | tf_op jit(solution)/shard_map/ppermute | solution.py:219
  34.3 0.1 collective-permute-start.15
  34.4 0.7 %collective-permute-done.7.other_ref = f32[128,256]{1,0:T(8,128)S(1)} collective-permute-done((f32[128,256]{1,0:T(8,128)S(1)}, f32[128,256]{1,0:T(8,128)S(1)}, u32[]{:S(2)}, u32[]{:S(2)}) %collective-permute-start.7) | collective-permute-done | bytes 131104 | tf_op jit(solution)/shard_map/ppermute | solution.py:219
  35.2 0.1 collective-permute-start.14
  35.3 0.5 %collective-permute-done.5.other_ref = f32[128,256]{1,0:T(8,128)S(1)} collective-permute-done((f32[128,256]{1,0:T(8,128)S(1)}, f32[128,256]{1,0:T(8,128)S(1)}, u32[]{:S(2)}, u32[]{:S(2)}) %collective-permute-start.5) | collective-permute-done | bytes 131104 | tf_op jit(solution)/shard_map/ppermute | solution.py:219
  35.8 0.1 collective-permute-start.13
  35.9 0.7 %collective-permute-done.14.refs_5_ = f32[128,256]{1,0:T(8,128)S(1)} collective-permute-done((f32[128,256]{1,0:T(8,128)S(1)}, f32[128,256]{1,0:T(8,128)S(1)}, u32[]{:S(2)}, u32[]{:S(2)}) %collective-permute-start.14) | collective-permute-done | bytes 131104 | tf_op jit(solution)/shard_map/ppermute | solution.py:219
  36.6 0.6 %collective-permute-done.13.refs_4_ = f32[128,256]{1,0:T(8,128)S(1)} collective-permute-done((f32[128,256]{1,0:T(8,128)S(1)}, f32[128,256]{1,0:T(8,128)S(1)}, u32[]{:S(2)}, u32[]{:S(2)}) %collective-permute-start.13) | collective-permute-done | bytes 131104 | tf_op jit(solution)/shard_map/ppermute | solution.py:219
  37.2 1.4 %scale.1 = f32[512,512]{1,0:T(8,128)} custom-call(f32[128,256]{1,0:T(8,128)S(1)} %add.9.refs_0_, f32[128,256]{1,0:T(8,128)S(1)} %add.11.refs_1_, f32[128,256]{1,0:T(8,128)S(1)} %add.13.refs_2_, f32[128,256]{1,0:T(8,128)S(1)} %add.15.refs_3_, f32[128,256]{1,0:T(8,128)S(1)} %collective-permute-done.13.refs_4_, f32[128,256]{1,0:T(8,128)S(1)} %collective-permute-done.14.refs_5_, ...), custom_call_target="tpu_custom_call" | custom-call | tf_op jit(solution)/shard_map/scale/pallas_call | solution.py:267
  (26 shorter events, 0.2 us)
Async XLA Ops:
  0.0 7.8 %copy-start = (bf16[1,8,512,512]{3,2,1,0:T(8,128)(2,1)S(1)}, bf16[1,8,512,512]{3,2,1,0:T(8,128)(2,1)}, u32[]{:S(2)}) copy-start(bf16[1,8,512,512]{3,2,1,0:T(8,128)(2,1)} %param.6) | copy-start | bytes 12582916
  0.0 7.8 %copy-start.3 = (s32[1,8]{1,0:T(1,128)S(1)}, s32[1,8]{1,0:T(1,128)}, u32[]{:S(2)}) copy-start(s32[1,8]{1,0:T(1,128)} %param.7) | copy-start | bytes 100
  2.1 11.2 %collective-permute-start = (f32[8,512]{1,0:T(8,128)S(1)}, f32[8,512]{1,0:T(8,128)S(1)}, u32[]{:S(2)}, u32[]{:S(2)}) collective-permute-start(f32[8,512]{1,0:T(8,128)S(1)} %get-tuple-element.19.stiff_ref), channel_id=1, source_target_pairs={{0,8},{8,0},{16,24},{24,16},{1,9},{9,1},{17,25},{25,17},{2,10},{10... | collective-permute-start | bytes 49160 | tf_op jit(solution)/shard_map/ppermute | solution.py:219
  5.2 8.1 %collective-permute-start.1 = (f32[8,512]{1,0:T(8,128)S(1)}, f32[8,512]{1,0:T(8,128)S(1)}, u32[]{:S(2)}, u32[]{:S(2)}) collective-permute-start(f32[8,512]{1,0:T(8,128)S(1)} %get-tuple-element.19.stiff_ref), channel_id=1, source_target_pairs={{0,16},{8,24},{16,0},{24,8},{1,17},{9,25},{17,1},{25,9},{2,18},{10... | collective-permute-start | bytes 49160 | tf_op jit(solution)/shard_map/ppermute | solution.py:219
  7.8 5.6 %collective-permute-start.2 = (f32[8,512]{1,0:T(8,128)S(1)}, f32[8,512]{1,0:T(8,128)S(1)}, u32[]{:S(2)}, u32[]{:S(2)}) collective-permute-start(f32[8,512]{1,0:T(8,128)S(1)} %get-tuple-element.19.stiff_ref), channel_id=1, source_target_pairs={{0,24},{8,16},{16,8},{24,0},{1,25},{9,17},{17,9},{25,1},{2,26},{10... | collective-permute-start | bytes 49160 | tf_op jit(solution)/shard_map/ppermute | solution.py:219
  7.8 5.6 %copy-start.1 = (s32[1,8,512]{2,1,0:T(8,128)S(1)}, s32[1,8,512]{2,1,0:T(8,128)}, u32[]{:S(2)}) copy-start(s32[1,8,512]{2,1,0:T(8,128)} %param.8) | copy-start | bytes 49156
  7.8 5.6 %copy-start.2 = (s32[3,4]{1,0:T(4,128)S(1)}, s32[3,4]{1,0:T(4,128)}, u32[]{:S(2)}) copy-start(s32[3,4]{1,0:T(4,128)} %partner_ref.1) | copy-start | bytes 148
  16.4 3.4 %collective-permute-start.8 = (f32[256,256]{1,0:T(8,128)S(1)}, f32[256,256]{1,0:T(8,128)S(1)}, u32[]{:S(2)}, u32[]{:S(2)}) collective-permute-start(f32[256,256]{1,0:T(8,128)S(1)} %get-tuple-element.26), channel_id=1, source_target_pairs={{0,1},{1,0},{2,3},{3,2},{4,5},{5,4},{6,7},{7,6},{8,9},{9,8},{10,11... | collective-permute-start | bytes 786440 | tf_op jit(solution)/shard_map/ppermute | solution.py:219
  16.4 6.6 %collective-permute-start.3 = (f32[256,256]{1,0:T(8,128)S(1)}, f32[256,256]{1,0:T(8,128)S(1)}, u32[]{:S(2)}, u32[]{:S(2)}) collective-permute-start(f32[256,256]{1,0:T(8,128)S(1)} %get-tuple-element.22), channel_id=1, source_target_pairs={{0,1},{1,0},{2,3},{3,2},{4,5},{5,4},{6,7},{7,6},{8,9},{9,8},{10,11... | collective-permute-start | bytes 786440 | tf_op jit(solution)/shard_map/ppermute | solution.py:219
  19.8 5.6 %collective-permute-start.11 = (f32[128,256]{1,0:T(8,128)S(1)}, f32[128,256]{1,0:T(8,128)S(1)}, u32[]{:S(2)}, u32[]{:S(2)}) collective-permute-start(f32[128,256]{1,0:T(8,128)S(1)} %get-tuple-element.28.own_ref), channel_id=1, source_target_pairs={{0,4},{1,5},{2,6},{3,7},{4,0},{5,1},{6,2},{7,3},{8,12},{9,13},{10,... | collective-permute-start | bytes 393224 | tf_op jit(solution)/shard_map/ppermute | solution.py:219
  21.5 6.4 %collective-permute-start.9 = (f32[128,256]{1,0:T(8,128)S(1)}, f32[128,256]{1,0:T(8,128)S(1)}, u32[]{:S(2)}, u32[]{:S(2)}) collective-permute-start(f32[128,256]{1,0:T(8,128)S(1)} %get-tuple-element.27.own_ref), channel_id=1, source_target_pairs={{0,2},{1,3},{2,0},{3,1},{4,6},{5,7},{6,4},{7,5},{8,10},{9,11},{10,... | collective-permute-start | bytes 393224 | tf_op jit(solution)/shard_map/ppermute | solution.py:219
  23.1 6.5 %collective-permute-start.6 = (f32[128,256]{1,0:T(8,128)S(1)}, f32[128,256]{1,0:T(8,128)S(1)}, u32[]{:S(2)}, u32[]{:S(2)}) collective-permute-start(f32[128,256]{1,0:T(8,128)S(1)} %get-tuple-element.24.own_ref), channel_id=1, source_target_pairs={{0,4},{1,5},{2,6},{3,7},{4,0},{5,1},{6,2},{7,3},{8,12},{9,13},{10,... | collective-permute-start | bytes 393224 | tf_op jit(solution)/shard_map/ppermute | solution.py:219
  23.6 7.1 %collective-permute-start.4 = (f32[128,256]{1,0:T(8,128)S(1)}, f32[128,256]{1,0:T(8,128)S(1)}, u32[]{:S(2)}, u32[]{:S(2)}) collective-permute-start(f32[128,256]{1,0:T(8,128)S(1)} %get-tuple-element.23.own_ref), channel_id=1, source_target_pairs={{0,2},{1,3},{2,0},{3,1},{4,6},{5,7},{6,4},{7,5},{8,10},{9,11},{10,... | collective-permute-start | bytes 393224 | tf_op jit(solution)/shard_map/ppermute | solution.py:219
  25.4 8.1 %collective-permute-start.12 = (f32[128,256]{1,0:T(8,128)S(1)}, f32[128,256]{1,0:T(8,128)S(1)}, u32[]{:S(2)}, u32[]{:S(2)}) collective-permute-start(f32[128,256]{1,0:T(8,128)S(1)} %add.14.own_ref), channel_id=1, source_target_pairs={{0,2},{1,3},{2,0},{3,1},{4,6},{5,7},{6,4},{7,5},{8,10},{9,11},{10,... | collective-permute-start | bytes 393224 | tf_op jit(solution)/shard_map/ppermute | solution.py:219
  28.0 6.4 %collective-permute-start.10 = (f32[128,256]{1,0:T(8,128)S(1)}, f32[128,256]{1,0:T(8,128)S(1)}, u32[]{:S(2)}, u32[]{:S(2)}) collective-permute-start(f32[128,256]{1,0:T(8,128)S(1)} %add.12.own_ref), channel_id=1, source_target_pairs={{0,4},{1,5},{2,6},{3,7},{4,0},{5,1},{6,2},{7,3},{8,12},{9,13},{10,... | collective-permute-start | bytes 393224 | tf_op jit(solution)/shard_map/ppermute | solution.py:219
  29.6 5.6 %collective-permute-start.7 = (f32[128,256]{1,0:T(8,128)S(1)}, f32[128,256]{1,0:T(8,128)S(1)}, u32[]{:S(2)}, u32[]{:S(2)}) collective-permute-start(f32[128,256]{1,0:T(8,128)S(1)} %add.10.own_ref), channel_id=1, source_target_pairs={{0,2},{1,3},{2,0},{3,1},{4,6},{5,7},{6,4},{7,5},{8,10},{9,11},{10,... | collective-permute-start | bytes 393224 | tf_op jit(solution)/shard_map/ppermute | solution.py:219
  30.8 5.0 %collective-permute-start.5 = (f32[128,256]{1,0:T(8,128)S(1)}, f32[128,256]{1,0:T(8,128)S(1)}, u32[]{:S(2)}, u32[]{:S(2)}) collective-permute-start(f32[128,256]{1,0:T(8,128)S(1)} %add.8.own_ref), channel_id=1, source_target_pairs={{0,4},{1,5},{2,6},{3,7},{4,0},{5,1},{6,2},{7,3},{8,12},{9,13},{10,... | collective-permute-start | bytes 393224 | tf_op jit(solution)/shard_map/ppermute | solution.py:219
  33.6 2.3 %collective-permute-start.16 = (f32[128,256]{1,0:T(8,128)S(1)}, f32[128,256]{1,0:T(8,128)S(1)}, u32[]{:S(2)}, u32[]{:S(2)}) collective-permute-start(f32[128,256]{1,0:T(8,128)S(1)} %add.15.refs_3_), channel_id=1, source_target_pairs={{0,1},{1,0},{2,3},{3,2},{4,5},{5,4},{6,7},{7,6},{8,9},{9,8},{10,11... | collective-permute-start | bytes 393224 | tf_op jit(solution)/shard_map/ppermute | solution.py:219
  34.3 1.6 %collective-permute-start.15 = (f32[128,256]{1,0:T(8,128)S(1)}, f32[128,256]{1,0:T(8,128)S(1)}, u32[]{:S(2)}, u32[]{:S(2)}) collective-permute-start(f32[128,256]{1,0:T(8,128)S(1)} %add.13.refs_2_), channel_id=1, source_target_pairs={{0,1},{1,0},{2,3},{3,2},{4,5},{5,4},{6,7},{7,6},{8,9},{9,8},{10,11... | collective-permute-start | bytes 393224 | tf_op jit(solution)/shard_map/ppermute | solution.py:219
  35.2 1.4 %collective-permute-start.14 = (f32[128,256]{1,0:T(8,128)S(1)}, f32[128,256]{1,0:T(8,128)S(1)}, u32[]{:S(2)}, u32[]{:S(2)}) collective-permute-start(f32[128,256]{1,0:T(8,128)S(1)} %add.11.refs_1_), channel_id=1, source_target_pairs={{0,1},{1,0},{2,3},{3,2},{4,5},{5,4},{6,7},{7,6},{8,9},{9,8},{10,11... | collective-permute-start | bytes 393224 | tf_op jit(solution)/shard_map/ppermute | solution.py:219
  35.8 1.4 %collective-permute-start.13 = (f32[128,256]{1,0:T(8,128)S(1)}, f32[128,256]{1,0:T(8,128)S(1)}, u32[]{:S(2)}, u32[]{:S(2)}) collective-permute-start(f32[128,256]{1,0:T(8,128)S(1)} %add.9.refs_0_), channel_id=1, source_target_pairs={{0,1},{1,0},{2,3},{3,2},{4,5},{5,4},{6,7},{7,6},{8,9},{9,8},{10,11... | collective-permute-start | bytes 393224 | tf_op jit(solution)/shard_map/ppermute | solution.py:219

commit v5 on v4

--- a/solution.py
+++ b/solution.py
@@ -84,14 +84,11 @@
 
 def schur_block(live, c, block, schur):
     half = R // 2
-    a, b = c[:, :half], c[:, half:]
     dims = (((0,), (0,)), ((), ()))
-    gram = lax.dot_general(a, a, dims, preferred_element_type=F32)
+    gram = lax.dot_general(c[:, :half], c[...], dims, preferred_element_type=F32)
     put(live, gram, block, schur, 0, 0)
-    gram = lax.dot_general(a, b, dims, preferred_element_type=F32)
-    put(live, gram, block, schur, 0, half)
-    put(live, gram.T, block, schur, half, 0)
-    gram = lax.dot_general(b, b, dims, preferred_element_type=F32)
+    put(live, gram[:, half:].T, block, schur, half, 0)
+    gram = lax.dot_general(c[:, half:], c[:, half:], dims, preferred_element_type=F32)
     put(live, gram, block, schur, half, half)
 
 
@@ -129,7 +126,7 @@
 
 
 def first_kernel(partner_ref, primal_ref, stiff_ref, *refs):
-    *others, schur_ref, up_ref, down_ref, basis_ref = refs
+    *others, schur_ref, tile_ref, basis_ref = refs
     subs = schur_ref.shape[0]
     column = lax.axis_index("gx")
     mine = stiff_ref[...]
@@ -153,8 +150,9 @@
         part = jnp.where(part_rows == local[one], weight[one], none)
         images.append(image_of(schur_ref[j], part))
     image = jnp.concatenate(images, axis=0)
-    for at, out_ref in ((0, up_ref), (HALF, down_ref)):
-        out_ref[...] = jnp.dot(basis_ref[at : at + HALF], image, preferred_element_type=F32)
+    for at in range(0, NC, 256):
+        rows = slice(at, at + 256)
+        tile_ref[rows] = jnp.dot(basis_ref[rows], image, preferred_element_type=F32)
 
 
 def image_of(schur, part):
@@ -163,23 +161,22 @@
     ).astype(BF16)
 
 
-def upper_kernel(schur_ref, basis_ref, image_ref, up_ref):
-    subs = schur_ref.shape[0]
+def second_kernel(schur_ref, basis_ref, image_ref, up_ref):
     at = pl.ds(pl.multiple_of(core() * HALF, HALF), HALF)
-    for j in range(subs):
+    for j in range(schur_ref.shape[0]):
         part = basis_ref[at, j * R : (j + 1) * R]
         image_ref[j * R : (j + 1) * R] = image_of(schur_ref[j], part)
     up_ref[...] = jnp.dot(basis_ref[:HALF], image_ref[...], preferred_element_type=F32)
 
 
-def lower_kernel(basis_ref, image_ref, down_ref):
-    down_ref[...] = jnp.dot(basis_ref[HALF:], image_ref[...], preferred_element_type=F32)
-
-
-def pair_kernel(own_ref, other_ref, *outs):
+def pieces_kernel(basis_ref, image_ref, up_ref, other_ref, *outs):
+    down = jnp.dot(basis_ref[HALF:], image_ref[...], preferred_element_type=F32)
     for d, out in enumerate(outs):
         at = slice(d * PIECE, (d + 1) * PIECE)
-        out[...] = own_ref[at] + other_ref[at]
+        if d * PIECE < HALF:
+            out[...] = up_ref[at] + other_ref[at]
+        else:
+            out[...] = down[d * PIECE - HALF : (d + 1) * PIECE - HALF] + other_ref[at]
 
 
 def add_kernel(own_ref, other_ref, out_ref):
@@ -242,23 +239,24 @@
     others = [swap(stiff, "gx", columns, d) for d in range(1, columns)]
     schur_all, _ = schur(0, subs, HEAD, subs, coupled)
 
-    block = ((HALF, HALF), F32)
-    up, down, basis = call(
-        "first_half", first_kernel, [block, block, ((NC, subs * R), BF16)], [SSPEC] + [VSPEC] * (columns + 2)
+    half, pieces = ((NC, HALF), F32), ((PIECE, HALF), F32)
+    tile, basis = call(
+        "first", first_kernel, [half, ((NC, subs * R), BF16)], [SSPEC] + [VSPEC] * (columns + 2)
     )(partner, primal, *in_vmem(stiff, *others, schur_all))
-    other_up, other_down = swap(up, "gy", line, 1), swap(down, "gy", line, 1)
+    tile = swap(tile, "gy", line, 1)
     image, up = call(
-        "upper", upper_kernel, [((subs * R, HALF), BF16), block], [VSPEC] * 2
+        "second",
+        second_kernel,
+        [((subs * R, HALF), BF16), ((HALF, HALF), F32)],
+        [VSPEC] * 2,
     )(*in_vmem(schur_all, basis))
-    pieces = ((PIECE, HALF), F32)
-    pair = call("pair", pair_kernel, [pieces] * (HALF // PIECE), [VSPEC] * 2)
-    upper = pair(*in_vmem(up, other_up))
-    (down,) = call("lower", lower_kernel, [block], [VSPEC] * 2)(*in_vmem(basis, image))
-    lower = pair(*in_vmem(down, other_down))
+    own = call("pieces", pieces_kernel, [pieces] * (NC // PIECE), [VSPEC] * 4)(
+        *in_vmem(basis, image, up, tile)
+    )
+    own = list(own)
 
     add = call("add", add_kernel, [pieces], [VSPEC] * 2)
     steps = [2 << b for b in range((line // 2 - 1).bit_length())]
-    own = [*upper, *lower]
     for step in range(len(steps)):
         for d in range(len(own)):
             bit = steps[step] if d % 2 == 0 else steps[-1 - step]

time: 38.7 us -> 38.3 us (0.990)
  waiting for transfers between devices: 6.82 us -> 6.37 us
    ppermute x17 -> x16, waiting for transfers between devices: 6.82 us -> 6.37 us  [swap(): return lax.ppermute(a, axis, [(i, i ^ bit) for i in range(size)])]
    pallas_call x5 -> x3, Pallas kernels: 5.79 us -> 5.74 us  [the longest x1 2.97 us: per_device(): call('first', first_kernel, [half, ((NC, subs * R), BF16)], [SSPEC] + [VS...]
    ppermute x17 -> x16, starting transfers between devices: 16.7 us -> 16.7 us  [swap(): return lax.ppermute(a, axis, [(i, i ^ bit) for i in range(size)])]
  transfers between devices with their start and end apart: 17 -> 16, of which waited for: 8 -> 7; matrix products, arithmetic and copies ran while one was open for 0% -> 0% of each run, Pallas kernels for 22% -> 20%
where the time goes in v5:
time: 38.3 us; the launch traced here: 38.1 us
  starting transfers between devices  16.7 us (44%)
  Pallas kernels  14.8 us (39%)
  waiting for transfers between devices  6.37 us (17%)
    ppermute x16, starting transfers between devices, swap(): return lax.ppermute(a, axis, [(i, i ^ bit) for i in range(size)])  16.7 us
    ppermute x16, waiting for transfers between devices, swap(): return lax.ppermute(a, axis, [(i, i ^ bit) for i in range(size)])  6.37 us
    pallas_call x1, Pallas kernels, schur(): call('schur', functools.partial(schur_kernel, first, last, here, stop), [...  5.5 us
    pallas_call x1, Pallas kernels, per_device(): call('first', first_kernel, [half, ((NC, subs * R), BF16)], [SSPEC] + [VS...  2.97 us
    pallas_call x1, Pallas kernels, per_device(): call('diag', diag_kernel, [((subs, R), F32), coupled_shape], [ASPEC, ASPE...  2.09 us
    pallas_call x1, Pallas kernels, per_device(): call('second', second_kernel, [((subs * R, HALF), BF16), ((HALF, HALF), F...  2.07 us
    pallas_call x1, Pallas kernels, per_device(): pl.pallas_call(scale_kernel, out_shape=jax.ShapeDtypeStruct((NC, NC), F32...  1.38 us
  transfers between devices with their start and end apart: 16, of which 7 were waited for; matrix products, arithmetic and copies ran while one was open for 0% of the time, Pallas kernels for 20%

profile of v5, /device:TPU:0, one launch (start us, length us, event | category | flops | bytes accessed | tf_op | source)
XLA Modules:
  0.0 38.1 jit_solution(4531262701172878796)
XLA Ops:
  0.0 2.1 %diag.1 = (f32[8,512]{1,0:T(8,128)S(1)}, bf16[8,1024,512]{2,1,0:T(8,128)(2,1)S(1)}) custom-call(bf16[8,512,512]{2,1,0:T(8,128)(2,1)} %bitcast.5, bf16[8,1024,512]{2,1,0:T(8,128)(2,1)} %bitcast.9), custom_call_target="tpu_custom_call" | custom-call | tf_op jit(solution)/shard_map/diag/pallas_call | solution.py:218
  2.1 3.1 %collective-permute-start = (f32[8,512]{1,0:T(8,128)S(1)}, f32[8,512]{1,0:T(8,128)S(1)}, u32[]{:S(2)}, u32[]{:S(2)}) collective-permute-start(f32[8,512]{1,0:T(8,128)S(1)} %get-tuple-element.16.stiff_ref), channel_id=1, source_target_pairs={{0,8},{8,0},{16,24},{24,16},{1,9},{9,1},{17,25},{25,17},{2,10},{10... | collective-permute-start | bytes 49160 | tf_op jit(solution)/shard_map/ppermute | solution.py:216
  5.2 2.6 %collective-permute-start.1 = (f32[8,512]{1,0:T(8,128)S(1)}, f32[8,512]{1,0:T(8,128)S(1)}, u32[]{:S(2)}, u32[]{:S(2)}) collective-permute-start(f32[8,512]{1,0:T(8,128)S(1)} %get-tuple-element.16.stiff_ref), channel_id=1, source_target_pairs={{0,16},{8,24},{16,0},{24,8},{1,17},{9,25},{17,1},{25,9},{2,18},{10... | collective-permute-start | bytes 49160 | tf_op jit(solution)/shard_map/ppermute | solution.py:216
  7.8 0.0 copy-start.1
  7.8 0.0 copy-start.2
  7.8 5.5 %schur.1 = (bf16[8,512,512]{2,1,0:T(8,128)(2,1)S(1)}, bf16[8,1024,512]{2,1,0:T(8,128)(2,1)S(1)}) custom-call(s32[8]{0:T(128)S(1)} %bitcast.8, bf16[8,1024,512]{2,1,0:T(8,128)(2,1)} %bitcast.10, bf16[8,1024,512]{2,1,0:T(8,128)(2,1)S(1)} %get-tuple-element.17._, bf16[8,512,512]{2,1,0:T(8,128)(2,1)S(1)} %bitcast.6), custom_call_target="tpu_custom_call", output_to_operand_aliasing={{1}: (2, {})} | custom-call | tf_op jit(solution)/shard_map/schur/pallas_call | solution.py:230
  13.3 0.0 collective-permute-done.refs_0_
  13.3 0.0 collective-permute-done.2.refs_2_
  13.4 3.0 %first.1 = (f32[512,256]{1,0:T(8,128)S(1)}, bf16[512,4096]{1,0:T(8,128)(2,1)S(1)}) custom-call(s32[3,4]{1,0:T(4,128)S(1)} %copy-done.2, s32[8,512]{1,0:T(8,128)S(1)} %bitcast.7, f32[8,512]{1,0:T(8,128)S(1)} %get-tuple-element.16.stiff_ref, f32[8,512]{1,0:T(8,128)S(1)} %collective-permute-done.refs_0_, f32[8,512]{1,0:T(8,128)S(1)} %collective-permute-done.1.refs_1_, ...), custom_call_target="tpu_custom_call" | custom-call | tf_op jit(solution)/shard_map/first/pallas_call | solution.py:243
  16.4 0.1 collective-permute-start.3
  16.4 2.1 %second.1 = (bf16[4096,256]{1,0:T(8,128)(2,1)S(1)}, f32[256,256]{1,0:T(8,128)S(1)}) custom-call(bf16[8,512,512]{2,1,0:T(8,128)(2,1)S(1)} %get-tuple-element.18.refs_3_.schur_ref, bf16[512,4096]{1,0:T(8,128)(2,1)S(1)} %get-tuple-element.19.basis_ref), custom_call_target="tpu_custom_call" | custom-call | tf_op jit(solution)/shard_map/second/pallas_call | solution.py:247
  18.5 0.7 %pieces.1 = (f32[128,256]{1,0:T(8,128)S(1)}, f32[128,256]{1,0:T(8,128)S(1)}, f32[128,256]{1,0:T(8,128)S(1)}, f32[128,256]{1,0:T(8,128)S(1)}) custom-call(bf16[512,4096]{1,0:T(8,128)(2,1)S(1)} %get-tuple-element.19.basis_ref, bf16[4096,256]{1,0:T(8,128)(2,1)S(1)} %get-tuple-element.20.image_ref, f32[256,256]{1,0:T(8,128)S(1)} %get-tuple-element.21.up_ref, ...), custom_call_target="tpu_custom_call" | custom-call | tf_op jit(solution)/shard_map/pieces/pallas_call | solution.py:253
  19.2 1.8 %collective-permute-start.10 = (f32[128,256]{1,0:T(8,128)S(1)}, f32[128,256]{1,0:T(8,128)S(1)}, u32[]{:S(2)}, u32[]{:S(2)}) collective-permute-start(f32[128,256]{1,0:T(8,128)S(1)} %get-tuple-element.26.own_ref), channel_id=1, source_target_pairs={{0,4},{1,5},{2,6},{3,7},{4,0},{5,1},{6,2},{7,3},{8,12},{9,13},{10,... | collective-permute-start | bytes 393224 | tf_op jit(solution)/shard_map/ppermute | solution.py:216
  21.0 1.5 %collective-permute-start.8 = (f32[128,256]{1,0:T(8,128)S(1)}, f32[128,256]{1,0:T(8,128)S(1)}, u32[]{:S(2)}, u32[]{:S(2)}) collective-permute-start(f32[128,256]{1,0:T(8,128)S(1)} %get-tuple-element.25.own_ref), channel_id=1, source_target_pairs={{0,2},{1,3},{2,0},{3,1},{4,6},{5,7},{6,4},{7,5},{8,10},{9,11},{10,... | collective-permute-start | bytes 393224 | tf_op jit(solution)/shard_map/ppermute | solution.py:216
  22.5 0.5 %collective-permute-start.6 = (f32[128,256]{1,0:T(8,128)S(1)}, f32[128,256]{1,0:T(8,128)S(1)}, u32[]{:S(2)}, u32[]{:S(2)}) collective-permute-start(f32[128,256]{1,0:T(8,128)S(1)} %get-tuple-element.24.own_ref), channel_id=1, source_target_pairs={{0,4},{1,5},{2,6},{3,7},{4,0},{5,1},{6,2},{7,3},{8,12},{9,13},{10,... | collective-permute-start | bytes 393224 | tf_op jit(solution)/shard_map/ppermute | solution.py:216
  23.0 0.3 collective-permute-start.4
  23.4 1.9 %collective-permute-done.10.other_ref = f32[128,256]{1,0:T(8,128)S(1)} collective-permute-done((f32[128,256]{1,0:T(8,128)S(1)}, f32[128,256]{1,0:T(8,128)S(1)}, u32[]{:S(2)}, u32[]{:S(2)}) %collective-permute-start.10) | collective-permute-done | bytes 131104 | tf_op jit(solution)/shard_map/ppermute | solution.py:216
  25.3 2.1 %collective-permute-start.11 = (f32[128,256]{1,0:T(8,128)S(1)}, f32[128,256]{1,0:T(8,128)S(1)}, u32[]{:S(2)}, u32[]{:S(2)}) collective-permute-start(f32[128,256]{1,0:T(8,128)S(1)} %add.14.own_ref), channel_id=1, source_target_pairs={{0,2},{1,3},{2,0},{3,1},{4,6},{5,7},{6,4},{7,5},{8,10},{9,11},{10,... | collective-permute-start | bytes 393224 | tf_op jit(solution)/shard_map/ppermute | solution.py:216
  27.4 1.6 %collective-permute-start.9 = (f32[128,256]{1,0:T(8,128)S(1)}, f32[128,256]{1,0:T(8,128)S(1)}, u32[]{:S(2)}, u32[]{:S(2)}) collective-permute-start(f32[128,256]{1,0:T(8,128)S(1)} %add.12.own_ref), channel_id=1, source_target_pairs={{0,4},{1,5},{2,6},{3,7},{4,0},{5,1},{6,2},{7,3},{8,12},{9,13},{10,... | collective-permute-start | bytes 393224 | tf_op jit(solution)/shard_map/ppermute | solution.py:216
  29.0 0.8 %collective-permute-start.7 = (f32[128,256]{1,0:T(8,128)S(1)}, f32[128,256]{1,0:T(8,128)S(1)}, u32[]{:S(2)}, u32[]{:S(2)}) collective-permute-start(f32[128,256]{1,0:T(8,128)S(1)} %add.10.own_ref), channel_id=1, source_target_pairs={{0,2},{1,3},{2,0},{3,1},{4,6},{5,7},{6,4},{7,5},{8,10},{9,11},{10,... | collective-permute-start | bytes 393224 | tf_op jit(solution)/shard_map/ppermute | solution.py:216
  29.8 0.4 %collective-permute-done.4.other_ref = f32[128,256]{1,0:T(8,128)S(1)} collective-permute-done((f32[128,256]{1,0:T(8,128)S(1)}, f32[128,256]{1,0:T(8,128)S(1)}, u32[]{:S(2)}, u32[]{:S(2)}) %collective-permute-start.4) | collective-permute-done | bytes 131104 | tf_op jit(solution)/shard_map/ppermute | solution.py:216
  30.2 1.2 %collective-permute-start.5 = (f32[128,256]{1,0:T(8,128)S(1)}, f32[128,256]{1,0:T(8,128)S(1)}, u32[]{:S(2)}, u32[]{:S(2)}) collective-permute-start(f32[128,256]{1,0:T(8,128)S(1)} %add.8.own_ref), channel_id=1, source_target_pairs={{0,4},{1,5},{2,6},{3,7},{4,0},{5,1},{6,2},{7,3},{8,12},{9,13},{10,... | collective-permute-start | bytes 393224 | tf_op jit(solution)/shard_map/ppermute | solution.py:216
  31.4 1.6 %collective-permute-done.11.other_ref = f32[128,256]{1,0:T(8,128)S(1)} collective-permute-done((f32[128,256]{1,0:T(8,128)S(1)}, f32[128,256]{1,0:T(8,128)S(1)}, u32[]{:S(2)}, u32[]{:S(2)}) %collective-permute-start.11) | collective-permute-done | bytes 131104 | tf_op jit(solution)/shard_map/ppermute | solution.py:216
  33.0 0.1 collective-permute-start.15
  33.1 0.5 %collective-permute-start.14 = (f32[128,256]{1,0:T(8,128)S(1)}, f32[128,256]{1,0:T(8,128)S(1)}, u32[]{:S(2)}, u32[]{:S(2)}) collective-permute-start(f32[128,256]{1,0:T(8,128)S(1)} %add.13.refs_2_), channel_id=1, source_target_pairs={{0,1},{1,0},{2,3},{3,2},{4,5},{5,4},{6,7},{7,6},{8,9},{9,8},{10,11... | collective-permute-start | bytes 393224 | tf_op jit(solution)/shard_map/ppermute | solution.py:216
  33.7 1.4 %collective-permute-done.7.other_ref = f32[128,256]{1,0:T(8,128)S(1)} collective-permute-done((f32[128,256]{1,0:T(8,128)S(1)}, f32[128,256]{1,0:T(8,128)S(1)}, u32[]{:S(2)}, u32[]{:S(2)}) %collective-permute-start.7) | collective-permute-done | bytes 131104 | tf_op jit(solution)/shard_map/ppermute | solution.py:216
  35.1 0.1 collective-permute-start.13
  35.2 0.1 collective-permute-done.5.other_ref
  35.3 0.5 %collective-permute-start.12 = (f32[128,256]{1,0:T(8,128)S(1)}, f32[128,256]{1,0:T(8,128)S(1)}, u32[]{:S(2)}, u32[]{:S(2)}) collective-permute-start(f32[128,256]{1,0:T(8,128)S(1)} %add.9.refs_0_), channel_id=1, source_target_pairs={{0,1},{1,0},{2,3},{3,2},{4,5},{5,4},{6,7},{7,6},{8,9},{9,8},{10,11... | collective-permute-start | bytes 393224 | tf_op jit(solution)/shard_map/ppermute | solution.py:216
  35.7 0.7 %collective-permute-done.13.refs_5_ = f32[128,256]{1,0:T(8,128)S(1)} collective-permute-done((f32[128,256]{1,0:T(8,128)S(1)}, f32[128,256]{1,0:T(8,128)S(1)}, u32[]{:S(2)}, u32[]{:S(2)}) %collective-permute-start.13) | collective-permute-done | bytes 131104 | tf_op jit(solution)/shard_map/ppermute | solution.py:216
  36.5 0.2 collective-permute-done.12.refs_4_
  36.7 1.4 %scale.1 = f32[512,512]{1,0:T(8,128)} custom-call(f32[128,256]{1,0:T(8,128)S(1)} %add.9.refs_0_, f32[128,256]{1,0:T(8,128)S(1)} %add.11.refs_1_, f32[128,256]{1,0:T(8,128)S(1)} %add.13.refs_2_, f32[128,256]{1,0:T(8,128)S(1)} %add.15.refs_3_, f32[128,256]{1,0:T(8,128)S(1)} %collective-permute-done.12.refs_4_, f32[128,256]{1,0:T(8,128)S(1)} %collective-permute-done.13.refs_5_, ...), custom_call_target="tpu_custom_call" | custom-call | tf_op jit(solution)/shard_map/scale/pallas_call | solution.py:265
  (22 shorter events, 0.2 us)
Async XLA Ops:
  0.0 7.8 %copy-start = (bf16[1,8,512,512]{3,2,1,0:T(8,128)(2,1)S(1)}, bf16[1,8,512,512]{3,2,1,0:T(8,128)(2,1)}, u32[]{:S(2)}) copy-start(bf16[1,8,512,512]{3,2,1,0:T(8,128)(2,1)} %param.6) | copy-start | bytes 12582916
  0.0 7.8 %copy-start.3 = (s32[1,8]{1,0:T(1,128)S(1)}, s32[1,8]{1,0:T(1,128)}, u32[]{:S(2)}) copy-start(s32[1,8]{1,0:T(1,128)} %param.7) | copy-start | bytes 100
  2.1 11.2 %collective-permute-start = (f32[8,512]{1,0:T(8,128)S(1)}, f32[8,512]{1,0:T(8,128)S(1)}, u32[]{:S(2)}, u32[]{:S(2)}) collective-permute-start(f32[8,512]{1,0:T(8,128)S(1)} %get-tuple-element.16.stiff_ref), channel_id=1, source_target_pairs={{0,8},{8,0},{16,24},{24,16},{1,9},{9,1},{17,25},{25,17},{2,10},{10... | collective-permute-start | bytes 49160 | tf_op jit(solution)/shard_map/ppermute | solution.py:216
  5.2 8.1 %collective-permute-start.1 = (f32[8,512]{1,0:T(8,128)S(1)}, f32[8,512]{1,0:T(8,128)S(1)}, u32[]{:S(2)}, u32[]{:S(2)}) collective-permute-start(f32[8,512]{1,0:T(8,128)S(1)} %get-tuple-element.16.stiff_ref), channel_id=1, source_target_pairs={{0,16},{8,24},{16,0},{24,8},{1,17},{9,25},{17,1},{25,9},{2,18},{10... | collective-permute-start | bytes 49160 | tf_op jit(solution)/shard_map/ppermute | solution.py:216
  7.8 5.6 %collective-permute-start.2 = (f32[8,512]{1,0:T(8,128)S(1)}, f32[8,512]{1,0:T(8,128)S(1)}, u32[]{:S(2)}, u32[]{:S(2)}) collective-permute-start(f32[8,512]{1,0:T(8,128)S(1)} %get-tuple-element.16.stiff_ref), channel_id=1, source_target_pairs={{0,24},{8,16},{16,8},{24,0},{1,25},{9,17},{17,9},{25,1},{2,26},{10... | collective-permute-start | bytes 49160 | tf_op jit(solution)/shard_map/ppermute | solution.py:216
  7.8 5.6 %copy-start.1 = (s32[1,8,512]{2,1,0:T(8,128)S(1)}, s32[1,8,512]{2,1,0:T(8,128)}, u32[]{:S(2)}) copy-start(s32[1,8,512]{2,1,0:T(8,128)} %param.8) | copy-start | bytes 49156
  7.8 5.6 %copy-start.2 = (s32[3,4]{1,0:T(4,128)S(1)}, s32[3,4]{1,0:T(4,128)}, u32[]{:S(2)}) copy-start(s32[3,4]{1,0:T(4,128)} %partner_ref.1) | copy-start | bytes 148
  16.4 2.2 %collective-permute-start.3 = (f32[512,256]{1,0:T(8,128)S(1)}, f32[512,256]{1,0:T(8,128)S(1)}, u32[]{:S(2)}, u32[]{:S(2)}) collective-permute-start(f32[512,256]{1,0:T(8,128)S(1)} %get-tuple-element.22), channel_id=1, source_target_pairs={{0,1},{1,0},{2,3},{3,2},{4,5},{5,4},{6,7},{7,6},{8,9},{9,8},{10,11... | collective-permute-start | bytes 1572872 | tf_op jit(solution)/shard_map/ppermute | solution.py:216
  19.2 6.0 %collective-permute-start.10 = (f32[128,256]{1,0:T(8,128)S(1)}, f32[128,256]{1,0:T(8,128)S(1)}, u32[]{:S(2)}, u32[]{:S(2)}) collective-permute-start(f32[128,256]{1,0:T(8,128)S(1)} %get-tuple-element.26.own_ref), channel_id=1, source_target_pairs={{0,4},{1,5},{2,6},{3,7},{4,0},{5,1},{6,2},{7,3},{8,12},{9,13},{10,... | collective-permute-start | bytes 393224 | tf_op jit(solution)/shard_map/ppermute | solution.py:216
  21.0 6.4 %collective-permute-start.8 = (f32[128,256]{1,0:T(8,128)S(1)}, f32[128,256]{1,0:T(8,128)S(1)}, u32[]{:S(2)}, u32[]{:S(2)}) collective-permute-start(f32[128,256]{1,0:T(8,128)S(1)} %get-tuple-element.25.own_ref), channel_id=1, source_target_pairs={{0,2},{1,3},{2,0},{3,1},{4,6},{5,7},{6,4},{7,5},{8,10},{9,11},{10,... | collective-permute-start | bytes 393224 | tf_op jit(solution)/shard_map/ppermute | solution.py:216
  22.5 6.5 %collective-permute-start.6 = (f32[128,256]{1,0:T(8,128)S(1)}, f32[128,256]{1,0:T(8,128)S(1)}, u32[]{:S(2)}, u32[]{:S(2)}) collective-permute-start(f32[128,256]{1,0:T(8,128)S(1)} %get-tuple-element.24.own_ref), channel_id=1, source_target_pairs={{0,4},{1,5},{2,6},{3,7},{4,0},{5,1},{6,2},{7,3},{8,12},{9,13},{10,... | collective-permute-start | bytes 393224 | tf_op jit(solution)/shard_map/ppermute | solution.py:216
  23.0 7.1 %collective-permute-start.4 = (f32[128,256]{1,0:T(8,128)S(1)}, f32[128,256]{1,0:T(8,128)S(1)}, u32[]{:S(2)}, u32[]{:S(2)}) collective-permute-start(f32[128,256]{1,0:T(8,128)S(1)} %get-tuple-element.23.own_ref), channel_id=1, source_target_pairs={{0,2},{1,3},{2,0},{3,1},{4,6},{5,7},{6,4},{7,5},{8,10},{9,11},{10,... | collective-permute-start | bytes 393224 | tf_op jit(solution)/shard_map/ppermute | solution.py:216
  25.3 7.7 %collective-permute-start.11 = (f32[128,256]{1,0:T(8,128)S(1)}, f32[128,256]{1,0:T(8,128)S(1)}, u32[]{:S(2)}, u32[]{:S(2)}) collective-permute-start(f32[128,256]{1,0:T(8,128)S(1)} %add.14.own_ref), channel_id=1, source_target_pairs={{0,2},{1,3},{2,0},{3,1},{4,6},{5,7},{6,4},{7,5},{8,10},{9,11},{10,... | collective-permute-start | bytes 393224 | tf_op jit(solution)/shard_map/ppermute | solution.py:216
  27.4 5.7 %collective-permute-start.9 = (f32[128,256]{1,0:T(8,128)S(1)}, f32[128,256]{1,0:T(8,128)S(1)}, u32[]{:S(2)}, u32[]{:S(2)}) collective-permute-start(f32[128,256]{1,0:T(8,128)S(1)} %add.12.own_ref), channel_id=1, source_target_pairs={{0,4},{1,5},{2,6},{3,7},{4,0},{5,1},{6,2},{7,3},{8,12},{9,13},{10,... | collective-permute-start | bytes 393224 | tf_op jit(solution)/shard_map/ppermute | solution.py:216
  29.0 6.0 %collective-permute-start.7 = (f32[128,256]{1,0:T(8,128)S(1)}, f32[128,256]{1,0:T(8,128)S(1)}, u32[]{:S(2)}, u32[]{:S(2)}) collective-permute-start(f32[128,256]{1,0:T(8,128)S(1)} %add.10.own_ref), channel_id=1, source_target_pairs={{0,2},{1,3},{2,0},{3,1},{4,6},{5,7},{6,4},{7,5},{8,10},{9,11},{10,... | collective-permute-start | bytes 393224 | tf_op jit(solution)/shard_map/ppermute | solution.py:216
  30.2 5.1 %collective-permute-start.5 = (f32[128,256]{1,0:T(8,128)S(1)}, f32[128,256]{1,0:T(8,128)S(1)}, u32[]{:S(2)}, u32[]{:S(2)}) collective-permute-start(f32[128,256]{1,0:T(8,128)S(1)} %add.8.own_ref), channel_id=1, source_target_pairs={{0,4},{1,5},{2,6},{3,7},{4,0},{5,1},{6,2},{7,3},{8,12},{9,13},{10,... | collective-permute-start | bytes 393224 | tf_op jit(solution)/shard_map/ppermute | solution.py:216
  33.0 2.7 %collective-permute-start.15 = (f32[128,256]{1,0:T(8,128)S(1)}, f32[128,256]{1,0:T(8,128)S(1)}, u32[]{:S(2)}, u32[]{:S(2)}) collective-permute-start(f32[128,256]{1,0:T(8,128)S(1)} %add.15.refs_3_), channel_id=1, source_target_pairs={{0,1},{1,0},{2,3},{3,2},{4,5},{5,4},{6,7},{7,6},{8,9},{9,8},{10,11... | collective-permute-start | bytes 393224 | tf_op jit(solution)/shard_map/ppermute | solution.py:216
  33.1 2.6 %collective-permute-start.14 = (f32[128,256]{1,0:T(8,128)S(1)}, f32[128,256]{1,0:T(8,128)S(1)}, u32[]{:S(2)}, u32[]{:S(2)}) collective-permute-start(f32[128,256]{1,0:T(8,128)S(1)} %add.13.refs_2_), channel_id=1, source_target_pairs={{0,1},{1,0},{2,3},{3,2},{4,5},{5,4},{6,7},{7,6},{8,9},{9,8},{10,11... | collective-permute-start | bytes 393224 | tf_op jit(solution)/shard_map/ppermute | solution.py:216
  35.1 1.4 %collective-permute-start.13 = (f32[128,256]{1,0:T(8,128)S(1)}, f32[128,256]{1,0:T(8,128)S(1)}, u32[]{:S(2)}, u32[]{:S(2)}) collective-permute-start(f32[128,256]{1,0:T(8,128)S(1)} %add.11.refs_1_), channel_id=1, source_target_pairs={{0,1},{1,0},{2,3},{3,2},{4,5},{5,4},{6,7},{7,6},{8,9},{9,8},{10,11... | collective-permute-start | bytes 393224 | tf_op jit(solution)/shard_map/ppermute | solution.py:216
  35.3 1.5 %collective-permute-start.12 = (f32[128,256]{1,0:T(8,128)S(1)}, f32[128,256]{1,0:T(8,128)S(1)}, u32[]{:S(2)}, u32[]{:S(2)}) collective-permute-start(f32[128,256]{1,0:T(8,128)S(1)} %add.9.refs_0_), channel_id=1, source_target_pairs={{0,1},{1,0},{2,3},{3,2},{4,5},{5,4},{6,7},{7,6},{8,9},{9,8},{10,11... | collective-permute-start | bytes 393224 | tf_op jit(solution)/shard_map/ppermute | solution.py:216

commit v6 on v5

--- a/solution.py
+++ b/solution.py
@@ -169,14 +169,18 @@
     up_ref[...] = jnp.dot(basis_ref[:HALF], image_ref[...], preferred_element_type=F32)
 
 
-def pieces_kernel(basis_ref, image_ref, up_ref, other_ref, *outs):
+def upper_kernel(own_ref, other_ref, token_ref, *outs):
+    for d, out in enumerate(outs):
+        at = slice(d * PIECE, (d + 1) * PIECE)
+        out[...] = own_ref[at] + other_ref[at]
+    token_ref[...] = outs[0][:8, :BLK]
+
+
+def lower_kernel(basis_ref, image_ref, other_ref, _, *outs):
     down = jnp.dot(basis_ref[HALF:], image_ref[...], preferred_element_type=F32)
     for d, out in enumerate(outs):
         at = slice(d * PIECE, (d + 1) * PIECE)
-        if d * PIECE < HALF:
-            out[...] = up_ref[at] + other_ref[at]
-        else:
-            out[...] = down[d * PIECE - HALF : (d + 1) * PIECE - HALF] + other_ref[at]
+        out[...] = down[at] + other_ref[HALF + d * PIECE : HALF + (d + 1) * PIECE]
 
 
 def add_kernel(own_ref, other_ref, out_ref):
@@ -187,24 +191,31 @@
     count = NC // PIECE
     own, other = refs[:count], refs[count : 2 * count]
     out_ref, tile, sems = refs[2 * count :]
-    for pieces, column in ((own, core()), (other, 1 - core())):
-        across = pl.ds(pl.multiple_of(column * HALF, HALF), HALF)
-        for d, piece in enumerate(pieces):
-            tile[d * PIECE : (d + 1) * PIECE, across] = piece[...]
-    mean = jnp.sum(jnp.abs(tile[...]), axis=1, keepdims=True) / NC
-    scale = 1.0 / jnp.sqrt(mean + 1e-06)
-    across = jnp.broadcast_to(scale, (NC, BLK)).T[:1, :]
-
-    def copy(b):
-        at = pl.ds(b * BLK, BLK)
-        return pltpu.make_async_copy(tile.at[at], out_ref.at[at], sems.at[b])
-
-    for b in range(NC // BLK):
-        at = slice(b * BLK, (b + 1) * BLK)
-        tile[at, :] = tile[at, :] * scale[at, :] * across
-        copy(b).start()
-    for b in range(NC // BLK):
-        copy(b).wait()
+
+    def copy(d):
+        at = pl.ds(d * PIECE, PIECE)
+        return pltpu.make_async_copy(tile.at[at], out_ref.at[at], sems.at[d])
+
+    down, across = [], []
+    for d in range(count):
+        total = jnp.abs(own[d][...]) + jnp.abs(other[d][...])
+        mean = jnp.sum(total, axis=1, keepdims=True) / NC
+        scale = jnp.broadcast_to(1.0 / jnp.sqrt(mean + 1e-06), (PIECE, BLK))
+        down.append(scale[:, :1])
+        across.append(scale.T[:1, :])
+    halves = [jnp.concatenate(across[:2], axis=1), jnp.concatenate(across[2:], axis=1)]
+    first = core() == 0
+    mine = jnp.where(first, halves[0], halves[1])
+    theirs = jnp.where(first, halves[1], halves[0])
+    here = pl.ds(pl.multiple_of(core() * HALF, HALF), HALF)
+    there = pl.ds(pl.multiple_of((1 - core()) * HALF, HALF), HALF)
+    for d in range(count):
+        at = slice(d * PIECE, (d + 1) * PIECE)
+        tile[at, here] = own[d][...] * down[d] * mine
+        tile[at, there] = other[d][...] * down[d] * theirs
+        copy(d).start()
+    for d in range(count):
+        copy(d).wait()
 
 
 def per_device(columns, line, coupling, local_block, counts, primal, partner):
@@ -250,10 +261,15 @@
         [((subs * R, HALF), BF16), ((HALF, HALF), F32)],
         [VSPEC] * 2,
     )(*in_vmem(schur_all, basis))
-    own = call("pieces", pieces_kernel, [pieces] * (NC // PIECE), [VSPEC] * 4)(
-        *in_vmem(basis, image, up, tile)
+    count = HALF // PIECE
+    token, *upper = call(
+        "upper", upper_kernel, [((8, BLK), F32)] + [pieces] * count, [VSPEC] * 2
+    )(*in_vmem(up, tile))
+    token = swap(token, "gy", line, 1)
+    lower = call("lower", lower_kernel, [pieces] * count, [VSPEC] * 4)(
+        *in_vmem(basis, image, tile, token)
     )
-    own = list(own)
+    own = [*upper, *lower]
 
     add = call("add", add_kernel, [pieces], [VSPEC] * 2)
     steps = [2 << b for b in range((line // 2 - 1).bit_length())]

time: 38.3 us -> 38 us (level)
  waiting for transfers between devices: 6.37 us -> 5.81 us
    ppermute x16 -> x17, waiting for transfers between devices: 6.37 us -> 5.81 us  [swap(): return lax.ppermute(a, axis, [(i, i ^ bit) for i in range(size)])]
    ppermute x16 -> x17, starting transfers between devices: 16.7 us -> 17 us  [swap(): return lax.ppermute(a, axis, [(i, i ^ bit) for i in range(size)])]
    pallas_call x1 -> x2, Pallas kernels: 0.71 us -> 0.78 us  [the longest x1 0.73 us: per_device(): call('lower', lower_kernel, [pieces] * count, [VSPEC] * 4)]
  transfers between devices with their start and end apart: 16 -> 17, of which waited for: 7 -> 8; matrix products, arithmetic and copies ran while one was open for 0% -> 0% of each run, Pallas kernels for 20% -> 22%
where the time goes in v6:
time: 38 us; the launch traced here: 37.9 us
  starting transfers between devices  17 us (45%)
  Pallas kernels  14.8 us (39%)
  waiting for transfers between devices  5.81 us (15%)
    ppermute x17, starting transfers between devices, swap(): return lax.ppermute(a, axis, [(i, i ^ bit) for i in range(size)])  17 us
    ppermute x17, waiting for transfers between devices, swap(): return lax.ppermute(a, axis, [(i, i ^ bit) for i in range(size)])  5.81 us
    pallas_call x1, Pallas kernels, schur(): call('schur', functools.partial(schur_kernel, first, last, here, stop), [...  5.5 us
    pallas_call x1, Pallas kernels, per_device(): call('first', first_kernel, [half, ((NC, subs * R), BF16)], [SSPEC] + [VS...  2.97 us
    pallas_call x1, Pallas kernels, per_device(): call('diag', diag_kernel, [((subs, R), F32), coupled_shape], [ASPEC, ASPE...  2.09 us
    pallas_call x1, Pallas kernels, per_device(): call('second', second_kernel, [((subs * R, HALF), BF16), ((HALF, HALF), F...  2.07 us
    pallas_call x1, Pallas kernels, per_device(): pl.pallas_call(scale_kernel, out_shape=jax.ShapeDtypeStruct((NC, NC), F32...  1.3 us
  transfers between devices with their start and end apart: 17, of which 8 were waited for; matrix products, arithmetic and copies ran while one was open for 0% of the time, Pallas kernels for 22%

profile of v6, /device:TPU:0, one launch (start us, length us, event | category | flops | bytes accessed | tf_op | source)
XLA Modules:
  0.0 37.9 jit_solution(9752707540725321043)
XLA Ops:
  0.0 2.1 %diag.1 = (f32[8,512]{1,0:T(8,128)S(1)}, bf16[8,1024,512]{2,1,0:T(8,128)(2,1)S(1)}) custom-call(bf16[8,512,512]{2,1,0:T(8,128)(2,1)} %bitcast.5, bf16[8,1024,512]{2,1,0:T(8,128)(2,1)} %bitcast.9), custom_call_target="tpu_custom_call" | custom-call | tf_op jit(solution)/shard_map/diag/pallas_call | solution.py:229
  2.1 3.1 %collective-permute-start = (f32[8,512]{1,0:T(8,128)S(1)}, f32[8,512]{1,0:T(8,128)S(1)}, u32[]{:S(2)}, u32[]{:S(2)}) collective-permute-start(f32[8,512]{1,0:T(8,128)S(1)} %get-tuple-element.19.stiff_ref), channel_id=1, source_target_pairs={{0,8},{8,0},{16,24},{24,16},{1,9},{9,1},{17,25},{25,17},{2,10},{10... | collective-permute-start | bytes 49160 | tf_op jit(solution)/shard_map/ppermute | solution.py:227
  5.2 2.6 %collective-permute-start.1 = (f32[8,512]{1,0:T(8,128)S(1)}, f32[8,512]{1,0:T(8,128)S(1)}, u32[]{:S(2)}, u32[]{:S(2)}) collective-permute-start(f32[8,512]{1,0:T(8,128)S(1)} %get-tuple-element.19.stiff_ref), channel_id=1, source_target_pairs={{0,16},{8,24},{16,0},{24,8},{1,17},{9,25},{17,1},{25,9},{2,18},{10... | collective-permute-start | bytes 49160 | tf_op jit(solution)/shard_map/ppermute | solution.py:227
  7.8 0.0 copy-start.1
  7.8 0.0 copy-start.2
  7.8 5.5 %schur.1 = (bf16[8,512,512]{2,1,0:T(8,128)(2,1)S(1)}, bf16[8,1024,512]{2,1,0:T(8,128)(2,1)S(1)}) custom-call(s32[8]{0:T(128)S(1)} %bitcast.8, bf16[8,1024,512]{2,1,0:T(8,128)(2,1)} %bitcast.10, bf16[8,1024,512]{2,1,0:T(8,128)(2,1)S(1)} %get-tuple-element.17._, bf16[8,512,512]{2,1,0:T(8,128)(2,1)S(1)} %bitcast.6), custom_call_target="tpu_custom_call", output_to_operand_aliasing={{1}: (2, {})} | custom-call | tf_op jit(solution)/shard_map/schur/pallas_call | solution.py:241
  13.4 3.0 %first.1 = (f32[512,256]{1,0:T(8,128)S(1)}, bf16[512,4096]{1,0:T(8,128)(2,1)S(1)}) custom-call(s32[3,4]{1,0:T(4,128)S(1)} %copy-done.2, s32[8,512]{1,0:T(8,128)S(1)} %bitcast.7, f32[8,512]{1,0:T(8,128)S(1)} %get-tuple-element.19.stiff_ref, f32[8,512]{1,0:T(8,128)S(1)} %collective-permute-done.refs_0_, f32[8,512]{1,0:T(8,128)S(1)} %collective-permute-done.1.refs_1_, ...), custom_call_target="tpu_custom_call" | custom-call | tf_op jit(solution)/shard_map/first/pallas_call | solution.py:254
  16.4 0.1 collective-permute-start.3
  16.4 2.1 %second.1 = (bf16[4096,256]{1,0:T(8,128)(2,1)S(1)}, f32[256,256]{1,0:T(8,128)S(1)}) custom-call(bf16[8,512,512]{2,1,0:T(8,128)(2,1)S(1)} %get-tuple-element.18.refs_3_.schur_ref, bf16[512,4096]{1,0:T(8,128)(2,1)S(1)} %get-tuple-element.20.basis_ref), custom_call_target="tpu_custom_call" | custom-call | tf_op jit(solution)/shard_map/second/pallas_call | solution.py:258
  18.6 0.6 %collective-permute-start.8 = (f32[8,128]{1,0:T(8,128)S(1)}, f32[8,128]{1,0:T(8,128)S(1)}, u32[]{:S(2)}, u32[]{:S(2)}) collective-permute-start(f32[8,128]{1,0:T(8,128)S(1)} %get-tuple-element.26), channel_id=1, source_target_pairs={{0,1},{1,0},{2,3},{3,2},{4,5},{5,4},{6,7},{7,6},{8,9},{9,8},{10,11... | collective-permute-start | bytes 12296 | tf_op jit(solution)/shard_map/ppermute | solution.py:227
  19.1 1.7 %collective-permute-start.6 = (f32[128,256]{1,0:T(8,128)S(1)}, f32[128,256]{1,0:T(8,128)S(1)}, u32[]{:S(2)}, u32[]{:S(2)}) collective-permute-start(f32[128,256]{1,0:T(8,128)S(1)} %get-tuple-element.24.own_ref), channel_id=1, source_target_pairs={{0,4},{1,5},{2,6},{3,7},{4,0},{5,1},{6,2},{7,3},{8,12},{9,13},{10,... | collective-permute-start | bytes 393224 | tf_op jit(solution)/shard_map/ppermute | solution.py:227
  20.8 1.5 %collective-permute-start.4 = (f32[128,256]{1,0:T(8,128)S(1)}, f32[128,256]{1,0:T(8,128)S(1)}, u32[]{:S(2)}, u32[]{:S(2)}) collective-permute-start(f32[128,256]{1,0:T(8,128)S(1)} %get-tuple-element.23.own_ref), channel_id=1, source_target_pairs={{0,2},{1,3},{2,0},{3,1},{4,6},{5,7},{6,4},{7,5},{8,10},{9,11},{10,... | collective-permute-start | bytes 393224 | tf_op jit(solution)/shard_map/ppermute | solution.py:227
  22.3 0.7 %lower.1 = (f32[128,256]{1,0:T(8,128)S(1)}, f32[128,256]{1,0:T(8,128)S(1)}) custom-call(bf16[512,4096]{1,0:T(8,128)(2,1)S(1)} %get-tuple-element.20.basis_ref, bf16[4096,256]{1,0:T(8,128)(2,1)S(1)} %get-tuple-element.25.image_ref, f32[512,256]{1,0:T(8,128)S(1)} %collective-permute-done.3.other_ref, f32[8,128]{1,0:T(8,128)S(1)} %collective-permute-done.8._), custom_call_target="tpu_custom_call" | custom-call | tf_op jit(solution)/shard_map/lower/pallas_call | solution.py:269
  23.1 0.6 %collective-permute-start.11 = (f32[128,256]{1,0:T(8,128)S(1)}, f32[128,256]{1,0:T(8,128)S(1)}, u32[]{:S(2)}, u32[]{:S(2)}) collective-permute-start(f32[128,256]{1,0:T(8,128)S(1)} %get-tuple-element.28.own_ref), channel_id=1, source_target_pairs={{0,4},{1,5},{2,6},{3,7},{4,0},{5,1},{6,2},{7,3},{8,12},{9,13},{10,... | collective-permute-start | bytes 393224 | tf_op jit(solution)/shard_map/ppermute | solution.py:227
  23.7 0.3 collective-permute-start.9
  24.0 0.6 %collective-permute-done.6.other_ref = f32[128,256]{1,0:T(8,128)S(1)} collective-permute-done((f32[128,256]{1,0:T(8,128)S(1)}, f32[128,256]{1,0:T(8,128)S(1)}, u32[]{:S(2)}, u32[]{:S(2)}) %collective-permute-start.6) | collective-permute-done | bytes 131104 | tf_op jit(solution)/shard_map/ppermute | solution.py:227
  24.6 2.2 %collective-permute-start.7 = (f32[128,256]{1,0:T(8,128)S(1)}, f32[128,256]{1,0:T(8,128)S(1)}, u32[]{:S(2)}, u32[]{:S(2)}) collective-permute-start(f32[128,256]{1,0:T(8,128)S(1)} %add.10.own_ref), channel_id=1, source_target_pairs={{0,2},{1,3},{2,0},{3,1},{4,6},{5,7},{6,4},{7,5},{8,10},{9,11},{10,... | collective-permute-start | bytes 393224 | tf_op jit(solution)/shard_map/ppermute | solution.py:227
  26.9 2.0 %collective-permute-start.5 = (f32[128,256]{1,0:T(8,128)S(1)}, f32[128,256]{1,0:T(8,128)S(1)}, u32[]{:S(2)}, u32[]{:S(2)}) collective-permute-start(f32[128,256]{1,0:T(8,128)S(1)} %add.8.own_ref), channel_id=1, source_target_pairs={{0,4},{1,5},{2,6},{3,7},{4,0},{5,1},{6,2},{7,3},{8,12},{9,13},{10,... | collective-permute-start | bytes 393224 | tf_op jit(solution)/shard_map/ppermute | solution.py:227
  28.9 0.3 collective-permute-start.12
  29.2 0.9 %collective-permute-done.9.other_ref = f32[128,256]{1,0:T(8,128)S(1)} collective-permute-done((f32[128,256]{1,0:T(8,128)S(1)}, f32[128,256]{1,0:T(8,128)S(1)}, u32[]{:S(2)}, u32[]{:S(2)}) %collective-permute-start.9) | collective-permute-done | bytes 131104 | tf_op jit(solution)/shard_map/ppermute | solution.py:227
  30.1 1.4 %collective-permute-start.10 = (f32[128,256]{1,0:T(8,128)S(1)}, f32[128,256]{1,0:T(8,128)S(1)}, u32[]{:S(2)}, u32[]{:S(2)}) collective-permute-start(f32[128,256]{1,0:T(8,128)S(1)} %add.12.own_ref), channel_id=1, source_target_pairs={{0,4},{1,5},{2,6},{3,7},{4,0},{5,1},{6,2},{7,3},{8,12},{9,13},{10,... | collective-permute-start | bytes 393224 | tf_op jit(solution)/shard_map/ppermute | solution.py:227
  31.5 1.4 %collective-permute-done.7.other_ref = f32[128,256]{1,0:T(8,128)S(1)} collective-permute-done((f32[128,256]{1,0:T(8,128)S(1)}, f32[128,256]{1,0:T(8,128)S(1)}, u32[]{:S(2)}, u32[]{:S(2)}) %collective-permute-start.7) | collective-permute-done | bytes 131104 | tf_op jit(solution)/shard_map/ppermute | solution.py:227
  32.9 0.1 collective-permute-start.14
  33.0 0.1 collective-permute-done.5.other_ref
  33.1 0.5 %collective-permute-start.13 = (f32[128,256]{1,0:T(8,128)S(1)}, f32[128,256]{1,0:T(8,128)S(1)}, u32[]{:S(2)}, u32[]{:S(2)}) collective-permute-start(f32[128,256]{1,0:T(8,128)S(1)} %add.9.refs_0_), channel_id=1, source_target_pairs={{0,1},{1,0},{2,3},{3,2},{4,5},{5,4},{6,7},{7,6},{8,9},{9,8},{10,11... | collective-permute-start | bytes 393224 | tf_op jit(solution)/shard_map/ppermute | solution.py:227
  33.6 0.9 %collective-permute-done.12.other_ref = f32[128,256]{1,0:T(8,128)S(1)} collective-permute-done((f32[128,256]{1,0:T(8,128)S(1)}, f32[128,256]{1,0:T(8,128)S(1)}, u32[]{:S(2)}, u32[]{:S(2)}) %collective-permute-start.12) | collective-permute-done | bytes 131104 | tf_op jit(solution)/shard_map/ppermute | solution.py:227
  34.5 0.1 collective-permute-start.16
  34.6 0.6 %collective-permute-done.10.other_ref = f32[128,256]{1,0:T(8,128)S(1)} collective-permute-done((f32[128,256]{1,0:T(8,128)S(1)}, f32[128,256]{1,0:T(8,128)S(1)}, u32[]{:S(2)}, u32[]{:S(2)}) %collective-permute-start.10) | collective-permute-done | bytes 131104 | tf_op jit(solution)/shard_map/ppermute | solution.py:227
  35.2 0.1 collective-permute-start.15
  35.3 0.6 %collective-permute-done.16.refs_7_ = f32[128,256]{1,0:T(8,128)S(1)} collective-permute-done((f32[128,256]{1,0:T(8,128)S(1)}, f32[128,256]{1,0:T(8,128)S(1)}, u32[]{:S(2)}, u32[]{:S(2)}) %collective-permute-start.16) | collective-permute-done | bytes 131104 | tf_op jit(solution)/shard_map/ppermute | solution.py:227
  35.9 0.7 %collective-permute-done.15.refs_6_ = f32[128,256]{1,0:T(8,128)S(1)} collective-permute-done((f32[128,256]{1,0:T(8,128)S(1)}, f32[128,256]{1,0:T(8,128)S(1)}, u32[]{:S(2)}, u32[]{:S(2)}) %collective-permute-start.15) | collective-permute-done | bytes 131104 | tf_op jit(solution)/shard_map/ppermute | solution.py:227
  36.6 1.3 %scale.1 = f32[512,512]{1,0:T(8,128)} custom-call(f32[128,256]{1,0:T(8,128)S(1)} %add.9.refs_0_, f32[128,256]{1,0:T(8,128)S(1)} %add.11.refs_1_, f32[128,256]{1,0:T(8,128)S(1)} %add.13.refs_2_, f32[128,256]{1,0:T(8,128)S(1)} %add.15.refs_3_, f32[128,256]{1,0:T(8,128)S(1)} %collective-permute-done.13.refs_4_, f32[128,256]{1,0:T(8,128)S(1)} %collective-permute-done.14.refs_5_, ...), custom_call_target="tpu_custom_call" | custom-call | tf_op jit(solution)/shard_map/scale/pallas_call | solution.py:281
  (25 shorter events, 0.2 us)
Async XLA Ops:
  0.0 7.8 %copy-start = (bf16[1,8,512,512]{3,2,1,0:T(8,128)(2,1)S(1)}, bf16[1,8,512,512]{3,2,1,0:T(8,128)(2,1)}, u32[]{:S(2)}) copy-start(bf16[1,8,512,512]{3,2,1,0:T(8,128)(2,1)} %param.6) | copy-start | bytes 12582916
  0.0 7.8 %copy-start.3 = (s32[1,8]{1,0:T(1,128)S(1)}, s32[1,8]{1,0:T(1,128)}, u32[]{:S(2)}) copy-start(s32[1,8]{1,0:T(1,128)} %param.7) | copy-start | bytes 100
  2.1 11.2 %collective-permute-start = (f32[8,512]{1,0:T(8,128)S(1)}, f32[8,512]{1,0:T(8,128)S(1)}, u32[]{:S(2)}, u32[]{:S(2)}) collective-permute-start(f32[8,512]{1,0:T(8,128)S(1)} %get-tuple-element.19.stiff_ref), channel_id=1, source_target_pairs={{0,8},{8,0},{16,24},{24,16},{1,9},{9,1},{17,25},{25,17},{2,10},{10... | collective-permute-start | bytes 49160 | tf_op jit(solution)/shard_map/ppermute | solution.py:227
  5.2 8.1 %collective-permute-start.1 = (f32[8,512]{1,0:T(8,128)S(1)}, f32[8,512]{1,0:T(8,128)S(1)}, u32[]{:S(2)}, u32[]{:S(2)}) collective-permute-start(f32[8,512]{1,0:T(8,128)S(1)} %get-tuple-element.19.stiff_ref), channel_id=1, source_target_pairs={{0,16},{8,24},{16,0},{24,8},{1,17},{9,25},{17,1},{25,9},{2,18},{10... | collective-permute-start | bytes 49160 | tf_op jit(solution)/shard_map/ppermute | solution.py:227
  7.8 5.6 %collective-permute-start.2 = (f32[8,512]{1,0:T(8,128)S(1)}, f32[8,512]{1,0:T(8,128)S(1)}, u32[]{:S(2)}, u32[]{:S(2)}) collective-permute-start(f32[8,512]{1,0:T(8,128)S(1)} %get-tuple-element.19.stiff_ref), channel_id=1, source_target_pairs={{0,24},{8,16},{16,8},{24,0},{1,25},{9,17},{17,9},{25,1},{2,26},{10... | collective-permute-start | bytes 49160 | tf_op jit(solution)/shard_map/ppermute | solution.py:227
  7.8 5.6 %copy-start.1 = (s32[1,8,512]{2,1,0:T(8,128)S(1)}, s32[1,8,512]{2,1,0:T(8,128)}, u32[]{:S(2)}) copy-start(s32[1,8,512]{2,1,0:T(8,128)} %param.8) | copy-start | bytes 49156
  7.8 5.6 %copy-start.2 = (s32[3,4]{1,0:T(4,128)S(1)}, s32[3,4]{1,0:T(4,128)}, u32[]{:S(2)}) copy-start(s32[3,4]{1,0:T(4,128)} %partner_ref.1) | copy-start | bytes 148
  16.4 2.2 %collective-permute-start.3 = (f32[512,256]{1,0:T(8,128)S(1)}, f32[512,256]{1,0:T(8,128)S(1)}, u32[]{:S(2)}, u32[]{:S(2)}) collective-permute-start(f32[512,256]{1,0:T(8,128)S(1)} %get-tuple-element.22), channel_id=1, source_target_pairs={{0,1},{1,0},{2,3},{3,2},{4,5},{5,4},{6,7},{7,6},{8,9},{9,8},{10,11... | collective-permute-start | bytes 1572872 | tf_op jit(solution)/shard_map/ppermute | solution.py:227
  18.6 3.8 %collective-permute-start.8 = (f32[8,128]{1,0:T(8,128)S(1)}, f32[8,128]{1,0:T(8,128)S(1)}, u32[]{:S(2)}, u32[]{:S(2)}) collective-permute-start(f32[8,128]{1,0:T(8,128)S(1)} %get-tuple-element.26), channel_id=1, source_target_pairs={{0,1},{1,0},{2,3},{3,2},{4,5},{5,4},{6,7},{7,6},{8,9},{9,8},{10,11... | collective-permute-start | bytes 12296 | tf_op jit(solution)/shard_map/ppermute | solution.py:227
  19.1 5.5 %collective-permute-start.6 = (f32[128,256]{1,0:T(8,128)S(1)}, f32[128,256]{1,0:T(8,128)S(1)}, u32[]{:S(2)}, u32[]{:S(2)}) collective-permute-start(f32[128,256]{1,0:T(8,128)S(1)} %get-tuple-element.24.own_ref), channel_id=1, source_target_pairs={{0,4},{1,5},{2,6},{3,7},{4,0},{5,1},{6,2},{7,3},{8,12},{9,13},{10,... | collective-permute-start | bytes 393224 | tf_op jit(solution)/shard_map/ppermute | solution.py:227
  20.8 6.0 %collective-permute-start.4 = (f32[128,256]{1,0:T(8,128)S(1)}, f32[128,256]{1,0:T(8,128)S(1)}, u32[]{:S(2)}, u32[]{:S(2)}) collective-permute-start(f32[128,256]{1,0:T(8,128)S(1)} %get-tuple-element.23.own_ref), channel_id=1, source_target_pairs={{0,2},{1,3},{2,0},{3,1},{4,6},{5,7},{6,4},{7,5},{8,10},{9,11},{10,... | collective-permute-start | bytes 393224 | tf_op jit(solution)/shard_map/ppermute | solution.py:227
  23.1 5.8 %collective-permute-start.11 = (f32[128,256]{1,0:T(8,128)S(1)}, f32[128,256]{1,0:T(8,128)S(1)}, u32[]{:S(2)}, u32[]{:S(2)}) collective-permute-start(f32[128,256]{1,0:T(8,128)S(1)} %get-tuple-element.28.own_ref), channel_id=1, source_target_pairs={{0,4},{1,5},{2,6},{3,7},{4,0},{5,1},{6,2},{7,3},{8,12},{9,13},{10,... | collective-permute-start | bytes 393224 | tf_op jit(solution)/shard_map/ppermute | solution.py:227
  23.7 6.4 %collective-permute-start.9 = (f32[128,256]{1,0:T(8,128)S(1)}, f32[128,256]{1,0:T(8,128)S(1)}, u32[]{:S(2)}, u32[]{:S(2)}) collective-permute-start(f32[128,256]{1,0:T(8,128)S(1)} %get-tuple-element.27.own_ref), channel_id=1, source_target_pairs={{0,2},{1,3},{2,0},{3,1},{4,6},{5,7},{6,4},{7,5},{8,10},{9,11},{10,... | collective-permute-start | bytes 393224 | tf_op jit(solution)/shard_map/ppermute | solution.py:227
  24.6 8.3 %collective-permute-start.7 = (f32[128,256]{1,0:T(8,128)S(1)}, f32[128,256]{1,0:T(8,128)S(1)}, u32[]{:S(2)}, u32[]{:S(2)}) collective-permute-start(f32[128,256]{1,0:T(8,128)S(1)} %add.10.own_ref), channel_id=1, source_target_pairs={{0,2},{1,3},{2,0},{3,1},{4,6},{5,7},{6,4},{7,5},{8,10},{9,11},{10,... | collective-permute-start | bytes 393224 | tf_op jit(solution)/shard_map/ppermute | solution.py:227
  26.9 6.2 %collective-permute-start.5 = (f32[128,256]{1,0:T(8,128)S(1)}, f32[128,256]{1,0:T(8,128)S(1)}, u32[]{:S(2)}, u32[]{:S(2)}) collective-permute-start(f32[128,256]{1,0:T(8,128)S(1)} %add.8.own_ref), channel_id=1, source_target_pairs={{0,4},{1,5},{2,6},{3,7},{4,0},{5,1},{6,2},{7,3},{8,12},{9,13},{10,... | collective-permute-start | bytes 393224 | tf_op jit(solution)/shard_map/ppermute | solution.py:227
  28.9 5.6 %collective-permute-start.12 = (f32[128,256]{1,0:T(8,128)S(1)}, f32[128,256]{1,0:T(8,128)S(1)}, u32[]{:S(2)}, u32[]{:S(2)}) collective-permute-start(f32[128,256]{1,0:T(8,128)S(1)} %add.14.own_ref), channel_id=1, source_target_pairs={{0,2},{1,3},{2,0},{3,1},{4,6},{5,7},{6,4},{7,5},{8,10},{9,11},{10,... | collective-permute-start | bytes 393224 | tf_op jit(solution)/shard_map/ppermute | solution.py:227
  30.1 5.0 %collective-permute-start.10 = (f32[128,256]{1,0:T(8,128)S(1)}, f32[128,256]{1,0:T(8,128)S(1)}, u32[]{:S(2)}, u32[]{:S(2)}) collective-permute-start(f32[128,256]{1,0:T(8,128)S(1)} %add.12.own_ref), channel_id=1, source_target_pairs={{0,4},{1,5},{2,6},{3,7},{4,0},{5,1},{6,2},{7,3},{8,12},{9,13},{10,... | collective-permute-start | bytes 393224 | tf_op jit(solution)/shard_map/ppermute | solution.py:227
  32.9 2.3 %collective-permute-start.14 = (f32[128,256]{1,0:T(8,128)S(1)}, f32[128,256]{1,0:T(8,128)S(1)}, u32[]{:S(2)}, u32[]{:S(2)}) collective-permute-start(f32[128,256]{1,0:T(8,128)S(1)} %add.11.refs_1_), channel_id=1, source_target_pairs={{0,1},{1,0},{2,3},{3,2},{4,5},{5,4},{6,7},{7,6},{8,9},{9,8},{10,11... | collective-permute-start | bytes 393224 | tf_op jit(solution)/shard_map/ppermute | solution.py:227
  33.1 2.2 %collective-permute-start.13 = (f32[128,256]{1,0:T(8,128)S(1)}, f32[128,256]{1,0:T(8,128)S(1)}, u32[]{:S(2)}, u32[]{:S(2)}) collective-permute-start(f32[128,256]{1,0:T(8,128)S(1)} %add.9.refs_0_), channel_id=1, source_target_pairs={{0,1},{1,0},{2,3},{3,2},{4,5},{5,4},{6,7},{7,6},{8,9},{9,8},{10,11... | collective-permute-start | bytes 393224 | tf_op jit(solution)/shard_map/ppermute | solution.py:227
  34.5 1.4 %collective-permute-start.16 = (f32[128,256]{1,0:T(8,128)S(1)}, f32[128,256]{1,0:T(8,128)S(1)}, u32[]{:S(2)}, u32[]{:S(2)}) collective-permute-start(f32[128,256]{1,0:T(8,128)S(1)} %add.15.refs_3_), channel_id=1, source_target_pairs={{0,1},{1,0},{2,3},{3,2},{4,5},{5,4},{6,7},{7,6},{8,9},{9,8},{10,11... | collective-permute-start | bytes 393224 | tf_op jit(solution)/shard_map/ppermute | solution.py:227
  35.2 1.4 %collective-permute-start.15 = (f32[128,256]{1,0:T(8,128)S(1)}, f32[128,256]{1,0:T(8,128)S(1)}, u32[]{:S(2)}, u32[]{:S(2)}) collective-permute-start(f32[128,256]{1,0:T(8,128)S(1)} %add.13.refs_2_), channel_id=1, source_target_pairs={{0,1},{1,0},{2,3},{3,2},{4,5},{5,4},{6,7},{7,6},{8,9},{9,8},{10,11... | collective-permute-start | bytes 393224 | tf_op jit(solution)/shard_map/ppermute | solution.py:227

commit v7 on v6

--- a/solution.py
+++ b/solution.py
@@ -93,15 +93,24 @@
 
 
 def schur_kernel(first, last, here, stop, counts_ref, coupling_ref, _, block_ref, schur_ref, coupled_ref, sems):
-    def copy(j):
-        return pltpu.make_async_copy(coupling_ref.at[j], coupled_ref.at[j], sems.at[j - here])
+    def each(j, act):
+        for live in range(1, RB + 1):
+
+            @pl.when(counts_ref[j] == live)
+            def _():
+                part = pl.ds(0, live * BLK)
+                act(
+                    pltpu.make_async_copy(
+                        coupling_ref.at[j, :, part], coupled_ref.at[j, :, part], sems.at[j - here]
+                    )
+                )
 
     def start(j, carry):
-        copy(j).start()
+        each(j, lambda copy: copy.start())
         return carry
 
     def wait(j, carry):
-        copy(j).wait()
+        each(j, lambda copy: copy.wait())
         return carry
 
     def pair(p, carry):
@@ -109,8 +118,8 @@
         if last > here:
             @pl.when(j >= here)
             def _():
-                copy(j).wait()
-                copy(j + 1).wait()
+                wait(j, 0)
+                wait(j + 1, 0)
 
         for k in range(2):
             schur_block(counts_ref[j + k], coupled_ref.at[j + k], block_ref.at[j + k], schur_ref.at[j + k - first])

time: 38 us -> 37.9 us (level)
  transfers between devices with their start and end apart: 17 -> 17, of which waited for: 8 -> 9; matrix products, arithmetic and copies ran while one was open for 0% -> 0% of each run, Pallas kernels for 22% -> 22%
where the time goes in v7:
time: 37.9 us; the launch traced here: 37.8 us
  starting transfers between devices  16.9 us (45%)
  Pallas kernels  14.7 us (39%)
  waiting for transfers between devices  6 us (16%)
    ppermute x17, starting transfers between devices, swap(): return lax.ppermute(a, axis, [(i, i ^ bit) for i in range(size)])  16.9 us
    ppermute x17, waiting for transfers between devices, swap(): return lax.ppermute(a, axis, [(i, i ^ bit) for i in range(size)])  6 us
    pallas_call x1, Pallas kernels, schur(): call('schur', functools.partial(schur_kernel, first, last, here, stop), [...  5.42 us
    pallas_call x1, Pallas kernels, per_device(): call('first', first_kernel, [half, ((NC, subs * R), BF16)], [SSPEC] + [VS...  2.96 us
    pallas_call x1, Pallas kernels, per_device(): call('diag', diag_kernel, [((subs, R), F32), coupled_shape], [ASPEC, ASPE...  2.09 us
    pallas_call x1, Pallas kernels, per_device(): call('second', second_kernel, [((subs * R, HALF), BF16), ((HALF, HALF), F...  2.08 us
    pallas_call x1, Pallas kernels, per_device(): pl.pallas_call(scale_kernel, out_shape=jax.ShapeDtypeStruct((NC, NC), F32...  1.3 us
  transfers between devices with their start and end apart: 17, of which 9 were waited for; matrix products, arithmetic and copies ran while one was open for 0% of the time, Pallas kernels for 22%

profile of v7, /device:TPU:0, one launch (start us, length us, event | category | flops | bytes accessed | tf_op | source)
XLA Modules:
  0.0 37.8 jit_solution(4828291041783198099)
XLA Ops:
  0.0 2.1 %diag.1 = (f32[8,512]{1,0:T(8,128)S(1)}, bf16[8,1024,512]{2,1,0:T(8,128)(2,1)S(1)}) custom-call(bf16[8,512,512]{2,1,0:T(8,128)(2,1)} %bitcast.5, bf16[8,1024,512]{2,1,0:T(8,128)(2,1)} %bitcast.9), custom_call_target="tpu_custom_call" | custom-call | tf_op jit(solution)/shard_map/diag/pallas_call | solution.py:238
  2.1 3.1 %collective-permute-start = (f32[8,512]{1,0:T(8,128)S(1)}, f32[8,512]{1,0:T(8,128)S(1)}, u32[]{:S(2)}, u32[]{:S(2)}) collective-permute-start(f32[8,512]{1,0:T(8,128)S(1)} %get-tuple-element.19.stiff_ref), channel_id=1, source_target_pairs={{0,8},{8,0},{16,24},{24,16},{1,9},{9,1},{17,25},{25,17},{2,10},{10... | collective-permute-start | bytes 49160 | tf_op jit(solution)/shard_map/ppermute | solution.py:236
  5.2 2.6 %collective-permute-start.1 = (f32[8,512]{1,0:T(8,128)S(1)}, f32[8,512]{1,0:T(8,128)S(1)}, u32[]{:S(2)}, u32[]{:S(2)}) collective-permute-start(f32[8,512]{1,0:T(8,128)S(1)} %get-tuple-element.19.stiff_ref), channel_id=1, source_target_pairs={{0,16},{8,24},{16,0},{24,8},{1,17},{9,25},{17,1},{25,9},{2,18},{10... | collective-permute-start | bytes 49160 | tf_op jit(solution)/shard_map/ppermute | solution.py:236
  7.8 0.0 copy-start.1
  7.8 5.4 %schur.1 = (bf16[8,512,512]{2,1,0:T(8,128)(2,1)S(1)}, bf16[8,1024,512]{2,1,0:T(8,128)(2,1)S(1)}) custom-call(s32[8]{0:T(128)S(1)} %bitcast.8, bf16[8,1024,512]{2,1,0:T(8,128)(2,1)} %bitcast.10, bf16[8,1024,512]{2,1,0:T(8,128)(2,1)S(1)} %get-tuple-element.17._, bf16[8,512,512]{2,1,0:T(8,128)(2,1)S(1)} %bitcast.6), custom_call_target="tpu_custom_call", output_to_operand_aliasing={{1}: (2, {})} | custom-call | tf_op jit(solution)/shard_map/schur/pallas_call | solution.py:250
  13.3 0.1 collective-permute-done.2.refs_2_
  13.3 3.0 %first.1 = (f32[512,256]{1,0:T(8,128)S(1)}, bf16[512,4096]{1,0:T(8,128)(2,1)S(1)}) custom-call(s32[3,4]{1,0:T(4,128)S(1)} %copy-done.2, s32[8,512]{1,0:T(8,128)S(1)} %bitcast.7, f32[8,512]{1,0:T(8,128)S(1)} %get-tuple-element.19.stiff_ref, f32[8,512]{1,0:T(8,128)S(1)} %collective-permute-done.refs_0_, f32[8,512]{1,0:T(8,128)S(1)} %collective-permute-done.1.refs_1_, ...), custom_call_target="tpu_custom_call" | custom-call | tf_op jit(solution)/shard_map/first/pallas_call | solution.py:263
  16.3 0.1 collective-permute-start.3
  16.4 2.1 %second.1 = (bf16[4096,256]{1,0:T(8,128)(2,1)S(1)}, f32[256,256]{1,0:T(8,128)S(1)}) custom-call(bf16[8,512,512]{2,1,0:T(8,128)(2,1)S(1)} %get-tuple-element.18.refs_3_.schur_ref, bf16[512,4096]{1,0:T(8,128)(2,1)S(1)} %get-tuple-element.20.basis_ref), custom_call_target="tpu_custom_call" | custom-call | tf_op jit(solution)/shard_map/second/pallas_call | solution.py:267
  18.5 0.6 %collective-permute-start.8 = (f32[8,128]{1,0:T(8,128)S(1)}, f32[8,128]{1,0:T(8,128)S(1)}, u32[]{:S(2)}, u32[]{:S(2)}) collective-permute-start(f32[8,128]{1,0:T(8,128)S(1)} %get-tuple-element.26), channel_id=1, source_target_pairs={{0,1},{1,0},{2,3},{3,2},{4,5},{5,4},{6,7},{7,6},{8,9},{9,8},{10,11... | collective-permute-start | bytes 12296 | tf_op jit(solution)/shard_map/ppermute | solution.py:236
  19.1 1.7 %collective-permute-start.6 = (f32[128,256]{1,0:T(8,128)S(1)}, f32[128,256]{1,0:T(8,128)S(1)}, u32[]{:S(2)}, u32[]{:S(2)}) collective-permute-start(f32[128,256]{1,0:T(8,128)S(1)} %get-tuple-element.24.own_ref), channel_id=1, source_target_pairs={{0,4},{1,5},{2,6},{3,7},{4,0},{5,1},{6,2},{7,3},{8,12},{9,13},{10,... | collective-permute-start | bytes 393224 | tf_op jit(solution)/shard_map/ppermute | solution.py:236
  20.7 1.4 %collective-permute-start.4 = (f32[128,256]{1,0:T(8,128)S(1)}, f32[128,256]{1,0:T(8,128)S(1)}, u32[]{:S(2)}, u32[]{:S(2)}) collective-permute-start(f32[128,256]{1,0:T(8,128)S(1)} %get-tuple-element.23.own_ref), channel_id=1, source_target_pairs={{0,2},{1,3},{2,0},{3,1},{4,6},{5,7},{6,4},{7,5},{8,10},{9,11},{10,... | collective-permute-start | bytes 393224 | tf_op jit(solution)/shard_map/ppermute | solution.py:236
  22.2 0.7 %lower.1 = (f32[128,256]{1,0:T(8,128)S(1)}, f32[128,256]{1,0:T(8,128)S(1)}) custom-call(bf16[512,4096]{1,0:T(8,128)(2,1)S(1)} %get-tuple-element.20.basis_ref, bf16[4096,256]{1,0:T(8,128)(2,1)S(1)} %get-tuple-element.25.image_ref, f32[512,256]{1,0:T(8,128)S(1)} %collective-permute-done.3.other_ref, f32[8,128]{1,0:T(8,128)S(1)} %collective-permute-done.8._), custom_call_target="tpu_custom_call" | custom-call | tf_op jit(solution)/shard_map/lower/pallas_call | solution.py:278
  22.9 0.6 %collective-permute-start.11 = (f32[128,256]{1,0:T(8,128)S(1)}, f32[128,256]{1,0:T(8,128)S(1)}, u32[]{:S(2)}, u32[]{:S(2)}) collective-permute-start(f32[128,256]{1,0:T(8,128)S(1)} %get-tuple-element.28.own_ref), channel_id=1, source_target_pairs={{0,4},{1,5},{2,6},{3,7},{4,0},{5,1},{6,2},{7,3},{8,12},{9,13},{10,... | collective-permute-start | bytes 393224 | tf_op jit(solution)/shard_map/ppermute | solution.py:236
  23.6 0.4 collective-permute-start.9
  23.9 0.6 %collective-permute-done.6.other_ref = f32[128,256]{1,0:T(8,128)S(1)} collective-permute-done((f32[128,256]{1,0:T(8,128)S(1)}, f32[128,256]{1,0:T(8,128)S(1)}, u32[]{:S(2)}, u32[]{:S(2)}) %collective-permute-start.6) | collective-permute-done | bytes 131104 | tf_op jit(solution)/shard_map/ppermute | solution.py:236
  24.6 2.2 %collective-permute-start.7 = (f32[128,256]{1,0:T(8,128)S(1)}, f32[128,256]{1,0:T(8,128)S(1)}, u32[]{:S(2)}, u32[]{:S(2)}) collective-permute-start(f32[128,256]{1,0:T(8,128)S(1)} %add.10.own_ref), channel_id=1, source_target_pairs={{0,2},{1,3},{2,0},{3,1},{4,6},{5,7},{6,4},{7,5},{8,10},{9,11},{10,... | collective-permute-start | bytes 393224 | tf_op jit(solution)/shard_map/ppermute | solution.py:236
  26.8 1.9 %collective-permute-start.5 = (f32[128,256]{1,0:T(8,128)S(1)}, f32[128,256]{1,0:T(8,128)S(1)}, u32[]{:S(2)}, u32[]{:S(2)}) collective-permute-start(f32[128,256]{1,0:T(8,128)S(1)} %add.8.own_ref), channel_id=1, source_target_pairs={{0,4},{1,5},{2,6},{3,7},{4,0},{5,1},{6,2},{7,3},{8,12},{9,13},{10,... | collective-permute-start | bytes 393224 | tf_op jit(solution)/shard_map/ppermute | solution.py:236
  28.7 0.4 %collective-permute-start.12 = (f32[128,256]{1,0:T(8,128)S(1)}, f32[128,256]{1,0:T(8,128)S(1)}, u32[]{:S(2)}, u32[]{:S(2)}) collective-permute-start(f32[128,256]{1,0:T(8,128)S(1)} %add.14.own_ref), channel_id=1, source_target_pairs={{0,2},{1,3},{2,0},{3,1},{4,6},{5,7},{6,4},{7,5},{8,10},{9,11},{10,... | collective-permute-start | bytes 393224 | tf_op jit(solution)/shard_map/ppermute | solution.py:236
  29.1 0.9 %collective-permute-done.9.other_ref = f32[128,256]{1,0:T(8,128)S(1)} collective-permute-done((f32[128,256]{1,0:T(8,128)S(1)}, f32[128,256]{1,0:T(8,128)S(1)}, u32[]{:S(2)}, u32[]{:S(2)}) %collective-permute-start.9) | collective-permute-done | bytes 131104 | tf_op jit(solution)/shard_map/ppermute | solution.py:236
  30.0 1.3 %collective-permute-start.10 = (f32[128,256]{1,0:T(8,128)S(1)}, f32[128,256]{1,0:T(8,128)S(1)}, u32[]{:S(2)}, u32[]{:S(2)}) collective-permute-start(f32[128,256]{1,0:T(8,128)S(1)} %add.12.own_ref), channel_id=1, source_target_pairs={{0,4},{1,5},{2,6},{3,7},{4,0},{5,1},{6,2},{7,3},{8,12},{9,13},{10,... | collective-permute-start | bytes 393224 | tf_op jit(solution)/shard_map/ppermute | solution.py:236
  31.3 1.5 %collective-permute-done.7.other_ref = f32[128,256]{1,0:T(8,128)S(1)} collective-permute-done((f32[128,256]{1,0:T(8,128)S(1)}, f32[128,256]{1,0:T(8,128)S(1)}, u32[]{:S(2)}, u32[]{:S(2)}) %collective-permute-start.7) | collective-permute-done | bytes 131104 | tf_op jit(solution)/shard_map/ppermute | solution.py:236
  32.8 0.1 collective-permute-start.14
  32.9 0.1 collective-permute-done.5.other_ref
  33.0 0.5 %collective-permute-start.13 = (f32[128,256]{1,0:T(8,128)S(1)}, f32[128,256]{1,0:T(8,128)S(1)}, u32[]{:S(2)}, u32[]{:S(2)}) collective-permute-start(f32[128,256]{1,0:T(8,128)S(1)} %add.9.refs_0_), channel_id=1, source_target_pairs={{0,1},{1,0},{2,3},{3,2},{4,5},{5,4},{6,7},{7,6},{8,9},{9,8},{10,11... | collective-permute-start | bytes 393224 | tf_op jit(solution)/shard_map/ppermute | solution.py:236
  33.5 0.9 %collective-permute-done.12.other_ref = f32[128,256]{1,0:T(8,128)S(1)} collective-permute-done((f32[128,256]{1,0:T(8,128)S(1)}, f32[128,256]{1,0:T(8,128)S(1)}, u32[]{:S(2)}, u32[]{:S(2)}) %collective-permute-start.12) | collective-permute-done | bytes 131104 | tf_op jit(solution)/shard_map/ppermute | solution.py:236
  34.4 0.1 collective-permute-start.16
  34.5 0.6 %collective-permute-done.10.other_ref = f32[128,256]{1,0:T(8,128)S(1)} collective-permute-done((f32[128,256]{1,0:T(8,128)S(1)}, f32[128,256]{1,0:T(8,128)S(1)}, u32[]{:S(2)}, u32[]{:S(2)}) %collective-permute-start.10) | collective-permute-done | bytes 131104 | tf_op jit(solution)/shard_map/ppermute | solution.py:236
  35.1 0.1 collective-permute-start.15
  35.2 0.6 %collective-permute-done.16.refs_7_ = f32[128,256]{1,0:T(8,128)S(1)} collective-permute-done((f32[128,256]{1,0:T(8,128)S(1)}, f32[128,256]{1,0:T(8,128)S(1)}, u32[]{:S(2)}, u32[]{:S(2)}) %collective-permute-start.16) | collective-permute-done | bytes 131104 | tf_op jit(solution)/shard_map/ppermute | solution.py:236
  35.8 0.7 %collective-permute-done.15.refs_6_ = f32[128,256]{1,0:T(8,128)S(1)} collective-permute-done((f32[128,256]{1,0:T(8,128)S(1)}, f32[128,256]{1,0:T(8,128)S(1)}, u32[]{:S(2)}, u32[]{:S(2)}) %collective-permute-start.15) | collective-permute-done | bytes 131104 | tf_op jit(solution)/shard_map/ppermute | solution.py:236
  36.5 1.3 %scale.1 = f32[512,512]{1,0:T(8,128)} custom-call(f32[128,256]{1,0:T(8,128)S(1)} %add.9.refs_0_, f32[128,256]{1,0:T(8,128)S(1)} %add.11.refs_1_, f32[128,256]{1,0:T(8,128)S(1)} %add.13.refs_2_, f32[128,256]{1,0:T(8,128)S(1)} %add.15.refs_3_, f32[128,256]{1,0:T(8,128)S(1)} %collective-permute-done.13.refs_4_, f32[128,256]{1,0:T(8,128)S(1)} %collective-permute-done.14.refs_5_, ...), custom_call_target="tpu_custom_call" | custom-call | tf_op jit(solution)/shard_map/scale/pallas_call | solution.py:290
  (25 shorter events, 0.2 us)
Async XLA Ops:
  0.0 7.8 %copy-start = (bf16[1,8,512,512]{3,2,1,0:T(8,128)(2,1)S(1)}, bf16[1,8,512,512]{3,2,1,0:T(8,128)(2,1)}, u32[]{:S(2)}) copy-start(bf16[1,8,512,512]{3,2,1,0:T(8,128)(2,1)} %param.6) | copy-start | bytes 12582916
  0.0 7.8 %copy-start.3 = (s32[1,8]{1,0:T(1,128)S(1)}, s32[1,8]{1,0:T(1,128)}, u32[]{:S(2)}) copy-start(s32[1,8]{1,0:T(1,128)} %param.7) | copy-start | bytes 100
  2.1 11.1 %collective-permute-start = (f32[8,512]{1,0:T(8,128)S(1)}, f32[8,512]{1,0:T(8,128)S(1)}, u32[]{:S(2)}, u32[]{:S(2)}) collective-permute-start(f32[8,512]{1,0:T(8,128)S(1)} %get-tuple-element.19.stiff_ref), channel_id=1, source_target_pairs={{0,8},{8,0},{16,24},{24,16},{1,9},{9,1},{17,25},{25,17},{2,10},{10... | collective-permute-start | bytes 49160 | tf_op jit(solution)/shard_map/ppermute | solution.py:236
  5.2 8.1 %collective-permute-start.1 = (f32[8,512]{1,0:T(8,128)S(1)}, f32[8,512]{1,0:T(8,128)S(1)}, u32[]{:S(2)}, u32[]{:S(2)}) collective-permute-start(f32[8,512]{1,0:T(8,128)S(1)} %get-tuple-element.19.stiff_ref), channel_id=1, source_target_pairs={{0,16},{8,24},{16,0},{24,8},{1,17},{9,25},{17,1},{25,9},{2,18},{10... | collective-permute-start | bytes 49160 | tf_op jit(solution)/shard_map/ppermute | solution.py:236
  7.8 5.5 %collective-permute-start.2 = (f32[8,512]{1,0:T(8,128)S(1)}, f32[8,512]{1,0:T(8,128)S(1)}, u32[]{:S(2)}, u32[]{:S(2)}) collective-permute-start(f32[8,512]{1,0:T(8,128)S(1)} %get-tuple-element.19.stiff_ref), channel_id=1, source_target_pairs={{0,24},{8,16},{16,8},{24,0},{1,25},{9,17},{17,9},{25,1},{2,26},{10... | collective-permute-start | bytes 49160 | tf_op jit(solution)/shard_map/ppermute | solution.py:236
  7.8 5.5 %copy-start.1 = (s32[1,8,512]{2,1,0:T(8,128)S(1)}, s32[1,8,512]{2,1,0:T(8,128)}, u32[]{:S(2)}) copy-start(s32[1,8,512]{2,1,0:T(8,128)} %param.8) | copy-start | bytes 49156
  7.8 5.5 %copy-start.2 = (s32[3,4]{1,0:T(4,128)S(1)}, s32[3,4]{1,0:T(4,128)}, u32[]{:S(2)}) copy-start(s32[3,4]{1,0:T(4,128)} %partner_ref.1) | copy-start | bytes 148
  16.3 2.2 %collective-permute-start.3 = (f32[512,256]{1,0:T(8,128)S(1)}, f32[512,256]{1,0:T(8,128)S(1)}, u32[]{:S(2)}, u32[]{:S(2)}) collective-permute-start(f32[512,256]{1,0:T(8,128)S(1)} %get-tuple-element.22), channel_id=1, source_target_pairs={{0,1},{1,0},{2,3},{3,2},{4,5},{5,4},{6,7},{7,6},{8,9},{9,8},{10,11... | collective-permute-start | bytes 1572872 | tf_op jit(solution)/shard_map/ppermute | solution.py:236
  18.5 3.7 %collective-permute-start.8 = (f32[8,128]{1,0:T(8,128)S(1)}, f32[8,128]{1,0:T(8,128)S(1)}, u32[]{:S(2)}, u32[]{:S(2)}) collective-permute-start(f32[8,128]{1,0:T(8,128)S(1)} %get-tuple-element.26), channel_id=1, source_target_pairs={{0,1},{1,0},{2,3},{3,2},{4,5},{5,4},{6,7},{7,6},{8,9},{9,8},{10,11... | collective-permute-start | bytes 12296 | tf_op jit(solution)/shard_map/ppermute | solution.py:236
  19.1 5.5 %collective-permute-start.6 = (f32[128,256]{1,0:T(8,128)S(1)}, f32[128,256]{1,0:T(8,128)S(1)}, u32[]{:S(2)}, u32[]{:S(2)}) collective-permute-start(f32[128,256]{1,0:T(8,128)S(1)} %get-tuple-element.24.own_ref), channel_id=1, source_target_pairs={{0,4},{1,5},{2,6},{3,7},{4,0},{5,1},{6,2},{7,3},{8,12},{9,13},{10,... | collective-permute-start | bytes 393224 | tf_op jit(solution)/shard_map/ppermute | solution.py:236
  20.7 6.0 %collective-permute-start.4 = (f32[128,256]{1,0:T(8,128)S(1)}, f32[128,256]{1,0:T(8,128)S(1)}, u32[]{:S(2)}, u32[]{:S(2)}) collective-permute-start(f32[128,256]{1,0:T(8,128)S(1)} %get-tuple-element.23.own_ref), channel_id=1, source_target_pairs={{0,2},{1,3},{2,0},{3,1},{4,6},{5,7},{6,4},{7,5},{8,10},{9,11},{10,... | collective-permute-start | bytes 393224 | tf_op jit(solution)/shard_map/ppermute | solution.py:236
  22.9 5.8 %collective-permute-start.11 = (f32[128,256]{1,0:T(8,128)S(1)}, f32[128,256]{1,0:T(8,128)S(1)}, u32[]{:S(2)}, u32[]{:S(2)}) collective-permute-start(f32[128,256]{1,0:T(8,128)S(1)} %get-tuple-element.28.own_ref), channel_id=1, source_target_pairs={{0,4},{1,5},{2,6},{3,7},{4,0},{5,1},{6,2},{7,3},{8,12},{9,13},{10,... | collective-permute-start | bytes 393224 | tf_op jit(solution)/shard_map/ppermute | solution.py:236
  23.6 6.4 %collective-permute-start.9 = (f32[128,256]{1,0:T(8,128)S(1)}, f32[128,256]{1,0:T(8,128)S(1)}, u32[]{:S(2)}, u32[]{:S(2)}) collective-permute-start(f32[128,256]{1,0:T(8,128)S(1)} %get-tuple-element.27.own_ref), channel_id=1, source_target_pairs={{0,2},{1,3},{2,0},{3,1},{4,6},{5,7},{6,4},{7,5},{8,10},{9,11},{10,... | collective-permute-start | bytes 393224 | tf_op jit(solution)/shard_map/ppermute | solution.py:236
  24.6 8.2 %collective-permute-start.7 = (f32[128,256]{1,0:T(8,128)S(1)}, f32[128,256]{1,0:T(8,128)S(1)}, u32[]{:S(2)}, u32[]{:S(2)}) collective-permute-start(f32[128,256]{1,0:T(8,128)S(1)} %add.10.own_ref), channel_id=1, source_target_pairs={{0,2},{1,3},{2,0},{3,1},{4,6},{5,7},{6,4},{7,5},{8,10},{9,11},{10,... | collective-permute-start | bytes 393224 | tf_op jit(solution)/shard_map/ppermute | solution.py:236
  26.8 6.2 %collective-permute-start.5 = (f32[128,256]{1,0:T(8,128)S(1)}, f32[128,256]{1,0:T(8,128)S(1)}, u32[]{:S(2)}, u32[]{:S(2)}) collective-permute-start(f32[128,256]{1,0:T(8,128)S(1)} %add.8.own_ref), channel_id=1, source_target_pairs={{0,4},{1,5},{2,6},{3,7},{4,0},{5,1},{6,2},{7,3},{8,12},{9,13},{10,... | collective-permute-start | bytes 393224 | tf_op jit(solution)/shard_map/ppermute | solution.py:236
  28.7 5.6 %collective-permute-start.12 = (f32[128,256]{1,0:T(8,128)S(1)}, f32[128,256]{1,0:T(8,128)S(1)}, u32[]{:S(2)}, u32[]{:S(2)}) collective-permute-start(f32[128,256]{1,0:T(8,128)S(1)} %add.14.own_ref), channel_id=1, source_target_pairs={{0,2},{1,3},{2,0},{3,1},{4,6},{5,7},{6,4},{7,5},{8,10},{9,11},{10,... | collective-permute-start | bytes 393224 | tf_op jit(solution)/shard_map/ppermute | solution.py:236
  30.0 5.0 %collective-permute-start.10 = (f32[128,256]{1,0:T(8,128)S(1)}, f32[128,256]{1,0:T(8,128)S(1)}, u32[]{:S(2)}, u32[]{:S(2)}) collective-permute-start(f32[128,256]{1,0:T(8,128)S(1)} %add.12.own_ref), channel_id=1, source_target_pairs={{0,4},{1,5},{2,6},{3,7},{4,0},{5,1},{6,2},{7,3},{8,12},{9,13},{10,... | collective-permute-start | bytes 393224 | tf_op jit(solution)/shard_map/ppermute | solution.py:236
  32.8 2.3 %collective-permute-start.14 = (f32[128,256]{1,0:T(8,128)S(1)}, f32[128,256]{1,0:T(8,128)S(1)}, u32[]{:S(2)}, u32[]{:S(2)}) collective-permute-start(f32[128,256]{1,0:T(8,128)S(1)} %add.11.refs_1_), channel_id=1, source_target_pairs={{0,1},{1,0},{2,3},{3,2},{4,5},{5,4},{6,7},{7,6},{8,9},{9,8},{10,11... | collective-permute-start | bytes 393224 | tf_op jit(solution)/shard_map/ppermute | solution.py:236
  33.0 2.1 %collective-permute-start.13 = (f32[128,256]{1,0:T(8,128)S(1)}, f32[128,256]{1,0:T(8,128)S(1)}, u32[]{:S(2)}, u32[]{:S(2)}) collective-permute-start(f32[128,256]{1,0:T(8,128)S(1)} %add.9.refs_0_), channel_id=1, source_target_pairs={{0,1},{1,0},{2,3},{3,2},{4,5},{5,4},{6,7},{7,6},{8,9},{9,8},{10,11... | collective-permute-start | bytes 393224 | tf_op jit(solution)/shard_map/ppermute | solution.py:236
  34.4 1.4 %collective-permute-start.16 = (f32[128,256]{1,0:T(8,128)S(1)}, f32[128,256]{1,0:T(8,128)S(1)}, u32[]{:S(2)}, u32[]{:S(2)}) collective-permute-start(f32[128,256]{1,0:T(8,128)S(1)} %add.15.refs_3_), channel_id=1, source_target_pairs={{0,1},{1,0},{2,3},{3,2},{4,5},{5,4},{6,7},{7,6},{8,9},{9,8},{10,11... | collective-permute-start | bytes 393224 | tf_op jit(solution)/shard_map/ppermute | solution.py:236
  35.1 1.4 %collective-permute-start.15 = (f32[128,256]{1,0:T(8,128)S(1)}, f32[128,256]{1,0:T(8,128)S(1)}, u32[]{:S(2)}, u32[]{:S(2)}) collective-permute-start(f32[128,256]{1,0:T(8,128)S(1)} %add.13.refs_2_), channel_id=1, source_target_pairs={{0,1},{1,0},{2,3},{3,2},{4,5},{5,4},{6,7},{7,6},{8,9},{9,8},{10,11... | collective-permute-start | bytes 393224 | tf_op jit(solution)/shard_map/ppermute | solution.py:236

commit v8 on v7

--- a/solution.py
+++ b/solution.py
@@ -283,9 +283,10 @@
     add = call("add", add_kernel, [pieces], [VSPEC] * 2)
     steps = [2 << b for b in range((line // 2 - 1).bit_length())]
     for step in range(len(steps)):
+        bits = steps[step], steps[-1 - step]
         for d in range(len(own)):
-            bit = steps[step] if d % 2 == 0 else steps[-1 - step]
-            (own[d],) = add(*in_vmem(own[d], swap(own[d], "gy", line, bit)))
+            hops = [(i, i ^ bits[(d ^ i) & 1]) for i in range(line)]
+            (own[d],) = add(*in_vmem(own[d], lax.ppermute(own[d], "gy", hops)))
     other = [swap(piece, "gy", line, 1) for piece in own]
     result = pl.pallas_call(
         scale_kernel,

time: 37.9 us -> 38 us (level)
  starting transfers between devices: 16.9 us -> 16.2 us
  waiting for transfers between devices: 6 us -> 6.68 us
    ppermute x17 -> x9, starting transfers between devices: 16.9 us -> 6.6 us  [swap(): return lax.ppermute(a, axis, [(i, i ^ bit) for i in range(size)])]
    ppermute x0 -> x8, starting transfers between devices: none -> 9.62 us  [per_device(): own[d], = add(*in_vmem(own[d], lax.ppermute(own[d], 'gy', hops)))]
    ppermute x0 -> x8, waiting for transfers between devices: none -> 5.25 us  [per_device(): own[d], = add(*in_vmem(own[d], lax.ppermute(own[d], 'gy', hops)))]
    ppermute x17 -> x9, waiting for transfers between devices: 6 us -> 1.44 us  [swap(): return lax.ppermute(a, axis, [(i, i ^ bit) for i in range(size)])]
where the time goes in v8:
time: 38 us; the launch traced here: 37.8 us
  starting transfers between devices  16.2 us (43%)
  Pallas kernels  14.7 us (39%)
  waiting for transfers between devices  6.68 us (18%)
    ppermute x8, starting transfers between devices, per_device(): own[d], = add(*in_vmem(own[d], lax.ppermute(own[d], 'gy', hops)))  9.62 us
    ppermute x9, starting transfers between devices, swap(): return lax.ppermute(a, axis, [(i, i ^ bit) for i in range(size)])  6.6 us
    pallas_call x1, Pallas kernels, schur(): call('schur', functools.partial(schur_kernel, first, last, here, stop), [...  5.36 us
    ppermute x8, waiting for transfers between devices, per_device(): own[d], = add(*in_vmem(own[d], lax.ppermute(own[d], 'gy', hops)))  5.25 us
    pallas_call x1, Pallas kernels, per_device(): call('first', first_kernel, [half, ((NC, subs * R), BF16)], [SSPEC] + [VS...  2.96 us
    pallas_call x1, Pallas kernels, per_device(): call('diag', diag_kernel, [((subs, R), F32), coupled_shape], [ASPEC, ASPE...  2.09 us
    pallas_call x1, Pallas kernels, per_device(): call('second', second_kernel, [((subs * R, HALF), BF16), ((HALF, HALF), F...  2.08 us
    ppermute x9, waiting for transfers between devices, swap(): return lax.ppermute(a, axis, [(i, i ^ bit) for i in range(size)])  1.44 us
  transfers between devices with their start and end apart: 17, of which 9 were waited for; matrix products, arithmetic and copies ran while one was open for 0% of the time, Pallas kernels for 22%

profile of v8, /device:TPU:0, one launch (start us, length us, event | category | flops | bytes accessed | tf_op | source)
XLA Modules:
  0.0 37.8 jit_solution(7615360295324897672)
XLA Ops:
  0.0 2.1 %diag.1 = (f32[8,512]{1,0:T(8,128)S(1)}, bf16[8,1024,512]{2,1,0:T(8,128)(2,1)S(1)}) custom-call(bf16[8,512,512]{2,1,0:T(8,128)(2,1)} %bitcast.5, bf16[8,1024,512]{2,1,0:T(8,128)(2,1)} %bitcast.9), custom_call_target="tpu_custom_call" | custom-call | tf_op jit(solution)/shard_map/diag/pallas_call | solution.py:238
  2.1 3.1 %collective-permute-start = (f32[8,512]{1,0:T(8,128)S(1)}, f32[8,512]{1,0:T(8,128)S(1)}, u32[]{:S(2)}, u32[]{:S(2)}) collective-permute-start(f32[8,512]{1,0:T(8,128)S(1)} %get-tuple-element.19.stiff_ref), channel_id=1, source_target_pairs={{0,8},{8,0},{16,24},{24,16},{1,9},{9,1},{17,25},{25,17},{2,10},{10... | collective-permute-start | bytes 49160 | tf_op jit(solution)/shard_map/ppermute | solution.py:236
  5.2 2.6 %collective-permute-start.1 = (f32[8,512]{1,0:T(8,128)S(1)}, f32[8,512]{1,0:T(8,128)S(1)}, u32[]{:S(2)}, u32[]{:S(2)}) collective-permute-start(f32[8,512]{1,0:T(8,128)S(1)} %get-tuple-element.19.stiff_ref), channel_id=1, source_target_pairs={{0,16},{8,24},{16,0},{24,8},{1,17},{9,25},{17,1},{25,9},{2,18},{10... | collective-permute-start | bytes 49160 | tf_op jit(solution)/shard_map/ppermute | solution.py:236
  7.8 0.0 copy-start.1
  7.8 5.4 %schur.1 = (bf16[8,512,512]{2,1,0:T(8,128)(2,1)S(1)}, bf16[8,1024,512]{2,1,0:T(8,128)(2,1)S(1)}) custom-call(s32[8]{0:T(128)S(1)} %bitcast.8, bf16[8,1024,512]{2,1,0:T(8,128)(2,1)} %bitcast.10, bf16[8,1024,512]{2,1,0:T(8,128)(2,1)S(1)} %get-tuple-element.17._, bf16[8,512,512]{2,1,0:T(8,128)(2,1)S(1)} %bitcast.6), custom_call_target="tpu_custom_call", output_to_operand_aliasing={{1}: (2, {})} | custom-call | tf_op jit(solution)/shard_map/schur/pallas_call | solution.py:250
  13.2 0.1 collective-permute-done.2.refs_2_
  13.3 3.0 %first.1 = (f32[512,256]{1,0:T(8,128)S(1)}, bf16[512,4096]{1,0:T(8,128)(2,1)S(1)}) custom-call(s32[3,4]{1,0:T(4,128)S(1)} %copy-done.2, s32[8,512]{1,0:T(8,128)S(1)} %bitcast.7, f32[8,512]{1,0:T(8,128)S(1)} %get-tuple-element.19.stiff_ref, f32[8,512]{1,0:T(8,128)S(1)} %collective-permute-done.refs_0_, f32[8,512]{1,0:T(8,128)S(1)} %collective-permute-done.1.refs_1_, ...), custom_call_target="tpu_custom_call" | custom-call | tf_op jit(solution)/shard_map/first/pallas_call | solution.py:263
  16.3 0.1 collective-permute-start.3
  16.4 2.1 %second.1 = (bf16[4096,256]{1,0:T(8,128)(2,1)S(1)}, f32[256,256]{1,0:T(8,128)S(1)}) custom-call(bf16[8,512,512]{2,1,0:T(8,128)(2,1)S(1)} %get-tuple-element.18.refs_3_.schur_ref, bf16[512,4096]{1,0:T(8,128)(2,1)S(1)} %get-tuple-element.20.basis_ref), custom_call_target="tpu_custom_call" | custom-call | tf_op jit(solution)/shard_map/second/pallas_call | solution.py:267
  18.5 0.6 %collective-permute-start.8 = (f32[8,128]{1,0:T(8,128)S(1)}, f32[8,128]{1,0:T(8,128)S(1)}, u32[]{:S(2)}, u32[]{:S(2)}) collective-permute-start(f32[8,128]{1,0:T(8,128)S(1)} %get-tuple-element.26), channel_id=1, source_target_pairs={{0,1},{1,0},{2,3},{3,2},{4,5},{5,4},{6,7},{7,6},{8,9},{9,8},{10,11... | collective-permute-start | bytes 12296 | tf_op jit(solution)/shard_map/ppermute | solution.py:236
  19.1 1.6 %collective-permute-start.6 = (f32[128,256]{1,0:T(8,128)S(1)}, f32[128,256]{1,0:T(8,128)S(1)}, u32[]{:S(2)}, u32[]{:S(2)}) collective-permute-start(f32[128,256]{1,0:T(8,128)S(1)} %get-tuple-element.24.own_ref), channel_id=1, source_target_pairs={{0,4},{1,3},{2,6},{3,1},{4,0},{5,7},{6,2},{7,5},{8,12},{9,11},{10,... | collective-permute-start | bytes 393224 | tf_op jit(solution)/shard_map/ppermute | solution.py:289
  20.7 1.5 %collective-permute-start.4 = (f32[128,256]{1,0:T(8,128)S(1)}, f32[128,256]{1,0:T(8,128)S(1)}, u32[]{:S(2)}, u32[]{:S(2)}) collective-permute-start(f32[128,256]{1,0:T(8,128)S(1)} %get-tuple-element.23.own_ref), channel_id=1, source_target_pairs={{0,2},{1,5},{2,0},{3,7},{4,6},{5,1},{6,4},{7,3},{8,10},{9,13},{10,... | collective-permute-start | bytes 393224 | tf_op jit(solution)/shard_map/ppermute | solution.py:289
  22.2 0.7 %lower.1 = (f32[128,256]{1,0:T(8,128)S(1)}, f32[128,256]{1,0:T(8,128)S(1)}) custom-call(bf16[512,4096]{1,0:T(8,128)(2,1)S(1)} %get-tuple-element.20.basis_ref, bf16[4096,256]{1,0:T(8,128)(2,1)S(1)} %get-tuple-element.25.image_ref, f32[512,256]{1,0:T(8,128)S(1)} %collective-permute-done.3.other_ref, f32[8,128]{1,0:T(8,128)S(1)} %collective-permute-done.8._), custom_call_target="tpu_custom_call" | custom-call | tf_op jit(solution)/shard_map/lower/pallas_call | solution.py:278
  22.9 0.6 %collective-permute-start.11 = (f32[128,256]{1,0:T(8,128)S(1)}, f32[128,256]{1,0:T(8,128)S(1)}, u32[]{:S(2)}, u32[]{:S(2)}) collective-permute-start(f32[128,256]{1,0:T(8,128)S(1)} %get-tuple-element.28.own_ref), channel_id=1, source_target_pairs={{0,4},{1,3},{2,6},{3,1},{4,0},{5,7},{6,2},{7,5},{8,12},{9,11},{10,... | collective-permute-start | bytes 393224 | tf_op jit(solution)/shard_map/ppermute | solution.py:289
  23.5 0.4 %collective-permute-start.9 = (f32[128,256]{1,0:T(8,128)S(1)}, f32[128,256]{1,0:T(8,128)S(1)}, u32[]{:S(2)}, u32[]{:S(2)}) collective-permute-start(f32[128,256]{1,0:T(8,128)S(1)} %get-tuple-element.27.own_ref), channel_id=1, source_target_pairs={{0,2},{1,5},{2,0},{3,7},{4,6},{5,1},{6,4},{7,3},{8,10},{9,13},{10,... | collective-permute-start | bytes 393224 | tf_op jit(solution)/shard_map/ppermute | solution.py:289
  23.9 1.2 %collective-permute-done.6.other_ref = f32[128,256]{1,0:T(8,128)S(1)} collective-permute-done((f32[128,256]{1,0:T(8,128)S(1)}, f32[128,256]{1,0:T(8,128)S(1)}, u32[]{:S(2)}, u32[]{:S(2)}) %collective-permute-start.6) | collective-permute-done | bytes 131104 | tf_op jit(solution)/shard_map/ppermute | solution.py:289
  25.1 1.2 %collective-permute-start.7 = (f32[128,256]{1,0:T(8,128)S(1)}, f32[128,256]{1,0:T(8,128)S(1)}, u32[]{:S(2)}, u32[]{:S(2)}) collective-permute-start(f32[128,256]{1,0:T(8,128)S(1)} %add.10.own_ref), channel_id=1, source_target_pairs={{0,2},{1,5},{2,0},{3,7},{4,6},{5,1},{6,4},{7,3},{8,10},{9,13},{10,... | collective-permute-start | bytes 393224 | tf_op jit(solution)/shard_map/ppermute | solution.py:289
  26.4 2.3 %collective-permute-start.5 = (f32[128,256]{1,0:T(8,128)S(1)}, f32[128,256]{1,0:T(8,128)S(1)}, u32[]{:S(2)}, u32[]{:S(2)}) collective-permute-start(f32[128,256]{1,0:T(8,128)S(1)} %add.8.own_ref), channel_id=1, source_target_pairs={{0,4},{1,3},{2,6},{3,1},{4,0},{5,7},{6,2},{7,5},{8,12},{9,11},{10,... | collective-permute-start | bytes 393224 | tf_op jit(solution)/shard_map/ppermute | solution.py:289
  28.7 0.8 %collective-permute-done.11.other_ref = f32[128,256]{1,0:T(8,128)S(1)} collective-permute-done((f32[128,256]{1,0:T(8,128)S(1)}, f32[128,256]{1,0:T(8,128)S(1)}, u32[]{:S(2)}, u32[]{:S(2)}) %collective-permute-start.11) | collective-permute-done | bytes 131104 | tf_op jit(solution)/shard_map/ppermute | solution.py:289
  29.4 0.6 %collective-permute-start.12 = (f32[128,256]{1,0:T(8,128)S(1)}, f32[128,256]{1,0:T(8,128)S(1)}, u32[]{:S(2)}, u32[]{:S(2)}) collective-permute-start(f32[128,256]{1,0:T(8,128)S(1)} %add.14.own_ref), channel_id=1, source_target_pairs={{0,2},{1,5},{2,0},{3,7},{4,6},{5,1},{6,4},{7,3},{8,10},{9,13},{10,... | collective-permute-start | bytes 393224 | tf_op jit(solution)/shard_map/ppermute | solution.py:289
  30.0 1.4 %collective-permute-start.10 = (f32[128,256]{1,0:T(8,128)S(1)}, f32[128,256]{1,0:T(8,128)S(1)}, u32[]{:S(2)}, u32[]{:S(2)}) collective-permute-start(f32[128,256]{1,0:T(8,128)S(1)} %add.12.own_ref), channel_id=1, source_target_pairs={{0,4},{1,3},{2,6},{3,1},{4,0},{5,7},{6,2},{7,5},{8,12},{9,11},{10,... | collective-permute-start | bytes 393224 | tf_op jit(solution)/shard_map/ppermute | solution.py:289
  31.5 0.1 collective-permute-done.7.other_ref
  31.6 0.1 collective-permute-start.14
  31.7 1.0 %collective-permute-done.5.other_ref = f32[128,256]{1,0:T(8,128)S(1)} collective-permute-done((f32[128,256]{1,0:T(8,128)S(1)}, f32[128,256]{1,0:T(8,128)S(1)}, u32[]{:S(2)}, u32[]{:S(2)}) %collective-permute-start.5) | collective-permute-done | bytes 131104 | tf_op jit(solution)/shard_map/ppermute | solution.py:289
  32.7 0.1 collective-permute-start.13
  32.8 1.7 %collective-permute-done.12.other_ref = f32[128,256]{1,0:T(8,128)S(1)} collective-permute-done((f32[128,256]{1,0:T(8,128)S(1)}, f32[128,256]{1,0:T(8,128)S(1)}, u32[]{:S(2)}, u32[]{:S(2)}) %collective-permute-start.12) | collective-permute-done | bytes 131104 | tf_op jit(solution)/shard_map/ppermute | solution.py:289
  34.5 0.1 collective-permute-start.16
  34.6 0.5 %collective-permute-done.10.other_ref = f32[128,256]{1,0:T(8,128)S(1)} collective-permute-done((f32[128,256]{1,0:T(8,128)S(1)}, f32[128,256]{1,0:T(8,128)S(1)}, u32[]{:S(2)}, u32[]{:S(2)}) %collective-permute-start.10) | collective-permute-done | bytes 131104 | tf_op jit(solution)/shard_map/ppermute | solution.py:289
  35.1 0.1 collective-permute-start.15
  35.2 0.7 %collective-permute-done.16.refs_7_ = f32[128,256]{1,0:T(8,128)S(1)} collective-permute-done((f32[128,256]{1,0:T(8,128)S(1)}, f32[128,256]{1,0:T(8,128)S(1)}, u32[]{:S(2)}, u32[]{:S(2)}) %collective-permute-start.16) | collective-permute-done | bytes 131104 | tf_op jit(solution)/shard_map/ppermute | solution.py:236
  35.9 0.6 %collective-permute-done.15.refs_6_ = f32[128,256]{1,0:T(8,128)S(1)} collective-permute-done((f32[128,256]{1,0:T(8,128)S(1)}, f32[128,256]{1,0:T(8,128)S(1)}, u32[]{:S(2)}, u32[]{:S(2)}) %collective-permute-start.15) | collective-permute-done | bytes 131104 | tf_op jit(solution)/shard_map/ppermute | solution.py:236
  36.5 1.3 %scale.1 = f32[512,512]{1,0:T(8,128)} custom-call(f32[128,256]{1,0:T(8,128)S(1)} %add.9.refs_0_, f32[128,256]{1,0:T(8,128)S(1)} %add.11.refs_1_, f32[128,256]{1,0:T(8,128)S(1)} %add.13.refs_2_, f32[128,256]{1,0:T(8,128)S(1)} %add.15.refs_3_, f32[128,256]{1,0:T(8,128)S(1)} %collective-permute-done.13.refs_4_, f32[128,256]{1,0:T(8,128)S(1)} %collective-permute-done.14.refs_5_, ...), custom_call_target="tpu_custom_call" | custom-call | tf_op jit(solution)/shard_map/scale/pallas_call | solution.py:291
  (25 shorter events, 0.2 us)
Async XLA Ops:
  0.0 7.8 %copy-start = (bf16[1,8,512,512]{3,2,1,0:T(8,128)(2,1)S(1)}, bf16[1,8,512,512]{3,2,1,0:T(8,128)(2,1)}, u32[]{:S(2)}) copy-start(bf16[1,8,512,512]{3,2,1,0:T(8,128)(2,1)} %param.6) | copy-start | bytes 12582916
  0.0 7.8 %copy-start.3 = (s32[1,8]{1,0:T(1,128)S(1)}, s32[1,8]{1,0:T(1,128)}, u32[]{:S(2)}) copy-start(s32[1,8]{1,0:T(1,128)} %param.7) | copy-start | bytes 100
  2.1 11.1 %collective-permute-start = (f32[8,512]{1,0:T(8,128)S(1)}, f32[8,512]{1,0:T(8,128)S(1)}, u32[]{:S(2)}, u32[]{:S(2)}) collective-permute-start(f32[8,512]{1,0:T(8,128)S(1)} %get-tuple-element.19.stiff_ref), channel_id=1, source_target_pairs={{0,8},{8,0},{16,24},{24,16},{1,9},{9,1},{17,25},{25,17},{2,10},{10... | collective-permute-start | bytes 49160 | tf_op jit(solution)/shard_map/ppermute | solution.py:236
  5.2 8.0 %collective-permute-start.1 = (f32[8,512]{1,0:T(8,128)S(1)}, f32[8,512]{1,0:T(8,128)S(1)}, u32[]{:S(2)}, u32[]{:S(2)}) collective-permute-start(f32[8,512]{1,0:T(8,128)S(1)} %get-tuple-element.19.stiff_ref), channel_id=1, source_target_pairs={{0,16},{8,24},{16,0},{24,8},{1,17},{9,25},{17,1},{25,9},{2,18},{10... | collective-permute-start | bytes 49160 | tf_op jit(solution)/shard_map/ppermute | solution.py:236
  7.8 5.5 %collective-permute-start.2 = (f32[8,512]{1,0:T(8,128)S(1)}, f32[8,512]{1,0:T(8,128)S(1)}, u32[]{:S(2)}, u32[]{:S(2)}) collective-permute-start(f32[8,512]{1,0:T(8,128)S(1)} %get-tuple-element.19.stiff_ref), channel_id=1, source_target_pairs={{0,24},{8,16},{16,8},{24,0},{1,25},{9,17},{17,9},{25,1},{2,26},{10... | collective-permute-start | bytes 49160 | tf_op jit(solution)/shard_map/ppermute | solution.py:236
  7.8 5.5 %copy-start.1 = (s32[1,8,512]{2,1,0:T(8,128)S(1)}, s32[1,8,512]{2,1,0:T(8,128)}, u32[]{:S(2)}) copy-start(s32[1,8,512]{2,1,0:T(8,128)} %param.8) | copy-start | bytes 49156
  7.8 5.5 %copy-start.2 = (s32[3,4]{1,0:T(4,128)S(1)}, s32[3,4]{1,0:T(4,128)}, u32[]{:S(2)}) copy-start(s32[3,4]{1,0:T(4,128)} %partner_ref.1) | copy-start | bytes 148
  16.3 2.2 %collective-permute-start.3 = (f32[512,256]{1,0:T(8,128)S(1)}, f32[512,256]{1,0:T(8,128)S(1)}, u32[]{:S(2)}, u32[]{:S(2)}) collective-permute-start(f32[512,256]{1,0:T(8,128)S(1)} %get-tuple-element.22), channel_id=1, source_target_pairs={{0,1},{1,0},{2,3},{3,2},{4,5},{5,4},{6,7},{7,6},{8,9},{9,8},{10,11... | collective-permute-start | bytes 1572872 | tf_op jit(solution)/shard_map/ppermute | solution.py:236
  18.5 3.7 %collective-permute-start.8 = (f32[8,128]{1,0:T(8,128)S(1)}, f32[8,128]{1,0:T(8,128)S(1)}, u32[]{:S(2)}, u32[]{:S(2)}) collective-permute-start(f32[8,128]{1,0:T(8,128)S(1)} %get-tuple-element.26), channel_id=1, source_target_pairs={{0,1},{1,0},{2,3},{3,2},{4,5},{5,4},{6,7},{7,6},{8,9},{9,8},{10,11... | collective-permute-start | bytes 12296 | tf_op jit(solution)/shard_map/ppermute | solution.py:236
  19.1 6.1 %collective-permute-start.6 = (f32[128,256]{1,0:T(8,128)S(1)}, f32[128,256]{1,0:T(8,128)S(1)}, u32[]{:S(2)}, u32[]{:S(2)}) collective-permute-start(f32[128,256]{1,0:T(8,128)S(1)} %get-tuple-element.24.own_ref), channel_id=1, source_target_pairs={{0,4},{1,3},{2,6},{3,1},{4,0},{5,7},{6,2},{7,5},{8,12},{9,11},{10,... | collective-permute-start | bytes 393224 | tf_op jit(solution)/shard_map/ppermute | solution.py:289
  20.7 5.7 %collective-permute-start.4 = (f32[128,256]{1,0:T(8,128)S(1)}, f32[128,256]{1,0:T(8,128)S(1)}, u32[]{:S(2)}, u32[]{:S(2)}) collective-permute-start(f32[128,256]{1,0:T(8,128)S(1)} %get-tuple-element.23.own_ref), channel_id=1, source_target_pairs={{0,2},{1,5},{2,0},{3,7},{4,6},{5,1},{6,4},{7,3},{8,10},{9,13},{10,... | collective-permute-start | bytes 393224 | tf_op jit(solution)/shard_map/ppermute | solution.py:289
  22.9 6.5 %collective-permute-start.11 = (f32[128,256]{1,0:T(8,128)S(1)}, f32[128,256]{1,0:T(8,128)S(1)}, u32[]{:S(2)}, u32[]{:S(2)}) collective-permute-start(f32[128,256]{1,0:T(8,128)S(1)} %get-tuple-element.28.own_ref), channel_id=1, source_target_pairs={{0,4},{1,3},{2,6},{3,1},{4,0},{5,7},{6,2},{7,5},{8,12},{9,11},{10,... | collective-permute-start | bytes 393224 | tf_op jit(solution)/shard_map/ppermute | solution.py:289
  23.5 6.5 %collective-permute-start.9 = (f32[128,256]{1,0:T(8,128)S(1)}, f32[128,256]{1,0:T(8,128)S(1)}, u32[]{:S(2)}, u32[]{:S(2)}) collective-permute-start(f32[128,256]{1,0:T(8,128)S(1)} %get-tuple-element.27.own_ref), channel_id=1, source_target_pairs={{0,2},{1,5},{2,0},{3,7},{4,6},{5,1},{6,4},{7,3},{8,10},{9,13},{10,... | collective-permute-start | bytes 393224 | tf_op jit(solution)/shard_map/ppermute | solution.py:289
  25.1 6.4 %collective-permute-start.7 = (f32[128,256]{1,0:T(8,128)S(1)}, f32[128,256]{1,0:T(8,128)S(1)}, u32[]{:S(2)}, u32[]{:S(2)}) collective-permute-start(f32[128,256]{1,0:T(8,128)S(1)} %add.10.own_ref), channel_id=1, source_target_pairs={{0,2},{1,5},{2,0},{3,7},{4,6},{5,1},{6,4},{7,3},{8,10},{9,13},{10,... | collective-permute-start | bytes 393224 | tf_op jit(solution)/shard_map/ppermute | solution.py:289
  26.4 6.3 %collective-permute-start.5 = (f32[128,256]{1,0:T(8,128)S(1)}, f32[128,256]{1,0:T(8,128)S(1)}, u32[]{:S(2)}, u32[]{:S(2)}) collective-permute-start(f32[128,256]{1,0:T(8,128)S(1)} %add.8.own_ref), channel_id=1, source_target_pairs={{0,4},{1,3},{2,6},{3,1},{4,0},{5,7},{6,2},{7,5},{8,12},{9,11},{10,... | collective-permute-start | bytes 393224 | tf_op jit(solution)/shard_map/ppermute | solution.py:289
  29.4 5.0 %collective-permute-start.12 = (f32[128,256]{1,0:T(8,128)S(1)}, f32[128,256]{1,0:T(8,128)S(1)}, u32[]{:S(2)}, u32[]{:S(2)}) collective-permute-start(f32[128,256]{1,0:T(8,128)S(1)} %add.14.own_ref), channel_id=1, source_target_pairs={{0,2},{1,5},{2,0},{3,7},{4,6},{5,1},{6,4},{7,3},{8,10},{9,13},{10,... | collective-permute-start | bytes 393224 | tf_op jit(solution)/shard_map/ppermute | solution.py:289
  30.0 5.0 %collective-permute-start.10 = (f32[128,256]{1,0:T(8,128)S(1)}, f32[128,256]{1,0:T(8,128)S(1)}, u32[]{:S(2)}, u32[]{:S(2)}) collective-permute-start(f32[128,256]{1,0:T(8,128)S(1)} %add.12.own_ref), channel_id=1, source_target_pairs={{0,4},{1,3},{2,6},{3,1},{4,0},{5,7},{6,2},{7,5},{8,12},{9,11},{10,... | collective-permute-start | bytes 393224 | tf_op jit(solution)/shard_map/ppermute | solution.py:289
  31.6 3.6 %collective-permute-start.14 = (f32[128,256]{1,0:T(8,128)S(1)}, f32[128,256]{1,0:T(8,128)S(1)}, u32[]{:S(2)}, u32[]{:S(2)}) collective-permute-start(f32[128,256]{1,0:T(8,128)S(1)} %add.11.refs_1_), channel_id=1, source_target_pairs={{0,1},{1,0},{2,3},{3,2},{4,5},{5,4},{6,7},{7,6},{8,9},{9,8},{10,11... | collective-permute-start | bytes 393224 | tf_op jit(solution)/shard_map/ppermute | solution.py:236
  32.7 2.5 %collective-permute-start.13 = (f32[128,256]{1,0:T(8,128)S(1)}, f32[128,256]{1,0:T(8,128)S(1)}, u32[]{:S(2)}, u32[]{:S(2)}) collective-permute-start(f32[128,256]{1,0:T(8,128)S(1)} %add.9.refs_0_), channel_id=1, source_target_pairs={{0,1},{1,0},{2,3},{3,2},{4,5},{5,4},{6,7},{7,6},{8,9},{9,8},{10,11... | collective-permute-start | bytes 393224 | tf_op jit(solution)/shard_map/ppermute | solution.py:236
  34.5 1.4 %collective-permute-start.16 = (f32[128,256]{1,0:T(8,128)S(1)}, f32[128,256]{1,0:T(8,128)S(1)}, u32[]{:S(2)}, u32[]{:S(2)}) collective-permute-start(f32[128,256]{1,0:T(8,128)S(1)} %add.15.refs_3_), channel_id=1, source_target_pairs={{0,1},{1,0},{2,3},{3,2},{4,5},{5,4},{6,7},{7,6},{8,9},{9,8},{10,11... | collective-permute-start | bytes 393224 | tf_op jit(solution)/shard_map/ppermute | solution.py:236
  35.1 1.4 %collective-permute-start.15 = (f32[128,256]{1,0:T(8,128)S(1)}, f32[128,256]{1,0:T(8,128)S(1)}, u32[]{:S(2)}, u32[]{:S(2)}) collective-permute-start(f32[128,256]{1,0:T(8,128)S(1)} %add.13.refs_2_), channel_id=1, source_target_pairs={{0,1},{1,0},{2,3},{3,2},{4,5},{5,4},{6,7},{7,6},{8,9},{9,8},{10,11... | collective-permute-start | bytes 393224 | tf_op jit(solution)/shard_map/ppermute | solution.py:236

commit v9 on v6

--- a/solution.py
+++ b/solution.py
@@ -274,9 +274,10 @@
     add = call("add", add_kernel, [pieces], [VSPEC] * 2)
     steps = [2 << b for b in range((line // 2 - 1).bit_length())]
     for step in range(len(steps)):
+        pair = steps[step], steps[-1 - step]
         for d in range(len(own)):
-            bit = steps[step] if d % 2 == 0 else steps[-1 - step]
-            (own[d],) = add(*in_vmem(own[d], swap(own[d], "gy", line, bit)))
+            hops = [(i, i ^ pair[(d // 2 ^ d) & 1]) for i in range(line)]
+            (own[d],) = add(*in_vmem(own[d], lax.ppermute(own[d], "gy", hops)))
     other = [swap(piece, "gy", line, 1) for piece in own]
     result = pl.pallas_call(
         scale_kernel,

time: 38 us -> 38.1 us (level)
  waiting for transfers between devices: 5.81 us -> 6.64 us
  starting transfers between devices: 17 us -> 16.3 us
    ppermute x17 -> x9, starting transfers between devices: 17 us -> 6.66 us  [swap(): return lax.ppermute(a, axis, [(i, i ^ bit) for i in range(size)])]
    ppermute x0 -> x8, starting transfers between devices: none -> 9.63 us  [per_device(): own[d], = add(*in_vmem(own[d], lax.ppermute(own[d], 'gy', hops)))]
    ppermute x0 -> x8, waiting for transfers between devices: none -> 5.35 us  [per_device(): own[d], = add(*in_vmem(own[d], lax.ppermute(own[d], 'gy', hops)))]
    ppermute x17 -> x9, waiting for transfers between devices: 5.81 us -> 1.28 us  [swap(): return lax.ppermute(a, axis, [(i, i ^ bit) for i in range(size)])]
  transfers between devices with their start and end apart: 17 -> 17, of which waited for: 8 -> 9; matrix products, arithmetic and copies ran while one was open for 0% -> 0% of each run, Pallas kernels for 22% -> 22%
where the time goes in v9:
time: 38.1 us; the launch traced here: 38 us
  starting transfers between devices  16.3 us (43%)
  Pallas kernels  14.8 us (39%)
  waiting for transfers between devices  6.64 us (17%)
    ppermute x8, starting transfers between devices, per_device(): own[d], = add(*in_vmem(own[d], lax.ppermute(own[d], 'gy', hops)))  9.63 us
    ppermute x9, starting transfers between devices, swap(): return lax.ppermute(a, axis, [(i, i ^ bit) for i in range(size)])  6.66 us
    pallas_call x1, Pallas kernels, schur(): call('schur', functools.partial(schur_kernel, first, last, here, stop), [...  5.5 us
    ppermute x8, waiting for transfers between devices, per_device(): own[d], = add(*in_vmem(own[d], lax.ppermute(own[d], 'gy', hops)))  5.35 us
    pallas_call x1, Pallas kernels, per_device(): call('first', first_kernel, [half, ((NC, subs * R), BF16)], [SSPEC] + [VS...  2.97 us
    pallas_call x1, Pallas kernels, per_device(): call('diag', diag_kernel, [((subs, R), F32), coupled_shape], [ASPEC, ASPE...  2.09 us
    pallas_call x1, Pallas kernels, per_device(): call('second', second_kernel, [((subs * R, HALF), BF16), ((HALF, HALF), F...  2.07 us
    pallas_call x1, Pallas kernels, per_device(): pl.pallas_call(scale_kernel, out_shape=jax.ShapeDtypeStruct((NC, NC), F32...  1.3 us
  transfers between devices with their start and end apart: 17, of which 9 were waited for; matrix products, arithmetic and copies ran while one was open for 0% of the time, Pallas kernels for 22%

profile of v9, /device:TPU:0, one launch (start us, length us, event | category | flops | bytes accessed | tf_op | source)
XLA Modules:
  0.0 38.0 jit_solution(1863075285150482968)
XLA Ops:
  0.0 2.1 %diag.1 = (f32[8,512]{1,0:T(8,128)S(1)}, bf16[8,1024,512]{2,1,0:T(8,128)(2,1)S(1)}) custom-call(bf16[8,512,512]{2,1,0:T(8,128)(2,1)} %bitcast.5, bf16[8,1024,512]{2,1,0:T(8,128)(2,1)} %bitcast.9), custom_call_target="tpu_custom_call" | custom-call | tf_op jit(solution)/shard_map/diag/pallas_call | solution.py:229
  2.1 3.1 %collective-permute-start = (f32[8,512]{1,0:T(8,128)S(1)}, f32[8,512]{1,0:T(8,128)S(1)}, u32[]{:S(2)}, u32[]{:S(2)}) collective-permute-start(f32[8,512]{1,0:T(8,128)S(1)} %get-tuple-element.19.stiff_ref), channel_id=1, source_target_pairs={{0,8},{8,0},{16,24},{24,16},{1,9},{9,1},{17,25},{25,17},{2,10},{10... | collective-permute-start | bytes 49160 | tf_op jit(solution)/shard_map/ppermute | solution.py:227
  5.2 2.6 %collective-permute-start.1 = (f32[8,512]{1,0:T(8,128)S(1)}, f32[8,512]{1,0:T(8,128)S(1)}, u32[]{:S(2)}, u32[]{:S(2)}) collective-permute-start(f32[8,512]{1,0:T(8,128)S(1)} %get-tuple-element.19.stiff_ref), channel_id=1, source_target_pairs={{0,16},{8,24},{16,0},{24,8},{1,17},{9,25},{17,1},{25,9},{2,18},{10... | collective-permute-start | bytes 49160 | tf_op jit(solution)/shard_map/ppermute | solution.py:227
  7.8 0.0 copy-start.1
  7.8 5.5 %schur.1 = (bf16[8,512,512]{2,1,0:T(8,128)(2,1)S(1)}, bf16[8,1024,512]{2,1,0:T(8,128)(2,1)S(1)}) custom-call(s32[8]{0:T(128)S(1)} %bitcast.8, bf16[8,1024,512]{2,1,0:T(8,128)(2,1)} %bitcast.10, bf16[8,1024,512]{2,1,0:T(8,128)(2,1)S(1)} %get-tuple-element.17._, bf16[8,512,512]{2,1,0:T(8,128)(2,1)S(1)} %bitcast.6), custom_call_target="tpu_custom_call", output_to_operand_aliasing={{1}: (2, {})} | custom-call | tf_op jit(solution)/shard_map/schur/pallas_call | solution.py:241
  13.4 3.0 %first.1 = (f32[512,256]{1,0:T(8,128)S(1)}, bf16[512,4096]{1,0:T(8,128)(2,1)S(1)}) custom-call(s32[3,4]{1,0:T(4,128)S(1)} %copy-done.2, s32[8,512]{1,0:T(8,128)S(1)} %bitcast.7, f32[8,512]{1,0:T(8,128)S(1)} %get-tuple-element.19.stiff_ref, f32[8,512]{1,0:T(8,128)S(1)} %collective-permute-done.refs_0_, f32[8,512]{1,0:T(8,128)S(1)} %collective-permute-done.1.refs_1_, ...), custom_call_target="tpu_custom_call" | custom-call | tf_op jit(solution)/shard_map/first/pallas_call | solution.py:254
  16.4 0.1 collective-permute-start.3
  16.4 2.1 %second.1 = (bf16[4096,256]{1,0:T(8,128)(2,1)S(1)}, f32[256,256]{1,0:T(8,128)S(1)}) custom-call(bf16[8,512,512]{2,1,0:T(8,128)(2,1)S(1)} %get-tuple-element.18.refs_3_.schur_ref, bf16[512,4096]{1,0:T(8,128)(2,1)S(1)} %get-tuple-element.20.basis_ref), custom_call_target="tpu_custom_call" | custom-call | tf_op jit(solution)/shard_map/second/pallas_call | solution.py:258
  18.6 0.6 %collective-permute-start.8 = (f32[8,128]{1,0:T(8,128)S(1)}, f32[8,128]{1,0:T(8,128)S(1)}, u32[]{:S(2)}, u32[]{:S(2)}) collective-permute-start(f32[8,128]{1,0:T(8,128)S(1)} %get-tuple-element.26), channel_id=1, source_target_pairs={{0,1},{1,0},{2,3},{3,2},{4,5},{5,4},{6,7},{7,6},{8,9},{9,8},{10,11... | collective-permute-start | bytes 12296 | tf_op jit(solution)/shard_map/ppermute | solution.py:227
  19.1 1.7 %collective-permute-start.6 = (f32[128,256]{1,0:T(8,128)S(1)}, f32[128,256]{1,0:T(8,128)S(1)}, u32[]{:S(2)}, u32[]{:S(2)}) collective-permute-start(f32[128,256]{1,0:T(8,128)S(1)} %get-tuple-element.24.own_ref), channel_id=1, source_target_pairs={{0,4},{1,5},{2,6},{3,7},{4,0},{5,1},{6,2},{7,3},{8,12},{9,13},{10,... | collective-permute-start | bytes 393224 | tf_op jit(solution)/shard_map/ppermute | solution.py:280
  20.8 1.5 %collective-permute-start.4 = (f32[128,256]{1,0:T(8,128)S(1)}, f32[128,256]{1,0:T(8,128)S(1)}, u32[]{:S(2)}, u32[]{:S(2)}) collective-permute-start(f32[128,256]{1,0:T(8,128)S(1)} %get-tuple-element.23.own_ref), channel_id=1, source_target_pairs={{0,2},{1,3},{2,0},{3,1},{4,6},{5,7},{6,4},{7,5},{8,10},{9,11},{10,... | collective-permute-start | bytes 393224 | tf_op jit(solution)/shard_map/ppermute | solution.py:280
  22.3 0.7 %lower.1 = (f32[128,256]{1,0:T(8,128)S(1)}, f32[128,256]{1,0:T(8,128)S(1)}) custom-call(bf16[512,4096]{1,0:T(8,128)(2,1)S(1)} %get-tuple-element.20.basis_ref, bf16[4096,256]{1,0:T(8,128)(2,1)S(1)} %get-tuple-element.25.image_ref, f32[512,256]{1,0:T(8,128)S(1)} %collective-permute-done.3.other_ref, f32[8,128]{1,0:T(8,128)S(1)} %collective-permute-done.8._), custom_call_target="tpu_custom_call" | custom-call | tf_op jit(solution)/shard_map/lower/pallas_call | solution.py:269
  23.1 0.6 %collective-permute-start.11 = (f32[128,256]{1,0:T(8,128)S(1)}, f32[128,256]{1,0:T(8,128)S(1)}, u32[]{:S(2)}, u32[]{:S(2)}) collective-permute-start(f32[128,256]{1,0:T(8,128)S(1)} %get-tuple-element.28.own_ref), channel_id=1, source_target_pairs={{0,2},{1,3},{2,0},{3,1},{4,6},{5,7},{6,4},{7,5},{8,10},{9,11},{10,... | collective-permute-start | bytes 393224 | tf_op jit(solution)/shard_map/ppermute | solution.py:280
  23.7 0.3 collective-permute-start.9
  24.0 0.6 %collective-permute-done.6.other_ref = f32[128,256]{1,0:T(8,128)S(1)} collective-permute-done((f32[128,256]{1,0:T(8,128)S(1)}, f32[128,256]{1,0:T(8,128)S(1)}, u32[]{:S(2)}, u32[]{:S(2)}) %collective-permute-start.6) | collective-permute-done | bytes 131104 | tf_op jit(solution)/shard_map/ppermute | solution.py:280
  24.6 1.8 %collective-permute-start.7 = (f32[128,256]{1,0:T(8,128)S(1)}, f32[128,256]{1,0:T(8,128)S(1)}, u32[]{:S(2)}, u32[]{:S(2)}) collective-permute-start(f32[128,256]{1,0:T(8,128)S(1)} %add.10.own_ref), channel_id=1, source_target_pairs={{0,2},{1,3},{2,0},{3,1},{4,6},{5,7},{6,4},{7,5},{8,10},{9,11},{10,... | collective-permute-start | bytes 393224 | tf_op jit(solution)/shard_map/ppermute | solution.py:280
  26.4 0.5 %collective-permute-done.4.other_ref = f32[128,256]{1,0:T(8,128)S(1)} collective-permute-done((f32[128,256]{1,0:T(8,128)S(1)}, f32[128,256]{1,0:T(8,128)S(1)}, u32[]{:S(2)}, u32[]{:S(2)}) %collective-permute-start.4) | collective-permute-done | bytes 131104 | tf_op jit(solution)/shard_map/ppermute | solution.py:280
  26.9 1.4 %collective-permute-start.5 = (f32[128,256]{1,0:T(8,128)S(1)}, f32[128,256]{1,0:T(8,128)S(1)}, u32[]{:S(2)}, u32[]{:S(2)}) collective-permute-start(f32[128,256]{1,0:T(8,128)S(1)} %add.8.own_ref), channel_id=1, source_target_pairs={{0,4},{1,5},{2,6},{3,7},{4,0},{5,1},{6,2},{7,3},{8,12},{9,13},{10,... | collective-permute-start | bytes 393224 | tf_op jit(solution)/shard_map/ppermute | solution.py:280
  28.2 1.4 %collective-permute-done.11.other_ref = f32[128,256]{1,0:T(8,128)S(1)} collective-permute-done((f32[128,256]{1,0:T(8,128)S(1)}, f32[128,256]{1,0:T(8,128)S(1)}, u32[]{:S(2)}, u32[]{:S(2)}) %collective-permute-start.11) | collective-permute-done | bytes 131104 | tf_op jit(solution)/shard_map/ppermute | solution.py:280
  29.7 0.5 %collective-permute-start.12 = (f32[128,256]{1,0:T(8,128)S(1)}, f32[128,256]{1,0:T(8,128)S(1)}, u32[]{:S(2)}, u32[]{:S(2)}) collective-permute-start(f32[128,256]{1,0:T(8,128)S(1)} %add.14.own_ref), channel_id=1, source_target_pairs={{0,4},{1,5},{2,6},{3,7},{4,0},{5,1},{6,2},{7,3},{8,12},{9,13},{10,... | collective-permute-start | bytes 393224 | tf_op jit(solution)/shard_map/ppermute | solution.py:280
  30.2 1.9 %collective-permute-start.10 = (f32[128,256]{1,0:T(8,128)S(1)}, f32[128,256]{1,0:T(8,128)S(1)}, u32[]{:S(2)}, u32[]{:S(2)}) collective-permute-start(f32[128,256]{1,0:T(8,128)S(1)} %add.12.own_ref), channel_id=1, source_target_pairs={{0,2},{1,3},{2,0},{3,1},{4,6},{5,7},{6,4},{7,5},{8,10},{9,11},{10,... | collective-permute-start | bytes 393224 | tf_op jit(solution)/shard_map/ppermute | solution.py:280
  32.1 0.2 collective-permute-done.7.other_ref
  32.3 0.1 collective-permute-start.14
  32.4 0.6 %collective-permute-done.5.other_ref = f32[128,256]{1,0:T(8,128)S(1)} collective-permute-done((f32[128,256]{1,0:T(8,128)S(1)}, f32[128,256]{1,0:T(8,128)S(1)}, u32[]{:S(2)}, u32[]{:S(2)}) %collective-permute-start.5) | collective-permute-done | bytes 131104 | tf_op jit(solution)/shard_map/ppermute | solution.py:280
  33.1 0.1 collective-permute-start.13
  33.1 1.6 %collective-permute-done.12.other_ref = f32[128,256]{1,0:T(8,128)S(1)} collective-permute-done((f32[128,256]{1,0:T(8,128)S(1)}, f32[128,256]{1,0:T(8,128)S(1)}, u32[]{:S(2)}, u32[]{:S(2)}) %collective-permute-start.12) | collective-permute-done | bytes 131104 | tf_op jit(solution)/shard_map/ppermute | solution.py:280
  34.7 0.1 collective-permute-start.16
  34.8 0.4 %collective-permute-done.10.other_ref = f32[128,256]{1,0:T(8,128)S(1)} collective-permute-done((f32[128,256]{1,0:T(8,128)S(1)}, f32[128,256]{1,0:T(8,128)S(1)}, u32[]{:S(2)}, u32[]{:S(2)}) %collective-permute-start.10) | collective-permute-done | bytes 131104 | tf_op jit(solution)/shard_map/ppermute | solution.py:280
  35.2 0.1 collective-permute-start.15
  35.4 0.7 %collective-permute-done.16.refs_7_ = f32[128,256]{1,0:T(8,128)S(1)} collective-permute-done((f32[128,256]{1,0:T(8,128)S(1)}, f32[128,256]{1,0:T(8,128)S(1)}, u32[]{:S(2)}, u32[]{:S(2)}) %collective-permute-start.16) | collective-permute-done | bytes 131104 | tf_op jit(solution)/shard_map/ppermute | solution.py:227
  36.1 0.5 %collective-permute-done.15.refs_6_ = f32[128,256]{1,0:T(8,128)S(1)} collective-permute-done((f32[128,256]{1,0:T(8,128)S(1)}, f32[128,256]{1,0:T(8,128)S(1)}, u32[]{:S(2)}, u32[]{:S(2)}) %collective-permute-start.15) | collective-permute-done | bytes 131104 | tf_op jit(solution)/shard_map/ppermute | solution.py:227
  36.7 1.3 %scale.1 = f32[512,512]{1,0:T(8,128)} custom-call(f32[128,256]{1,0:T(8,128)S(1)} %add.9.refs_0_, f32[128,256]{1,0:T(8,128)S(1)} %add.11.refs_1_, f32[128,256]{1,0:T(8,128)S(1)} %add.13.refs_2_, f32[128,256]{1,0:T(8,128)S(1)} %add.15.refs_3_, f32[128,256]{1,0:T(8,128)S(1)} %collective-permute-done.13.refs_4_, f32[128,256]{1,0:T(8,128)S(1)} %collective-permute-done.14.refs_5_, ...), custom_call_target="tpu_custom_call" | custom-call | tf_op jit(solution)/shard_map/scale/pallas_call | solution.py:282
  (25 shorter events, 0.2 us)
Async XLA Ops:
  0.0 7.8 %copy-start = (bf16[1,8,512,512]{3,2,1,0:T(8,128)(2,1)S(1)}, bf16[1,8,512,512]{3,2,1,0:T(8,128)(2,1)}, u32[]{:S(2)}) copy-start(bf16[1,8,512,512]{3,2,1,0:T(8,128)(2,1)} %param.6) | copy-start | bytes 12582916
  0.0 7.8 %copy-start.3 = (s32[1,8]{1,0:T(1,128)S(1)}, s32[1,8]{1,0:T(1,128)}, u32[]{:S(2)}) copy-start(s32[1,8]{1,0:T(1,128)} %param.7) | copy-start | bytes 100
  2.1 11.2 %collective-permute-start = (f32[8,512]{1,0:T(8,128)S(1)}, f32[8,512]{1,0:T(8,128)S(1)}, u32[]{:S(2)}, u32[]{:S(2)}) collective-permute-start(f32[8,512]{1,0:T(8,128)S(1)} %get-tuple-element.19.stiff_ref), channel_id=1, source_target_pairs={{0,8},{8,0},{16,24},{24,16},{1,9},{9,1},{17,25},{25,17},{2,10},{10... | collective-permute-start | bytes 49160 | tf_op jit(solution)/shard_map/ppermute | solution.py:227
  5.2 8.1 %collective-permute-start.1 = (f32[8,512]{1,0:T(8,128)S(1)}, f32[8,512]{1,0:T(8,128)S(1)}, u32[]{:S(2)}, u32[]{:S(2)}) collective-permute-start(f32[8,512]{1,0:T(8,128)S(1)} %get-tuple-element.19.stiff_ref), channel_id=1, source_target_pairs={{0,16},{8,24},{16,0},{24,8},{1,17},{9,25},{17,1},{25,9},{2,18},{10... | collective-permute-start | bytes 49160 | tf_op jit(solution)/shard_map/ppermute | solution.py:227
  7.8 5.6 %collective-permute-start.2 = (f32[8,512]{1,0:T(8,128)S(1)}, f32[8,512]{1,0:T(8,128)S(1)}, u32[]{:S(2)}, u32[]{:S(2)}) collective-permute-start(f32[8,512]{1,0:T(8,128)S(1)} %get-tuple-element.19.stiff_ref), channel_id=1, source_target_pairs={{0,24},{8,16},{16,8},{24,0},{1,25},{9,17},{17,9},{25,1},{2,26},{10... | collective-permute-start | bytes 49160 | tf_op jit(solution)/shard_map/ppermute | solution.py:227
  7.8 5.6 %copy-start.1 = (s32[1,8,512]{2,1,0:T(8,128)S(1)}, s32[1,8,512]{2,1,0:T(8,128)}, u32[]{:S(2)}) copy-start(s32[1,8,512]{2,1,0:T(8,128)} %param.8) | copy-start | bytes 49156
  7.8 5.6 %copy-start.2 = (s32[3,4]{1,0:T(4,128)S(1)}, s32[3,4]{1,0:T(4,128)}, u32[]{:S(2)}) copy-start(s32[3,4]{1,0:T(4,128)} %partner_ref.1) | copy-start | bytes 148
  16.4 2.2 %collective-permute-start.3 = (f32[512,256]{1,0:T(8,128)S(1)}, f32[512,256]{1,0:T(8,128)S(1)}, u32[]{:S(2)}, u32[]{:S(2)}) collective-permute-start(f32[512,256]{1,0:T(8,128)S(1)} %get-tuple-element.22), channel_id=1, source_target_pairs={{0,1},{1,0},{2,3},{3,2},{4,5},{5,4},{6,7},{7,6},{8,9},{9,8},{10,11... | collective-permute-start | bytes 1572872 | tf_op jit(solution)/shard_map/ppermute | solution.py:227
  18.6 3.8 %collective-permute-start.8 = (f32[8,128]{1,0:T(8,128)S(1)}, f32[8,128]{1,0:T(8,128)S(1)}, u32[]{:S(2)}, u32[]{:S(2)}) collective-permute-start(f32[8,128]{1,0:T(8,128)S(1)} %get-tuple-element.26), channel_id=1, source_target_pairs={{0,1},{1,0},{2,3},{3,2},{4,5},{5,4},{6,7},{7,6},{8,9},{9,8},{10,11... | collective-permute-start | bytes 12296 | tf_op jit(solution)/shard_map/ppermute | solution.py:227
  19.1 5.5 %collective-permute-start.6 = (f32[128,256]{1,0:T(8,128)S(1)}, f32[128,256]{1,0:T(8,128)S(1)}, u32[]{:S(2)}, u32[]{:S(2)}) collective-permute-start(f32[128,256]{1,0:T(8,128)S(1)} %get-tuple-element.24.own_ref), channel_id=1, source_target_pairs={{0,4},{1,5},{2,6},{3,7},{4,0},{5,1},{6,2},{7,3},{8,12},{9,13},{10,... | collective-permute-start | bytes 393224 | tf_op jit(solution)/shard_map/ppermute | solution.py:280
  20.8 6.0 %collective-permute-start.4 = (f32[128,256]{1,0:T(8,128)S(1)}, f32[128,256]{1,0:T(8,128)S(1)}, u32[]{:S(2)}, u32[]{:S(2)}) collective-permute-start(f32[128,256]{1,0:T(8,128)S(1)} %get-tuple-element.23.own_ref), channel_id=1, source_target_pairs={{0,2},{1,3},{2,0},{3,1},{4,6},{5,7},{6,4},{7,5},{8,10},{9,11},{10,... | collective-permute-start | bytes 393224 | tf_op jit(solution)/shard_map/ppermute | solution.py:280
  23.1 6.6 %collective-permute-start.11 = (f32[128,256]{1,0:T(8,128)S(1)}, f32[128,256]{1,0:T(8,128)S(1)}, u32[]{:S(2)}, u32[]{:S(2)}) collective-permute-start(f32[128,256]{1,0:T(8,128)S(1)} %get-tuple-element.28.own_ref), channel_id=1, source_target_pairs={{0,2},{1,3},{2,0},{3,1},{4,6},{5,7},{6,4},{7,5},{8,10},{9,11},{10,... | collective-permute-start | bytes 393224 | tf_op jit(solution)/shard_map/ppermute | solution.py:280
  23.7 6.5 %collective-permute-start.9 = (f32[128,256]{1,0:T(8,128)S(1)}, f32[128,256]{1,0:T(8,128)S(1)}, u32[]{:S(2)}, u32[]{:S(2)}) collective-permute-start(f32[128,256]{1,0:T(8,128)S(1)} %get-tuple-element.27.own_ref), channel_id=1, source_target_pairs={{0,4},{1,5},{2,6},{3,7},{4,0},{5,1},{6,2},{7,3},{8,12},{9,13},{10,... | collective-permute-start | bytes 393224 | tf_op jit(solution)/shard_map/ppermute | solution.py:280
  24.6 7.7 %collective-permute-start.7 = (f32[128,256]{1,0:T(8,128)S(1)}, f32[128,256]{1,0:T(8,128)S(1)}, u32[]{:S(2)}, u32[]{:S(2)}) collective-permute-start(f32[128,256]{1,0:T(8,128)S(1)} %add.10.own_ref), channel_id=1, source_target_pairs={{0,2},{1,3},{2,0},{3,1},{4,6},{5,7},{6,4},{7,5},{8,10},{9,11},{10,... | collective-permute-start | bytes 393224 | tf_op jit(solution)/shard_map/ppermute | solution.py:280
  26.9 6.2 %collective-permute-start.5 = (f32[128,256]{1,0:T(8,128)S(1)}, f32[128,256]{1,0:T(8,128)S(1)}, u32[]{:S(2)}, u32[]{:S(2)}) collective-permute-start(f32[128,256]{1,0:T(8,128)S(1)} %add.8.own_ref), channel_id=1, source_target_pairs={{0,4},{1,5},{2,6},{3,7},{4,0},{5,1},{6,2},{7,3},{8,12},{9,13},{10,... | collective-permute-start | bytes 393224 | tf_op jit(solution)/shard_map/ppermute | solution.py:280
  29.7 5.0 %collective-permute-start.12 = (f32[128,256]{1,0:T(8,128)S(1)}, f32[128,256]{1,0:T(8,128)S(1)}, u32[]{:S(2)}, u32[]{:S(2)}) collective-permute-start(f32[128,256]{1,0:T(8,128)S(1)} %add.14.own_ref), channel_id=1, source_target_pairs={{0,4},{1,5},{2,6},{3,7},{4,0},{5,1},{6,2},{7,3},{8,12},{9,13},{10,... | collective-permute-start | bytes 393224 | tf_op jit(solution)/shard_map/ppermute | solution.py:280
  30.2 5.0 %collective-permute-start.10 = (f32[128,256]{1,0:T(8,128)S(1)}, f32[128,256]{1,0:T(8,128)S(1)}, u32[]{:S(2)}, u32[]{:S(2)}) collective-permute-start(f32[128,256]{1,0:T(8,128)S(1)} %add.12.own_ref), channel_id=1, source_target_pairs={{0,2},{1,3},{2,0},{3,1},{4,6},{5,7},{6,4},{7,5},{8,10},{9,11},{10,... | collective-permute-start | bytes 393224 | tf_op jit(solution)/shard_map/ppermute | solution.py:280
  32.3 3.1 %collective-permute-start.14 = (f32[128,256]{1,0:T(8,128)S(1)}, f32[128,256]{1,0:T(8,128)S(1)}, u32[]{:S(2)}, u32[]{:S(2)}) collective-permute-start(f32[128,256]{1,0:T(8,128)S(1)} %add.11.refs_1_), channel_id=1, source_target_pairs={{0,1},{1,0},{2,3},{3,2},{4,5},{5,4},{6,7},{7,6},{8,9},{9,8},{10,11... | collective-permute-start | bytes 393224 | tf_op jit(solution)/shard_map/ppermute | solution.py:227
  33.1 2.3 %collective-permute-start.13 = (f32[128,256]{1,0:T(8,128)S(1)}, f32[128,256]{1,0:T(8,128)S(1)}, u32[]{:S(2)}, u32[]{:S(2)}) collective-permute-start(f32[128,256]{1,0:T(8,128)S(1)} %add.9.refs_0_), channel_id=1, source_target_pairs={{0,1},{1,0},{2,3},{3,2},{4,5},{5,4},{6,7},{7,6},{8,9},{9,8},{10,11... | collective-permute-start | bytes 393224 | tf_op jit(solution)/shard_map/ppermute | solution.py:227
  34.7 1.4 %collective-permute-start.16 = (f32[128,256]{1,0:T(8,128)S(1)}, f32[128,256]{1,0:T(8,128)S(1)}, u32[]{:S(2)}, u32[]{:S(2)}) collective-permute-start(f32[128,256]{1,0:T(8,128)S(1)} %add.15.refs_3_), channel_id=1, source_target_pairs={{0,1},{1,0},{2,3},{3,2},{4,5},{5,4},{6,7},{7,6},{8,9},{9,8},{10,11... | collective-permute-start | bytes 393224 | tf_op jit(solution)/shard_map/ppermute | solution.py:227
  35.2 1.4 %collective-permute-start.15 = (f32[128,256]{1,0:T(8,128)S(1)}, f32[128,256]{1,0:T(8,128)S(1)}, u32[]{:S(2)}, u32[]{:S(2)}) collective-permute-start(f32[128,256]{1,0:T(8,128)S(1)} %add.13.refs_2_), channel_id=1, source_target_pairs={{0,1},{1,0},{2,3},{3,2},{4,5},{5,4},{6,7},{7,6},{8,9},{9,8},{10,11... | collective-permute-start | bytes 393224 | tf_op jit(solution)/shard_map/ppermute | solution.py:227
